TPU v7x, 512 devices: a whole 4x4x16 slice. The times are simulated.
512 devices in a mesh: wide: 64 (over z, x), narrow: 8 (over y, core).
Axes of the slice: x: 4, y: 4, z: 16, core: 2. Of those that a mesh axis runs over, the one named last changes fastest.
Arguments:
- points: bfloat16 [98304, 1024], P('wide')
- coarse_ids: int32 [64], P('wide'), may hold values from 0 to 15
- lists: int32 [16, 2048], replicated, may hold values from 0 to 8191, as said below
- owner_map: int32 [8192], replicated, may hold values from 0 to 8191, as said below
- centroids: bfloat16 [8192, 1024], P('wide'), may hold values from -0.1875 to 0.1875
Outputs:
- new_table: float32 [8192, 1024], P('wide')
- masses: float32 [8192], P('wide')
Inputs may be any that keep to these rules, and one draw needn't show every extreme that they name: owner_map is a permutation: the storage row of each centroid; storage row r is held by owner r // 128. `lists`: ids in a row are distinct; in each aligned block of 256 entries of a row, at most 8 ids have storage rows of any one owner, and some owner has exactly 8.
All inputs are finite; a program needn't handle non-finite values.
Results may differ from a plain program's by a relative error of at most 0.0075.
Values may be sent and summed in bfloat16 or wider, within the bound.
No kernel may reach another device: no remote copies, remote signals or barrier semaphores. Data moves between devices by JAX's collectives and lax.ppermute only.
A program may use at most 64 MiB of HBM per device.

v0:
```python
import jax
import jax.numpy as jnp
from jax import lax
from jax.sharding import PartitionSpec as P

temper = 0.1
prior = 0.01


def slot_arrangement(listed, owner_map, held, wide_n, slots):
    stored = owner_map[listed]
    owners = stored // held
    inner = stored % held
    onehot = (owners[:, None] == jnp.arange(wide_n, dtype=jnp.int32)[None, :]).astype(jnp.int32)
    ranked = jnp.sum(jnp.cumsum(onehot, axis=0) * onehot, axis=1) - 1
    slot_index = owners * slots + ranked
    request = jnp.zeros((wide_n * slots,), jnp.int32).at[slot_index].set(inner)
    return (slot_index, request.reshape(wide_n, slots))


def shards(points, coarse_ids, lists, owner_map, centroids):
    wide_n = lax.axis_size("wide")
    narrow_n = lax.axis_size("narrow")
    column = lax.axis_index("narrow")
    per_dev = lists.shape[1] // narrow_n
    held = centroids.shape[0]
    slots = 2 * per_dev // wide_n
    listed = lax.dynamic_slice(lists, (coarse_ids[0], column * per_dev), (1, per_dev))[0]
    slot_index, request = slot_arrangement(listed, owner_map, held, wide_n, slots)
    incoming = lax.all_to_all(request, "wide", split_axis=0, concat_axis=0, tiled=True)
    outgoing = centroids[incoming]
    answered = lax.all_to_all(outgoing, "wide", split_axis=0, concat_axis=0, tiled=True)
    means = answered.reshape(wide_n * slots, -1)[slot_index]
    norms = jnp.sum(means.astype(jnp.float32) ** 2, axis=1)
    dots = jnp.dot(points, means.T, preferred_element_type=jnp.float32)
    scores = (2.0 * dots - norms[None, :]) / temper
    local_best_scores = jnp.max(scores, axis=1)
    top = lax.pmax(local_best_scores, "narrow")
    expo = jnp.exp(scores - top[:, None])
    total = lax.psum(jnp.sum(expo, axis=1), "narrow")
    resp = (expo / total[:, None]).astype(jnp.bfloat16)
    sums = jnp.dot(resp.T, points, preferred_element_type=jnp.float32).astype(jnp.bfloat16)
    mass = jnp.sum(resp.astype(jnp.float32), axis=0).astype(jnp.bfloat16)
    width = points.shape[1]
    sum_slots = jnp.zeros((wide_n * slots, width), jnp.bfloat16).at[slot_index].set(sums)
    mass_slots = jnp.zeros((wide_n * slots,), jnp.bfloat16).at[slot_index].set(mass)
    received_sums, got_mass = (
        lax.all_to_all(
            sum_slots.reshape(wide_n, slots, width), "wide", split_axis=0, concat_axis=0, tiled=True
        ),
        lax.all_to_all(
            mass_slots.reshape(wide_n, slots), "wide", split_axis=0, concat_axis=0, tiled=True
        ),
    )
    placing = (jnp.arange(held, dtype=jnp.int32)[:, None] == incoming.reshape(-1)[None, :]).astype(
        jnp.float32
    )
    totals = jnp.dot(
        placing,
        received_sums.reshape(wide_n * slots, width).astype(jnp.float32),
        precision=lax.Precision.HIGHEST,
    )
    weight = jnp.dot(
        placing, got_mass.reshape(-1).astype(jnp.float32), precision=lax.Precision.HIGHEST
    )
    totals, weight = lax.psum((totals, weight), "narrow")
    new_table = (totals + prior * centroids.astype(jnp.float32)) / (weight + prior)[:, None]
    return (new_table, weight)


def solution(mesh):
    placed = (P("wide", None), P("wide"), P(), P(), P("wide", None))
    return jax.shard_map(
        shards, mesh=mesh, in_specs=placed, out_specs=(P("wide", None), P("wide")), check_vma=False
    )
```

profile of v0, /device:TPU:1, one launch (start us, length us, event | category | flops | bytes accessed | tf_op | source)
XLA Modules:
  0.0 308.7 jit_solution(13990720911818246101)
XLA Ops:
  7.2 0.0 copy-start
  7.2 0.0 copy-start.1
  8.0 0.9 compare_select_fusion.2
  8.9 2.0 gather_fusion
  11.0 0.6 reduce-window.6
  11.6 0.2 slice_reduce_fusion
  11.8 0.1 fusion.10
  11.9 1.4 scatter_custom_fusion
  13.4 0.1 all_to_all.20
  13.4 32.4 %all_to_all.32 = s32[64,1,8]{2,1,0:T(1,128)S(1)} all-to-all(s32[64,1,8]{2,1,0:T(1,128)S(1)} %bitcast.56), channel_id=1, replica_groups=mesh['wide'=64,'narrow'=8] {'wide'}, dimensions={0} | all-to-all | bytes 4096 | tf_op jit(solution)/shard_map/all_to_all | solution.py:30
  45.8 0.1 reshape.194
  45.9 0.0 copy-done.1
  45.9 2.8 gather_fusion.1
  48.7 5.5 %all-to-all-start.1 = ((bf16[64,8,1024]{2,1,0:T(8,128)(2,1)}), bf16[64,8,1024]{2,1,0:T(8,128)(2,1)}, u32[]{:S(2)}, u32[]{:S(2)}) async-start(bf16[64,8,1024]{2,1,0:T(8,128)(2,1)} %bitcast.53), calls=%async_computation.1 | async-start | bytes 2097152 | tf_op jit(solution)/shard_map/all_to_all | solution.py:32
  54.3 50.1 %all-to-all-done.1 = bf16[64,8,1024]{2,1,0:T(8,128)(2,1)} async-done(((bf16[64,8,1024]{2,1,0:T(8,128)(2,1)}), bf16[64,8,1024]{2,1,0:T(8,128)(2,1)}, u32[]{:S(2)}, u32[]{:S(2)}) %all-to-all-start.1) | async-done | bytes 1048608 | tf_op jit(solution)/shard_map/all_to_all | solution.py:32
  104.4 3.7 %gather_fusion.2 = bf16[256,1024]{1,0:T(8,128)(2,1)} fusion(bf16[512,1024]{1,0:T(8,128)(2,1)} %bitcast.11, s32[1024]{0:T(1024)S(1)} %pad_clamp_fusion), kind=kCustom, calls=%fused_computation.2 | custom fusion | bytes 1049600 | tf_op jit(solution)/shard_map/gather | solution.py:33
  108.1 1.2 multiply_reduce_fusion
  109.3 0.0 copy-done
  109.3 3.2 %fusion.17 = (f32[1536]{0:T(1024)S(1)}, f32[256,1536]{1,0:T(8,128)}) fusion(f32[256]{0:T(256)S(1)} %multiply_reduce_fusion, bf16[256,1024]{1,0:T(8,128)(2,1)} %gather_fusion.2, bf16[1536,1024]{1,0:T(8,128)(2,1)S(1)} %copy-done), kind=kOutput, calls=%fused_computation.60 | convolution fusion | flops 806877696 | bytes 5250048 | tf_op jit(solution)/shard_map/dot_general | solution.py:35
  112.5 18.1 %pmax.7 = f32[1536]{0:T(1024)S(1)} all-reduce(f32[1536]{0:T(1024)S(1)} %get-tuple-element.6), channel_id=1, replica_groups=mesh['wide'=64,'narrow'=8] {'narrow'}, use_global_device_ids=true, to_apply=%region_6.7 | all-reduce | flops 1536 | bytes 12288 | tf_op jit(solution)/shard_map/pmax | solution.py:38
  130.7 1.6 fusion.2
  132.3 12.5 %psum.21 = f32[1536]{0:T(1024)S(1)} all-reduce(f32[1536]{0:T(1024)S(1)} %fusion.2), channel_id=1, replica_groups=mesh['wide'=64,'narrow'=8] {'narrow'}, use_global_device_ids=true, to_apply=%region_8.9 | all-reduce | flops 1536 | bytes 12288 | tf_op jit(solution)/shard_map/psum | solution.py:40
  144.8 2.6 fusion.16
  147.4 2.2 scatter_custom_fusion.2
  149.5 0.7 all_to_all.27
  150.2 7.3 %all-to-all-start.3 = ((bf16[64,1,8]{2,1,0:T(2,128)(2,1)}), bf16[64,1,8]{2,1,0:T(2,128)(2,1)S(1)}, u32[]{:S(2)}, u32[]{:S(2)}) async-start(bf16[64,1,8]{2,1,0:T(2,128)(2,1)} %all_to_all.27), calls=%async_computation.3 | async-start | bytes 65536 | tf_op jit(solution)/shard_map/all_to_all | solution.py:51
  157.6 2.9 convolution_convert_fusion
  160.5 3.2 %scatter_custom_fusion.1 = bf16[512,1024]{1,0:T(8,128)(2,1)} fusion(s32[256]{0:T(256)S(1)} %bitcast.61, bf16[256,1024]{1,0:T(8,128)(2,1)} %convolution_convert_fusion, bf16[]{:T(256)} %constant.65.clone.1), kind=kCustom, calls=%fused_computation.18 | custom fusion | bytes 1049088 | tf_op jit(solution)/shard_map/scatter | solution.py:45
  163.6 7.3 %all-to-all-done.3 = bf16[64,1,8]{2,1,0:T(2,128)(2,1)S(1)} async-done(((bf16[64,1,8]{2,1,0:T(2,128)(2,1)}), bf16[64,1,8]{2,1,0:T(2,128)(2,1)S(1)}, u32[]{:S(2)}, u32[]{:S(2)}) %all-to-all-start.3) | async-done | bytes 1056 | tf_op jit(solution)/shard_map/all_to_all | solution.py:51
  171.0 7.3 %all-to-all-start.2 = ((bf16[64,8,1024]{2,1,0:T(8,128)(2,1)}), bf16[64,8,1024]{2,1,0:T(8,128)(2,1)}, u32[]{:S(2)}, u32[]{:S(2)}) async-start(bf16[64,8,1024]{2,1,0:T(8,128)(2,1)} %bitcast.54), calls=%async_computation.2 | async-start | bytes 2097152 | tf_op jit(solution)/shard_map/all_to_all | solution.py:48
  178.3 0.0 all-reduce.2.cloned.1.call-start
  178.3 0.5 broadcast.236
  178.8 0.7 reduce.10
  179.6 0.1 eq.45
  179.6 0.1 reduce.6
  179.7 0.1 reshape.233
  179.8 49.1 %all-to-all-done.2 = bf16[64,8,1024]{2,1,0:T(8,128)(2,1)} async-done(((bf16[64,8,1024]{2,1,0:T(8,128)(2,1)}), bf16[64,8,1024]{2,1,0:T(8,128)(2,1)}, u32[]{:S(2)}, u32[]{:S(2)}) %all-to-all-start.2) | async-done | bytes 1048608 | tf_op jit(solution)/shard_map/all_to_all | solution.py:48
  229.0 2.3 fusion.3
  231.3 0.0 all-reduce.2.cloned.1.call-update
  231.3 0.2 convolution_bitcast_fusion
  231.5 17.1 %psum.23 = f32[128]{0:T(128)S(1)} all-reduce(f32[128]{0:T(128)S(1)} %convolution_bitcast_fusion), channel_id=1, replica_groups=mesh['wide'=64,'narrow'=8] {'narrow'}, use_global_device_ids=true, to_apply=%region_13.14 | all-reduce | flops 128 | bytes 1024 | tf_op jit(solution)/shard_map/psum | solution.py:66
  248.6 0.0 copy-start.2
  248.6 51.3 %all-reduce.2.cloned.1.call-done = f32[128,1024]{1,0:T(8,128)} async-done(((f32[128,1024]{1,0:T(8,128)}), f32[128,1024]{1,0:T(8,128)}) %all-reduce.2.cloned.1.call-update) | async-done | bytes 524304 | tf_op jit(solution)/shard_map/psum | solution.py:66
  299.9 1.9 add_divide_fusion
  301.9 0.0 copy-done.2
  (12 shorter events, 0.1 us)
Async XLA Ops:
  7.2 102.1 %copy-start = (bf16[1536,1024]{1,0:T(8,128)(2,1)S(1)}, bf16[1536,1024]{1,0:T(8,128)(2,1)}, u32[]{:S(2)}) copy-start(bf16[1536,1024]{1,0:T(8,128)(2,1)} %param.5) | copy-start | bytes 9437188
  7.2 38.7 %copy-start.1 = (bf16[128,1024]{1,0:T(8,128)(2,1)S(1)}, bf16[128,1024]{1,0:T(8,128)(2,1)}, u32[]{:S(2)}) copy-start(bf16[128,1024]{1,0:T(8,128)(2,1)} %param.9) | copy-start | bytes 786436
  48.7 55.6 %all-to-all-start.1 = ((bf16[64,8,1024]{2,1,0:T(8,128)(2,1)}), bf16[64,8,1024]{2,1,0:T(8,128)(2,1)}, u32[]{:S(2)}, u32[]{:S(2)}) async-start(bf16[64,8,1024]{2,1,0:T(8,128)(2,1)} %bitcast.53), calls=%async_computation.1 | async-start | bytes 2097152 | tf_op jit(solution)/shard_map/all_to_all | solution.py:32
  150.2 20.7 %all-to-all-start.3 = ((bf16[64,1,8]{2,1,0:T(2,128)(2,1)}), bf16[64,1,8]{2,1,0:T(2,128)(2,1)S(1)}, u32[]{:S(2)}, u32[]{:S(2)}) async-start(bf16[64,1,8]{2,1,0:T(2,128)(2,1)} %all_to_all.27), calls=%async_computation.3 | async-start | bytes 65536 | tf_op jit(solution)/shard_map/all_to_all | solution.py:51
  171.0 58.0 %all-to-all-start.2 = ((bf16[64,8,1024]{2,1,0:T(8,128)(2,1)}), bf16[64,8,1024]{2,1,0:T(8,128)(2,1)}, u32[]{:S(2)}, u32[]{:S(2)}) async-start(bf16[64,8,1024]{2,1,0:T(8,128)(2,1)} %bitcast.54), calls=%async_computation.2 | async-start | bytes 2097152 | tf_op jit(solution)/shard_map/all_to_all | solution.py:48
  178.3 121.7 %all-reduce.2.cloned.1.call-start = ((), (), s32[]{:S(2)}) async-start(), calls=%async_computation.4 | async-start | bytes 1048576 | tf_op jit(solution)/shard_map/psum | solution.py:66
  248.6 53.2 %copy-start.2 = (f32[128]{0:T(128)}, f32[128]{0:T(128)S(1)}, u32[]{:S(2)}) copy-start(f32[128]{0:T(128)S(1)} %psum.23) | copy-start | bytes 1540
Sparse Core Ops, SparseCore 0:
  231.4 68.4 all-reduce.1
where the time goes:
time: 310 us; the launch traced here: 309 us
  waiting for transfers between devices  158 us (51%)
  blocking collectives  80.1 us (26%)
  starting transfers between devices  20.1 us (6%)
  local copies, waits for them, and re-layouts  17 us (5%)
  between operations  15 us (5%)
  other arithmetic  9.98 us (3%)
  matrix products  8.63 us (3%)
    psum x1, waiting for transfers between devices, shards(): totals, weight = lax.psum((totals, weight), 'narrow')  51.3 us
    all_to_all x1, waiting for transfers between devices, shards(): lax.all_to_all(outgoing, 'wide', split_axis=0, concat_axis=0, tiled=True)  50.1 us
    all_to_all x1, waiting for transfers between devices, shards(): lax.all_to_all(sum_slots.reshape(wide_n, slots, width), 'wide', split_axi...  49.1 us
    all_to_all x1, blocking collectives, shards(): lax.all_to_all(request, 'wide', split_axis=0, concat_axis=0, tiled=True)  32.4 us
    pmax x1, blocking collectives, shards(): top = lax.pmax(local_best_scores, 'narrow')  18.1 us
    psum x1, blocking collectives, shards(): totals, weight = lax.psum((totals, weight), 'narrow')  17.1 us
    psum x1, blocking collectives, shards(): total = lax.psum(jnp.sum(expo, axis=1), 'narrow')  12.5 us
    all_to_all x1, waiting for transfers between devices, shards(): lax.all_to_all(mass_slots.reshape(wide_n, slots), 'wide', split_axis=0, c...  7.34 us
  transfers between devices with their start and end apart: 4, of which 4 were waited for; matrix products, arithmetic and copies ran while one was open for 3% of the time, Pallas kernels for 0%

commit v1 on v0

v1 whole, which is shorter than its diff:
```python
import functools

import jax
import jax.numpy as jnp
from jax import lax
from jax.experimental import pallas as pl
from jax.experimental.pallas import tpu as pltpu
from jax.sharding import Mesh, PartitionSpec as P

temper = 0.1
prior = 0.01
gone = -3e38
f32 = jnp.float32
bf16 = jnp.bfloat16
i32 = jnp.int32
near = (0, 1, 2, -1)
lane = 128


def vmem(n):
    return [pl.BlockSpec(memory_space=pltpu.VMEM)] * n


def params():
    return pltpu.CompilerParams(vmem_limit_bytes=40 * 1024 * 1024)


def mask_kernel(place_ref, lists_ref, owner_ref, mask_ref):
    cluster, z, x, n = (place_ref[i] for i in range(4))
    ids = lists_ref[pl.ds(cluster, 1), :]
    count = ids.shape[1]
    blocks = owner_ref.shape[0]
    in_block = lax.broadcasted_iota(i32, (lane, count), 0)
    which = (lax.broadcasted_iota(i32, (blocks, count), 0) == (ids >> 7)).astype(bf16)
    here = in_block == (ids & 127)
    rows = owner_ref[...]

    def pick(table):
        found = lax.dot_general(
            table.astype(f32).astype(bf16),
            which,
            (((0,), (0,)), ((), ())),
            preferred_element_type=f32,
        )
        return jnp.sum(jnp.where(here, found, 0.0), axis=0, keepdims=True).astype(i32)

    owner = pick(rows >> 7)
    inner = pick(rows & 127)
    dx = ((owner & 3) - x) & 3
    dz = ((owner >> 2) - z) & 15
    j = dz & 3
    k = jnp.where(j == 3, ((dz + 1) >> 2) & 3, dz >> 2)
    row = ((dx * 4 + j) * 4 + k) * 16 + (inner & 15)
    mine = (inner >> 4) == n
    block = jnp.where(mine, row >> 7, lane)
    left = (in_block == (row & 127)).astype(bf16)
    right = (in_block == block).astype(bf16)
    mask_ref[...] = lax.dot_general(
        left, right, (((1,), (1,)), ((), ())), preferred_element_type=f32
    )


def score_kernel(piece, means_ref, points_ref, mask_ref, expo_ref, stat_ref):
    means = means_ref[...]
    wide = means.astype(f32)
    norms = jnp.sum(wide * wide, axis=1, keepdims=True)
    first = piece * (means.shape[0] // lane)
    listed = jnp.concatenate(
        [mask_ref[:, first + i : first + i + 1] for i in range(means.shape[0] // lane)], axis=0
    )
    bias = jnp.where(listed > 0.5, norms * (-1.0 / temper), gone)
    step = 256

    def body(c, _):
        at = pl.ds(pl.multiple_of(c * step, step), step)
        dots = lax.dot_general(
            means, points_ref[at, :], (((1,), (1,)), ((), ())), preferred_element_type=f32
        )
        t = dots * (2.0 / temper) + bias
        t = jnp.where(listed > 0.5, t, gone)
        top = jnp.max(t, axis=0, keepdims=True)
        expo = jnp.exp(t - top)
        expo_ref[:, at] = expo
        stat_ref[0:1, at] = top
        stat_ref[1:2, at] = jnp.sum(expo, axis=0, keepdims=True)
        return 0

    lax.fori_loop(0, points_ref.shape[0] // step, body, 0)


def sums_kernel(expo_ref, stat_ref, all_ref, points_ref, out_ref):
    tops = all_ref[:, 0, :]
    top = jnp.max(tops, axis=0, keepdims=True)
    total = jnp.sum(all_ref[:, 1, :] * jnp.exp(tops - top), axis=0, keepdims=True)
    scale = jnp.exp(stat_ref[0:1, :] - top) / total
    resp = (expo_ref[...] * scale).astype(bf16)
    width = points_ref.shape[1]
    step = 256
    for c in range(width // step):
        at = slice(c * step, (c + 1) * step)
        out_ref[:, at] = jnp.dot(
            resp, points_ref[:, at], preferred_element_type=f32
        ).astype(bf16)
    mass = jnp.sum(resp.astype(f32), axis=1, keepdims=True)
    lanes = lax.broadcasted_iota(i32, (resp.shape[0], lane), 1)
    out_ref[:, width:] = jnp.where(lanes == 0, mass, 0.0).astype(bf16)


def added(refs, width):
    total = functools.reduce(lambda a, b: a + b, [r[:, :width].astype(f32) for r in refs])
    mass = functools.reduce(lambda a, b: a + b, [r[:, width:].astype(f32) for r in refs])
    return total, mass[:, 0:1] + mass[:, 1:2]


def add_kernel(a, b, c, d, *outs):
    width = a.shape[1] - lane
    total, mass = added((a, b, c, d), width)
    high = mass.astype(bf16).astype(f32)
    lanes = lax.broadcasted_iota(i32, (a.shape[0], lane), 1)
    tail = jnp.where(lanes == 0, high, jnp.where(lanes == 1, mass - high, 0.0)).astype(bf16)
    total = total.astype(bf16)
    rows = a.shape[0] // 4
    for k, out in enumerate(outs):
        out[:, :width] = total[k * rows : (k + 1) * rows]
        out[:, width:] = tail[k * rows : (k + 1) * rows]


def last_kernel(a, b, c, d, cen, out):
    width = cen.shape[1]
    total, mass = added((a, b, c, d), width)
    out[:, :width] = (total + prior * cen[...].astype(f32)) / (mass + prior)
    out[:, width:] = jnp.broadcast_to(mass, (mass.shape[0], lane))


def shifted(a, axis, by):
    n = lax.axis_size(axis)
    return lax.ppermute(a, axis, [(i, (i + by) % n) for i in range(n)])


def call(kernel, outs, args, specs=None, flops=0, moved=0):
    return pl.pallas_call(
        kernel,
        out_shape=outs,
        in_specs=specs or vmem(len(args)),
        out_specs=jax.tree.map(lambda _: pl.BlockSpec(memory_space=pltpu.VMEM), outs),
        compiler_params=params(),
        cost_estimate=pl.CostEstimate(flops=flops, bytes_accessed=moved, transcendentals=0),
    )(*args)


def shards(points, coarse_ids, lists, owner_map, centroids):
    z, x = lax.axis_index("z"), lax.axis_index("x")
    n = lax.axis_index(("y", "c"))
    count, width = points.shape
    held = centroids.shape[0]
    rows = held // lax.axis_size(("y", "c"))
    sds = jax.ShapeDtypeStruct

    own = lax.dynamic_slice(centroids, (n * rows, 0), (rows, width))
    far = [own] + [shifted(own, "z", -4 * k) for k in (1, 2, 3)]
    group = jnp.concatenate(far, axis=0)
    close = [group] + [shifted(group, "z", -d) for d in near[1:]]
    column = jnp.concatenate(close, axis=0)
    pieces = [column] + [shifted(column, "x", -d) for d in near[1:]]

    place = jnp.stack([coarse_ids[0], z, x, n]).astype(i32)
    mask = call(
        mask_kernel,
        sds((lane, lane), f32),
        (place, lists, owner_map.reshape(-1, lane)),
        [pl.BlockSpec(memory_space=pltpu.SMEM)] + vmem(2),
        moved=4 << 20,
    )
    size = column.shape[0]
    flops = 2 * size * count * width
    scored = [
        call(
            functools.partial(score_kernel, i),
            (sds((size, count), f32), sds((2, count), f32)),
            (piece, points, mask),
            flops=flops,
            moved=4 << 20,
        )
        for i, piece in enumerate(pieces)
    ]
    tops = jnp.stack([s[0] for _, s in scored])
    totals = jnp.stack([s[1] for _, s in scored])
    top = jnp.max(tops, axis=0)
    total = jnp.sum(totals * jnp.exp(tops - top), axis=0)
    both = jnp.stack([top, total])
    shared = lax.all_to_all(
        jnp.broadcast_to(both, (lax.axis_size(("y", "c")), 2, count)), ("y", "c"), 0, 0, tiled=True
    )
    padded = width + lane
    back = [None] * 4
    for i in (2, 1, 3, 0):
        expo, stat = scored[i]
        out = call(
            sums_kernel,
            sds((size, padded), bf16),
            (expo, stat, shared, points),
            flops=flops,
            moved=4 << 20,
        )
        back[i] = shifted(out, "x", near[i]) if i else out
    parts = call(add_kernel, tuple(sds((size // 4, padded), bf16) for _ in near), tuple(back))
    back = [parts[0]] + [shifted(parts[i], "z", near[i]) for i in (1, 2, 3)]
    parts = call(add_kernel, tuple(sds((size // 16, padded), bf16) for _ in near), tuple(back))
    back = [parts[0]] + [shifted(parts[k], "z", 4 * k) for k in (1, 2, 3)]
    table = call(last_kernel, sds((rows, padded), f32), tuple(back) + (own,))
    whole = lax.all_gather(table, ("y", "c"), axis=0, tiled=True)
    return whole[:, :width], whole[:, width]


def solution(mesh):
    chips = Mesh(mesh.devices.reshape(16, 4, 4, 2), ("z", "x", "y", "c"))
    wide = ("z", "x")
    return jax.shard_map(
        shards,
        mesh=chips,
        in_specs=(P(wide, None), P(wide), P(), P(), P(wide, None)),
        out_specs=(P(wide, None), P(wide)),
        check_vma=False,
    )
```

time: 310 us -> 181 us (0.58)
  waiting for transfers between devices: 158 us -> 47.4 us
  starting transfers between devices: 20.1 us -> 80.3 us
  blocking collectives: 80.1 us -> 27.1 us
  Pallas kernels: 0 us -> 17.4 us
  between operations: 15 us -> 1.65 us
  local copies, waits for them, and re-layouts: 17 us -> 5.87 us
  other arithmetic: 9.98 us -> 0.23 us
  matrix products: 8.63 us -> 0 us
    all_to_all x3 -> x0, waiting for transfers between devices: 107 us -> none  [the longest x1 50.1 us: shards(): lax.all_to_all(outgoing, 'wide', split_axis=0, concat_axis=0, tiled=True)]
    ppermute x0 -> x18, starting transfers between devices: none -> 80.3 us  [shifted(): return lax.ppermute(a, axis, [(i, (i + by) % n) for i in range(n)])]
    psum x1 -> x0, waiting for transfers between devices: 51.3 us -> none  [shards(): totals, weight = lax.psum((totals, weight), 'narrow')]
    ppermute x0 -> x18, waiting for transfers between devices: none -> 47.4 us  [shifted(): return lax.ppermute(a, axis, [(i, (i + by) % n) for i in range(n)])]
    psum x2 -> x0, blocking collectives: 29.6 us -> none  [the longest x1 17.1 us: shards(): totals, weight = lax.psum((totals, weight), 'narrow')]
    all_to_all x1, blocking collectives: 32.4 us -> 9.74 us  [shards(): lax.all_to_all(jnp.broadcast_to(both, (lax.axis_size(('y', 'c')), 2, coun...]
    all_to_all x3 -> x0, starting transfers between devices: 20.1 us -> none  [the longest x1 7.3 us: shards(): lax.all_to_all(mass_slots.reshape(wide_n, slots), 'wide', split_axis=0, c...]
    pmax x1 -> x0, blocking collectives: 18.1 us -> none  [shards(): top = lax.pmax(local_best_scores, 'narrow')]
  transfers between devices with their start and end apart: 4 -> 18, of which waited for: 4 -> 9; matrix products, arithmetic and copies ran while one was open for 3% -> 0% of each run, Pallas kernels for 0% -> 7%
where the time goes in v1:
time: 181 us; the launch traced here: 180 us
  starting transfers between devices  80.3 us (44%)
  waiting for transfers between devices  47.4 us (26%)
  blocking collectives  27.1 us (15%)
  Pallas kernels  17.4 us (10%)
  local copies, waits for them, and re-layouts  5.87 us (3%)
    ppermute x18, starting transfers between devices, shifted(): return lax.ppermute(a, axis, [(i, (i + by) % n) for i in range(n)])  80.3 us
    ppermute x18, waiting for transfers between devices, shifted(): return lax.ppermute(a, axis, [(i, (i + by) % n) for i in range(n)])  47.4 us
    all_gather x1, blocking collectives, shards(): whole = lax.all_gather(table, ('y', 'c'), axis=0, tiled=True)  17.4 us
    pallas_call x12, Pallas kernels, call(): pl.pallas_call(kernel, out_shape=outs, in_specs=specs or vmem(len(args)),...  17.4 us
    all_to_all x1, blocking collectives, shards(): lax.all_to_all(jnp.broadcast_to(both, (lax.axis_size(('y', 'c')), 2, coun...  9.74 us
    unnamed x14, local copies, waits for them, and re-layouts  4.36 us
  transfers between devices with their start and end apart: 18, of which 9 were waited for; matrix products, arithmetic and copies ran while one was open for 0% of the time, Pallas kernels for 7%

profile of v1, /device:TPU:1, one launch (start us, length us, event | category | flops | bytes accessed | tf_op | source)
XLA Modules:
  0.0 179.9 jit_solution(14318320907295775461)
XLA Ops:
  0.6 0.8 constant_dynamic-update-slice_fusion.6
  1.4 9.6 %collective-permute-start.2 = (bf16[16,1024]{1,0:T(8,128)(2,1)S(1)}, bf16[16,1024]{1,0:T(8,128)(2,1)S(1)}, u32[]{:S(2)}, u32[]{:S(2)}) collective-permute-start(bf16[16,1024]{1,0:T(8,128)(2,1)S(1)} %get-tuple-element.37.cen), channel_id=1, source_target_pairs={{0,128},{32,160},{64,192},{96,224},{128,256},{160,288},{192,320},{... | collective-permute-start | bytes 98312 | tf_op jit(solution)/shard_map/ppermute | solution.py:137
  11.0 10.6 %collective-permute-start.1 = (bf16[16,1024]{1,0:T(8,128)(2,1)S(1)}, bf16[16,1024]{1,0:T(8,128)(2,1)S(1)}, u32[]{:S(2)}, u32[]{:S(2)}) collective-permute-start(bf16[16,1024]{1,0:T(8,128)(2,1)S(1)} %get-tuple-element.37.cen), channel_id=1, source_target_pairs={{0,256},{32,288},{64,320},{96,352},{128,384},{160,416},{192,448},{... | collective-permute-start | bytes 98312 | tf_op jit(solution)/shard_map/ppermute | solution.py:137
  21.7 5.2 %collective-permute-start = (bf16[16,1024]{1,0:T(8,128)(2,1)S(1)}, bf16[16,1024]{1,0:T(8,128)(2,1)S(1)}, u32[]{:S(2)}, u32[]{:S(2)}) collective-permute-start(bf16[16,1024]{1,0:T(8,128)(2,1)S(1)} %get-tuple-element.37.cen), channel_id=1, source_target_pairs={{0,384},{32,416},{64,448},{96,480},{128,0},{160,32},{192,64},{224,... | collective-permute-start | bytes 98312 | tf_op jit(solution)/shard_map/ppermute | solution.py:137
  26.9 3.4 %collective-permute-done = bf16[16,1024]{1,0:T(8,128)(2,1)S(1)} collective-permute-done((bf16[16,1024]{1,0:T(8,128)(2,1)S(1)}, bf16[16,1024]{1,0:T(8,128)(2,1)S(1)}, u32[]{:S(2)}, u32[]{:S(2)}) %collective-permute-start) | collective-permute-done | bytes 32800 | tf_op jit(solution)/shard_map/ppermute | solution.py:137
  30.3 2.8 %collective-permute-start.5 = (bf16[64,1024]{1,0:T(8,128)(2,1)S(1)}, bf16[64,1024]{1,0:T(8,128)(2,1)S(1)}, u32[]{:S(2)}, u32[]{:S(2)}) collective-permute-start(bf16[64,1024]{1,0:T(8,128)(2,1)S(1)} %pad_maximum_fusion), channel_id=1, source_target_pairs={{0,32},{32,64},{64,96},{96,128},{128,160},{160,192},{192,224},{224... | collective-permute-start | bytes 393224 | tf_op jit(solution)/shard_map/ppermute | solution.py:137
  33.0 4.2 %collective-permute-start.4 = (bf16[64,1024]{1,0:T(8,128)(2,1)S(1)}, bf16[64,1024]{1,0:T(8,128)(2,1)S(1)}, u32[]{:S(2)}, u32[]{:S(2)}) collective-permute-start(bf16[64,1024]{1,0:T(8,128)(2,1)S(1)} %pad_maximum_fusion), channel_id=1, source_target_pairs={{0,448},{32,480},{64,0},{96,32},{128,64},{160,96},{192,128},{224,1... | collective-permute-start | bytes 393224 | tf_op jit(solution)/shard_map/ppermute | solution.py:137
  37.2 2.6 %collective-permute-start.3 = (bf16[64,1024]{1,0:T(8,128)(2,1)S(1)}, bf16[64,1024]{1,0:T(8,128)(2,1)S(1)}, u32[]{:S(2)}, u32[]{:S(2)}) collective-permute-start(bf16[64,1024]{1,0:T(8,128)(2,1)S(1)} %pad_maximum_fusion), channel_id=1, source_target_pairs={{0,480},{32,0},{64,32},{96,64},{128,96},{160,128},{192,160},{224,1... | collective-permute-start | bytes 393224 | tf_op jit(solution)/shard_map/ppermute | solution.py:137
  39.9 5.7 %collective-permute-done.3 = bf16[64,1024]{1,0:T(8,128)(2,1)S(1)} collective-permute-done((bf16[64,1024]{1,0:T(8,128)(2,1)S(1)}, bf16[64,1024]{1,0:T(8,128)(2,1)S(1)}, u32[]{:S(2)}, u32[]{:S(2)}) %collective-permute-start.3) | collective-permute-done | bytes 131104 | tf_op jit(solution)/shard_map/ppermute | solution.py:137
  45.6 4.4 %collective-permute-start.6 = (bf16[256,1024]{1,0:T(8,128)(2,1)S(1)}, bf16[256,1024]{1,0:T(8,128)(2,1)S(1)}, u32[]{:S(2)}, u32[]{:S(2)}) collective-permute-start(bf16[256,1024]{1,0:T(8,128)(2,1)S(1)} %constant_dynamic-update-slice_fusion.means_ref), channel_id=1, source_target_pairs={{0,24},{8,0},{16,8},{24,16},{1,25},{9,1},{17,9},{25,17},{2,26},{10... | collective-permute-start | bytes 1572872 | tf_op jit(solution)/shard_map/ppermute | solution.py:137
  50.0 2.4 %collective-permute-start.7 = (bf16[256,1024]{1,0:T(8,128)(2,1)S(1)}, bf16[256,1024]{1,0:T(8,128)(2,1)S(1)}, u32[]{:S(2)}, u32[]{:S(2)}) collective-permute-start(bf16[256,1024]{1,0:T(8,128)(2,1)S(1)} %constant_dynamic-update-slice_fusion.means_ref), channel_id=1, source_target_pairs={{0,16},{8,24},{16,0},{24,8},{1,17},{9,25},{17,1},{25,9},{2,18},{10... | collective-permute-start | bytes 1572872 | tf_op jit(solution)/shard_map/ppermute | solution.py:137
  52.5 2.5 %collective-permute-start.8 = (bf16[256,1024]{1,0:T(8,128)(2,1)S(1)}, bf16[256,1024]{1,0:T(8,128)(2,1)S(1)}, u32[]{:S(2)}, u32[]{:S(2)}) collective-permute-start(bf16[256,1024]{1,0:T(8,128)(2,1)S(1)} %constant_dynamic-update-slice_fusion.means_ref), channel_id=1, source_target_pairs={{0,8},{8,16},{16,24},{24,0},{1,9},{9,17},{17,25},{25,1},{2,10},{10... | collective-permute-start | bytes 1572872 | tf_op jit(solution)/shard_map/ppermute | solution.py:137
  55.6 0.1 pad_add_fusion.place_ref
  55.7 0.9 copy-done.2
  56.6 0.8 copy-done.3
  57.4 1.5 shard_map.68.mask_ref
  58.9 1.9 %copy-done = bf16[1536,1024]{1,0:T(8,128)(2,1)S(1)} copy-done((bf16[1536,1024]{1,0:T(8,128)(2,1)S(1)}, bf16[1536,1024]{1,0:T(8,128)(2,1)}, u32[]{:S(2)}) %copy-start) | copy-done | bytes 3145752
  60.8 2.7 %shard_map.69 = (f32[256,1536]{1,0:T(8,128)S(1)}, f32[2,1536]{1,0:T(2,128)S(1)}) custom-call(bf16[256,1024]{1,0:T(8,128)(2,1)S(1)} %constant_dynamic-update-slice_fusion.means_ref, bf16[1536,1024]{1,0:T(8,128)(2,1)S(1)} %copy-done, f32[128,128]{1,0:T(8,128)S(1)} %shard_map.68.mask_ref), custom_call_target="tpu_custom_call" | custom-call | flops 805306368 | bytes 4194304 | tf_op jit(solution)/shard_map/pallas_call | solution.py:141
  63.6 2.8 %shard_map.70 = (f32[256,1536]{1,0:T(8,128)S(1)}, f32[2,1536]{1,0:T(2,128)S(1)}) custom-call(bf16[256,1024]{1,0:T(8,128)(2,1)S(1)} %collective-permute-done.6.means_ref, bf16[1536,1024]{1,0:T(8,128)(2,1)S(1)} %copy-done.1, f32[128,128]{1,0:T(8,128)S(1)} %shard_map.68.mask_ref), custom_call_target="tpu_custom_call" | custom-call | flops 805306368 | bytes 4194304 | tf_op jit(solution)/shard_map/pallas_call | solution.py:141
  66.3 2.8 %shard_map.71 = (f32[256,1536]{1,0:T(8,128)S(1)}, f32[2,1536]{1,0:T(2,128)S(1)}) custom-call(bf16[256,1024]{1,0:T(8,128)(2,1)S(1)} %collective-permute-done.7.means_ref, bf16[1536,1024]{1,0:T(8,128)(2,1)S(1)} %copy-done.1, f32[128,128]{1,0:T(8,128)S(1)} %shard_map.68.mask_ref), custom_call_target="tpu_custom_call" | custom-call | flops 805306368 | bytes 4194304 | tf_op jit(solution)/shard_map/pallas_call | solution.py:141
  69.1 9.4 %collective-permute-done.8.means_ref = bf16[256,1024]{1,0:T(8,128)(2,1)S(1)} collective-permute-done((bf16[256,1024]{1,0:T(8,128)(2,1)S(1)}, bf16[256,1024]{1,0:T(8,128)(2,1)S(1)}, u32[]{:S(2)}, u32[]{:S(2)}) %collective-permute-start.8) | collective-permute-done | bytes 524320 | tf_op jit(solution)/shard_map/ppermute | solution.py:137
  78.5 2.8 %shard_map.72 = (f32[256,1536]{1,0:T(8,128)S(1)}, f32[2,1536]{1,0:T(2,128)S(1)}) custom-call(bf16[256,1024]{1,0:T(8,128)(2,1)S(1)} %collective-permute-done.8.means_ref, bf16[1536,1024]{1,0:T(8,128)(2,1)S(1)} %copy-done.1, f32[128,128]{1,0:T(8,128)S(1)} %shard_map.68.mask_ref), custom_call_target="tpu_custom_call" | custom-call | flops 805306368 | bytes 4194304 | tf_op jit(solution)/shard_map/pallas_call | solution.py:141
  81.5 9.7 %all_to_all.5.all_ref = f32[8,2,1536]{2,1,0:T(2,128)S(1)} all-to-all(f32[8,2,1536]{2,1,0:T(2,128)S(1)} %broadcast_in_dim.4), channel_id=1, replica_groups=mesh['z'=16,'x'=4,'y'=4,'c'=2] {'y','c'}, dimensions={0} | all-to-all | bytes 196608 | tf_op jit(solution)/shard_map/all_to_all | solution.py:191
  91.2 1.0 shard_map.74
  92.2 1.9 %collective-permute-start.9 = (bf16[256,1152]{1,0:T(8,128)(2,1)S(1)}, bf16[256,1152]{1,0:T(8,128)(2,1)S(1)}, u32[]{:S(2)}, u32[]{:S(2)}) collective-permute-start(bf16[256,1152]{1,0:T(8,128)(2,1)S(1)} %shard_map.74), channel_id=1, source_target_pairs={{0,8},{8,16},{16,24},{24,0},{1,9},{9,17},{17,25},{25,1},{2,10},{10... | collective-permute-start | bytes 1769480 | tf_op jit(solution)/shard_map/ppermute | solution.py:137
  94.2 1.0 shard_map.75
  95.2 6.4 %collective-permute-start.10 = (bf16[256,1152]{1,0:T(8,128)(2,1)S(1)}, bf16[256,1152]{1,0:T(8,128)(2,1)S(1)}, u32[]{:S(2)}, u32[]{:S(2)}) collective-permute-start(bf16[256,1152]{1,0:T(8,128)(2,1)S(1)} %shard_map.75), channel_id=1, source_target_pairs={{0,16},{8,24},{16,0},{24,8},{1,17},{9,25},{17,1},{25,9},{2,18},{10... | collective-permute-start | bytes 1769480 | tf_op jit(solution)/shard_map/ppermute | solution.py:137
  101.6 1.0 shard_map.76
  102.6 1.9 %collective-permute-start.11 = (bf16[256,1152]{1,0:T(8,128)(2,1)S(1)}, bf16[256,1152]{1,0:T(8,128)(2,1)S(1)}, u32[]{:S(2)}, u32[]{:S(2)}) collective-permute-start(bf16[256,1152]{1,0:T(8,128)(2,1)S(1)} %shard_map.76), channel_id=1, source_target_pairs={{0,24},{8,0},{16,8},{24,16},{1,25},{9,1},{17,9},{25,17},{2,26},{10... | collective-permute-start | bytes 1769480 | tf_op jit(solution)/shard_map/ppermute | solution.py:137
  104.5 1.0 shard_map.73.a
  105.5 4.8 %collective-permute-done.9.b = bf16[256,1152]{1,0:T(8,128)(2,1)S(1)} collective-permute-done((bf16[256,1152]{1,0:T(8,128)(2,1)S(1)}, bf16[256,1152]{1,0:T(8,128)(2,1)S(1)}, u32[]{:S(2)}, u32[]{:S(2)}) %collective-permute-start.9) | collective-permute-done | bytes 589856 | tf_op jit(solution)/shard_map/ppermute | solution.py:137
  110.4 13.5 %collective-permute-done.10.c = bf16[256,1152]{1,0:T(8,128)(2,1)S(1)} collective-permute-done((bf16[256,1152]{1,0:T(8,128)(2,1)S(1)}, bf16[256,1152]{1,0:T(8,128)(2,1)S(1)}, u32[]{:S(2)}, u32[]{:S(2)}) %collective-permute-start.10) | collective-permute-done | bytes 589856 | tf_op jit(solution)/shard_map/ppermute | solution.py:137
  123.8 2.6 %collective-permute-done.11.d = bf16[256,1152]{1,0:T(8,128)(2,1)S(1)} collective-permute-done((bf16[256,1152]{1,0:T(8,128)(2,1)S(1)}, bf16[256,1152]{1,0:T(8,128)(2,1)S(1)}, u32[]{:S(2)}, u32[]{:S(2)}) %collective-permute-start.11) | collective-permute-done | bytes 589856 | tf_op jit(solution)/shard_map/ppermute | solution.py:137
  126.4 0.5 shard_map.77
  126.9 3.0 %collective-permute-start.12 = (bf16[64,1152]{1,0:T(8,128)(2,1)S(1)}, bf16[64,1152]{1,0:T(8,128)(2,1)S(1)}, u32[]{:S(2)}, u32[]{:S(2)}) collective-permute-start(bf16[64,1152]{1,0:T(8,128)(2,1)S(1)} %get-tuple-element.27), channel_id=1, source_target_pairs={{0,32},{32,64},{64,96},{96,128},{128,160},{160,192},{192,224},{224... | collective-permute-start | bytes 442376 | tf_op jit(solution)/shard_map/ppermute | solution.py:137
  129.9 3.3 %collective-permute-start.13 = (bf16[64,1152]{1,0:T(8,128)(2,1)S(1)}, bf16[64,1152]{1,0:T(8,128)(2,1)S(1)}, u32[]{:S(2)}, u32[]{:S(2)}) collective-permute-start(bf16[64,1152]{1,0:T(8,128)(2,1)S(1)} %get-tuple-element.28), channel_id=1, source_target_pairs={{0,64},{32,96},{64,128},{96,160},{128,192},{160,224},{192,256},{22... | collective-permute-start | bytes 442376 | tf_op jit(solution)/shard_map/ppermute | solution.py:137
  133.3 2.9 %collective-permute-start.14 = (bf16[64,1152]{1,0:T(8,128)(2,1)S(1)}, bf16[64,1152]{1,0:T(8,128)(2,1)S(1)}, u32[]{:S(2)}, u32[]{:S(2)}) collective-permute-start(bf16[64,1152]{1,0:T(8,128)(2,1)S(1)} %get-tuple-element.29), channel_id=1, source_target_pairs={{0,480},{32,0},{64,32},{96,64},{128,96},{160,128},{192,160},{224,1... | collective-permute-start | bytes 442376 | tf_op jit(solution)/shard_map/ppermute | solution.py:137
  136.2 2.9 %collective-permute-done.13.c = bf16[64,1152]{1,0:T(8,128)(2,1)S(1)} collective-permute-done((bf16[64,1152]{1,0:T(8,128)(2,1)S(1)}, bf16[64,1152]{1,0:T(8,128)(2,1)S(1)}, u32[]{:S(2)}, u32[]{:S(2)}) %collective-permute-start.13) | collective-permute-done | bytes 147488 | tf_op jit(solution)/shard_map/ppermute | solution.py:137
  139.1 0.4 collective-permute-done.14.d
  139.4 0.2 shard_map.78
  139.6 7.0 %collective-permute-start.15 = (bf16[16,1152]{1,0:T(8,128)(2,1)S(1)}, bf16[16,1152]{1,0:T(8,128)(2,1)S(1)}, u32[]{:S(2)}, u32[]{:S(2)}) collective-permute-start(bf16[16,1152]{1,0:T(8,128)(2,1)S(1)} %get-tuple-element.31), channel_id=1, source_target_pairs={{0,128},{32,160},{64,192},{96,224},{128,256},{160,288},{192,320},{... | collective-permute-start | bytes 110600 | tf_op jit(solution)/shard_map/ppermute | solution.py:137
  146.6 3.9 %collective-permute-start.16 = (bf16[16,1152]{1,0:T(8,128)(2,1)S(1)}, bf16[16,1152]{1,0:T(8,128)(2,1)S(1)}, u32[]{:S(2)}, u32[]{:S(2)}) collective-permute-start(bf16[16,1152]{1,0:T(8,128)(2,1)S(1)} %get-tuple-element.32), channel_id=1, source_target_pairs={{0,256},{32,288},{64,320},{96,352},{128,384},{160,416},{192,448},{... | collective-permute-start | bytes 110600 | tf_op jit(solution)/shard_map/ppermute | solution.py:137
  150.5 5.5 %collective-permute-start.17 = (bf16[16,1152]{1,0:T(8,128)(2,1)S(1)}, bf16[16,1152]{1,0:T(8,128)(2,1)S(1)}, u32[]{:S(2)}, u32[]{:S(2)}) collective-permute-start(bf16[16,1152]{1,0:T(8,128)(2,1)S(1)} %get-tuple-element.33), channel_id=1, source_target_pairs={{0,384},{32,416},{64,448},{96,480},{128,0},{160,32},{192,64},{224,... | collective-permute-start | bytes 110600 | tf_op jit(solution)/shard_map/ppermute | solution.py:137
  156.0 4.8 %collective-permute-done.16.c = bf16[16,1152]{1,0:T(8,128)(2,1)S(1)} collective-permute-done((bf16[16,1152]{1,0:T(8,128)(2,1)S(1)}, bf16[16,1152]{1,0:T(8,128)(2,1)S(1)}, u32[]{:S(2)}, u32[]{:S(2)}) %collective-permute-start.16) | collective-permute-done | bytes 36896 | tf_op jit(solution)/shard_map/ppermute | solution.py:137
  160.8 0.2 shard_map.79
  161.0 17.4 %all_gather.3 = f32[128,1152]{1,0:T(8,128)S(1)} all-gather(f32[16,1152]{1,0:T(8,128)S(1)} %shard_map.79), channel_id=1, replica_groups=mesh['z'=16,'x'=4,'y'=4,'c'=2] {'y','c'}, dimensions={0}, use_global_device_ids=true | all-gather | bytes 663552 | tf_op jit(solution)/shard_map/all_gather | solution.py:211
  178.4 0.6 slice_reduce_fusion
  179.0 0.8 slice.40
  (26 shorter events, 0.3 us)
Async XLA Ops:
  1.4 25.5 %collective-permute-start.2 = (bf16[16,1024]{1,0:T(8,128)(2,1)S(1)}, bf16[16,1024]{1,0:T(8,128)(2,1)S(1)}, u32[]{:S(2)}, u32[]{:S(2)}) collective-permute-start(bf16[16,1024]{1,0:T(8,128)(2,1)S(1)} %get-tuple-element.37.cen), channel_id=1, source_target_pairs={{0,128},{32,160},{64,192},{96,224},{128,256},{160,288},{192,320},{... | collective-permute-start | bytes 98312 | tf_op jit(solution)/shard_map/ppermute | solution.py:137
  11.0 15.8 %collective-permute-start.1 = (bf16[16,1024]{1,0:T(8,128)(2,1)S(1)}, bf16[16,1024]{1,0:T(8,128)(2,1)S(1)}, u32[]{:S(2)}, u32[]{:S(2)}) collective-permute-start(bf16[16,1024]{1,0:T(8,128)(2,1)S(1)} %get-tuple-element.37.cen), channel_id=1, source_target_pairs={{0,256},{32,288},{64,320},{96,352},{128,384},{160,416},{192,448},{... | collective-permute-start | bytes 98312 | tf_op jit(solution)/shard_map/ppermute | solution.py:137
  21.7 8.6 %collective-permute-start = (bf16[16,1024]{1,0:T(8,128)(2,1)S(1)}, bf16[16,1024]{1,0:T(8,128)(2,1)S(1)}, u32[]{:S(2)}, u32[]{:S(2)}) collective-permute-start(bf16[16,1024]{1,0:T(8,128)(2,1)S(1)} %get-tuple-element.37.cen), channel_id=1, source_target_pairs={{0,384},{32,416},{64,448},{96,480},{128,0},{160,32},{192,64},{224,... | collective-permute-start | bytes 98312 | tf_op jit(solution)/shard_map/ppermute | solution.py:137
  30.3 15.3 %collective-permute-start.5 = (bf16[64,1024]{1,0:T(8,128)(2,1)S(1)}, bf16[64,1024]{1,0:T(8,128)(2,1)S(1)}, u32[]{:S(2)}, u32[]{:S(2)}) collective-permute-start(bf16[64,1024]{1,0:T(8,128)(2,1)S(1)} %pad_maximum_fusion), channel_id=1, source_target_pairs={{0,32},{32,64},{64,96},{96,128},{128,160},{160,192},{192,224},{224... | collective-permute-start | bytes 393224 | tf_op jit(solution)/shard_map/ppermute | solution.py:137
  33.0 12.5 %collective-permute-start.4 = (bf16[64,1024]{1,0:T(8,128)(2,1)S(1)}, bf16[64,1024]{1,0:T(8,128)(2,1)S(1)}, u32[]{:S(2)}, u32[]{:S(2)}) collective-permute-start(bf16[64,1024]{1,0:T(8,128)(2,1)S(1)} %pad_maximum_fusion), channel_id=1, source_target_pairs={{0,448},{32,480},{64,0},{96,32},{128,64},{160,96},{192,128},{224,1... | collective-permute-start | bytes 393224 | tf_op jit(solution)/shard_map/ppermute | solution.py:137
  37.2 8.3 %collective-permute-start.3 = (bf16[64,1024]{1,0:T(8,128)(2,1)S(1)}, bf16[64,1024]{1,0:T(8,128)(2,1)S(1)}, u32[]{:S(2)}, u32[]{:S(2)}) collective-permute-start(bf16[64,1024]{1,0:T(8,128)(2,1)S(1)} %pad_maximum_fusion), channel_id=1, source_target_pairs={{0,480},{32,0},{64,32},{96,64},{128,96},{160,128},{192,160},{224,1... | collective-permute-start | bytes 393224 | tf_op jit(solution)/shard_map/ppermute | solution.py:137
  45.6 17.9 %collective-permute-start.6 = (bf16[256,1024]{1,0:T(8,128)(2,1)S(1)}, bf16[256,1024]{1,0:T(8,128)(2,1)S(1)}, u32[]{:S(2)}, u32[]{:S(2)}) collective-permute-start(bf16[256,1024]{1,0:T(8,128)(2,1)S(1)} %constant_dynamic-update-slice_fusion.means_ref), channel_id=1, source_target_pairs={{0,24},{8,0},{16,8},{24,16},{1,25},{9,1},{17,9},{25,17},{2,26},{10... | collective-permute-start | bytes 1572872 | tf_op jit(solution)/shard_map/ppermute | solution.py:137
  50.0 16.3 %collective-permute-start.7 = (bf16[256,1024]{1,0:T(8,128)(2,1)S(1)}, bf16[256,1024]{1,0:T(8,128)(2,1)S(1)}, u32[]{:S(2)}, u32[]{:S(2)}) collective-permute-start(bf16[256,1024]{1,0:T(8,128)(2,1)S(1)} %constant_dynamic-update-slice_fusion.means_ref), channel_id=1, source_target_pairs={{0,16},{8,24},{16,0},{24,8},{1,17},{9,25},{17,1},{25,9},{2,18},{10... | collective-permute-start | bytes 1572872 | tf_op jit(solution)/shard_map/ppermute | solution.py:137
  52.5 26.0 %collective-permute-start.8 = (bf16[256,1024]{1,0:T(8,128)(2,1)S(1)}, bf16[256,1024]{1,0:T(8,128)(2,1)S(1)}, u32[]{:S(2)}, u32[]{:S(2)}) collective-permute-start(bf16[256,1024]{1,0:T(8,128)(2,1)S(1)} %constant_dynamic-update-slice_fusion.means_ref), channel_id=1, source_target_pairs={{0,8},{8,16},{16,24},{24,0},{1,9},{9,17},{17,25},{25,1},{2,10},{10... | collective-permute-start | bytes 1572872 | tf_op jit(solution)/shard_map/ppermute | solution.py:137
  55.7 0.9 copy-start.2
  56.6 0.8 copy-start.3
  58.9 1.9 %copy-start = (bf16[1536,1024]{1,0:T(8,128)(2,1)S(1)}, bf16[1536,1024]{1,0:T(8,128)(2,1)}, u32[]{:S(2)}) copy-start(bf16[1536,1024]{1,0:T(8,128)(2,1)} %points_ref.15) | copy-start | bytes 9437188
  60.8 2.8 %copy-start.1 = (bf16[1536,1024]{1,0:T(8,128)(2,1)S(1)}, bf16[1536,1024]{1,0:T(8,128)(2,1)}, u32[]{:S(2)}) copy-start(bf16[1536,1024]{1,0:T(8,128)(2,1)} %points_ref.15) | copy-start | bytes 9437188
  92.2 18.1 %collective-permute-start.9 = (bf16[256,1152]{1,0:T(8,128)(2,1)S(1)}, bf16[256,1152]{1,0:T(8,128)(2,1)S(1)}, u32[]{:S(2)}, u32[]{:S(2)}) collective-permute-start(bf16[256,1152]{1,0:T(8,128)(2,1)S(1)} %shard_map.74), channel_id=1, source_target_pairs={{0,8},{8,16},{16,24},{24,0},{1,9},{9,17},{17,25},{25,1},{2,10},{10... | collective-permute-start | bytes 1769480 | tf_op jit(solution)/shard_map/ppermute | solution.py:137
  95.2 28.7 %collective-permute-start.10 = (bf16[256,1152]{1,0:T(8,128)(2,1)S(1)}, bf16[256,1152]{1,0:T(8,128)(2,1)S(1)}, u32[]{:S(2)}, u32[]{:S(2)}) collective-permute-start(bf16[256,1152]{1,0:T(8,128)(2,1)S(1)} %shard_map.75), channel_id=1, source_target_pairs={{0,16},{8,24},{16,0},{24,8},{1,17},{9,25},{17,1},{25,9},{2,18},{10... | collective-permute-start | bytes 1769480 | tf_op jit(solution)/shard_map/ppermute | solution.py:137
  102.6 23.8 %collective-permute-start.11 = (bf16[256,1152]{1,0:T(8,128)(2,1)S(1)}, bf16[256,1152]{1,0:T(8,128)(2,1)S(1)}, u32[]{:S(2)}, u32[]{:S(2)}) collective-permute-start(bf16[256,1152]{1,0:T(8,128)(2,1)S(1)} %shard_map.76), channel_id=1, source_target_pairs={{0,24},{8,0},{16,8},{24,16},{1,25},{9,1},{17,9},{25,17},{2,26},{10... | collective-permute-start | bytes 1769480 | tf_op jit(solution)/shard_map/ppermute | solution.py:137
  126.9 9.3 %collective-permute-start.12 = (bf16[64,1152]{1,0:T(8,128)(2,1)S(1)}, bf16[64,1152]{1,0:T(8,128)(2,1)S(1)}, u32[]{:S(2)}, u32[]{:S(2)}) collective-permute-start(bf16[64,1152]{1,0:T(8,128)(2,1)S(1)} %get-tuple-element.27), channel_id=1, source_target_pairs={{0,32},{32,64},{64,96},{96,128},{128,160},{160,192},{192,224},{224... | collective-permute-start | bytes 442376 | tf_op jit(solution)/shard_map/ppermute | solution.py:137
  129.9 9.1 %collective-permute-start.13 = (bf16[64,1152]{1,0:T(8,128)(2,1)S(1)}, bf16[64,1152]{1,0:T(8,128)(2,1)S(1)}, u32[]{:S(2)}, u32[]{:S(2)}) collective-permute-start(bf16[64,1152]{1,0:T(8,128)(2,1)S(1)} %get-tuple-element.28), channel_id=1, source_target_pairs={{0,64},{32,96},{64,128},{96,160},{128,192},{160,224},{192,256},{22... | collective-permute-start | bytes 442376 | tf_op jit(solution)/shard_map/ppermute | solution.py:137
  133.3 6.2 %collective-permute-start.14 = (bf16[64,1152]{1,0:T(8,128)(2,1)S(1)}, bf16[64,1152]{1,0:T(8,128)(2,1)S(1)}, u32[]{:S(2)}, u32[]{:S(2)}) collective-permute-start(bf16[64,1152]{1,0:T(8,128)(2,1)S(1)} %get-tuple-element.29), channel_id=1, source_target_pairs={{0,480},{32,0},{64,32},{96,64},{128,96},{160,128},{192,160},{224,1... | collective-permute-start | bytes 442376 | tf_op jit(solution)/shard_map/ppermute | solution.py:137
  139.6 16.4 %collective-permute-start.15 = (bf16[16,1152]{1,0:T(8,128)(2,1)S(1)}, bf16[16,1152]{1,0:T(8,128)(2,1)S(1)}, u32[]{:S(2)}, u32[]{:S(2)}) collective-permute-start(bf16[16,1152]{1,0:T(8,128)(2,1)S(1)} %get-tuple-element.31), channel_id=1, source_target_pairs={{0,128},{32,160},{64,192},{96,224},{128,256},{160,288},{192,320},{... | collective-permute-start | bytes 110600 | tf_op jit(solution)/shard_map/ppermute | solution.py:137
  146.6 14.2 %collective-permute-start.16 = (bf16[16,1152]{1,0:T(8,128)(2,1)S(1)}, bf16[16,1152]{1,0:T(8,128)(2,1)S(1)}, u32[]{:S(2)}, u32[]{:S(2)}) collective-permute-start(bf16[16,1152]{1,0:T(8,128)(2,1)S(1)} %get-tuple-element.32), channel_id=1, source_target_pairs={{0,256},{32,288},{64,320},{96,352},{128,384},{160,416},{192,448},{... | collective-permute-start | bytes 110600 | tf_op jit(solution)/shard_map/ppermute | solution.py:137
  150.5 10.3 %collective-permute-start.17 = (bf16[16,1152]{1,0:T(8,128)(2,1)S(1)}, bf16[16,1152]{1,0:T(8,128)(2,1)S(1)}, u32[]{:S(2)}, u32[]{:S(2)}) collective-permute-start(bf16[16,1152]{1,0:T(8,128)(2,1)S(1)} %get-tuple-element.33), channel_id=1, source_target_pairs={{0,384},{32,416},{64,448},{96,480},{128,0},{160,32},{192,64},{224,... | collective-permute-start | bytes 110600 | tf_op jit(solution)/shard_map/ppermute | solution.py:137

commit v2 on v1

v2 whole, which is shorter than its diff:
```python
import jax
import jax.numpy as jnp
from jax import lax
from jax.experimental import pallas as pl
from jax.experimental.pallas import tpu as pltpu
from jax.sharding import Mesh, PartitionSpec as P

temper = 0.1
prior = 0.01
gone = -3e38
f32 = jnp.float32
bf16 = jnp.bfloat16
i32 = jnp.int32
lane = 128


def vmem(n):
    return [pl.BlockSpec(memory_space=pltpu.VMEM)] * n


def params():
    return pltpu.CompilerParams(vmem_limit_bytes=40 * 1024 * 1024)


def mask_kernel(place_ref, lists_ref, owner_ref, mask_ref):
    cluster, n = place_ref[0], place_ref[1]
    ids = lists_ref[pl.ds(cluster, 1), :]
    count = ids.shape[1]
    blocks = owner_ref.shape[0]
    in_block = lax.broadcasted_iota(i32, (lane, count), 0)
    which = (lax.broadcasted_iota(i32, (blocks, count), 0) == (ids >> 7)).astype(bf16)
    here = in_block == (ids & 127)
    rows = owner_ref[...]

    def pick(table):
        found = lax.dot_general(
            table.astype(f32).astype(bf16),
            which,
            (((0,), (0,)), ((), ())),
            preferred_element_type=f32,
        )
        return jnp.sum(jnp.where(here, found, 0.0), axis=0, keepdims=True).astype(i32)

    owner = pick(rows >> 7)
    inner = pick(rows & 127)
    row = (owner & 3) * 256 + (owner >> 2) * 16 + (inner & 15)
    block = jnp.where((inner >> 4) == n, row >> 7, lane)
    left = (in_block == (row & 127)).astype(bf16)
    right = (in_block == block).astype(bf16)
    mask_ref[...] = lax.dot_general(
        left, right, (((1,), (1,)), ((), ())), preferred_element_type=f32
    )


def turn_kernel(points_ref, turned_ref):
    step = 256
    for c in range(points_ref.shape[0] // step):
        at = slice(c * step, (c + 1) * step)
        turned_ref[:, at] = points_ref[at, :].T


def score_kernel(means_ref, turned_ref, mask_ref, expo_ref, stat_ref):
    rows = means_ref.shape[0]
    step = 256
    biases, listed = [], []
    for p in range(rows // step):
        wide = means_ref[p * step : (p + 1) * step, :].astype(f32)
        norms = jnp.sum(wide * wide, axis=1, keepdims=True)
        first = p * (step // lane)
        mask = jnp.concatenate([mask_ref[:, first + i : first + i + 1] for i in range(step // lane)])
        listed.append(mask > 0.5)
        biases.append(norms * (-1.0 / temper))
    for c in range(turned_ref.shape[1] // step):
        at = slice(c * step, (c + 1) * step)
        tops = []
        for p in range(rows // step):
            here = slice(p * step, (p + 1) * step)
            dots = jnp.dot(means_ref[here, :], turned_ref[:, at], preferred_element_type=f32)
            t = jnp.where(listed[p], dots * (2.0 / temper) + biases[p], gone)
            expo_ref[here, at] = t
            tops.append(jnp.max(t, axis=0, keepdims=True))
        top = jnp.maximum(jnp.maximum(tops[0], tops[1]), jnp.maximum(tops[2], tops[3]))
        total = jnp.zeros_like(top)
        for p in range(rows // step):
            here = slice(p * step, (p + 1) * step)
            expo = jnp.exp(expo_ref[here, at] - top)
            expo_ref[here, at] = expo
            total = total + jnp.sum(expo, axis=0, keepdims=True)
        stat_ref[0:1, at] = top
        stat_ref[1:2, at] = total


def sums_kernel(expo_ref, stat_ref, all_ref, points_ref, out_ref):
    tops = all_ref[:, 0, :]
    top = jnp.max(tops, axis=0, keepdims=True)
    total = jnp.sum(all_ref[:, 1, :] * jnp.exp(tops - top), axis=0, keepdims=True)
    scale = jnp.exp(stat_ref[0:1, :] - top) / total
    width = points_ref.shape[1]
    step = 256
    for p in range(expo_ref.shape[0] // step):
        here = slice(p * step, (p + 1) * step)
        resp = (expo_ref[here, :] * scale).astype(bf16)
        for c in range(width // step):
            at = slice(c * step, (c + 1) * step)
            out_ref[here, at] = jnp.dot(
                resp, points_ref[:, at], preferred_element_type=f32
            ).astype(bf16)
        mass = jnp.sum(resp.astype(f32), axis=1, keepdims=True)
        lanes = lax.broadcasted_iota(i32, (step, lane), 1)
        out_ref[here, width:] = jnp.where(lanes == 0, mass, 0.0).astype(bf16)


def added(ref, width):
    total = ref[0].astype(f32)
    for k in range(1, ref.shape[0]):
        total = total + ref[k].astype(f32)
    return total[:, :width], total[:, width : width + 1] + total[:, width + 1 : width + 2]


def halves(mass):
    high = mass.astype(bf16).astype(f32)
    lanes = lax.broadcasted_iota(i32, (mass.shape[0], lane), 1)
    return jnp.where(lanes == 0, high, jnp.where(lanes == 1, mass - high, 0.0)).astype(bf16)


def add_kernel(ref, out):
    width = ref.shape[2] - lane
    total, mass = added(ref, width)
    out[:, :width] = total.astype(bf16)
    out[:, width:] = halves(mass)


def last_kernel(ref, cen, out):
    width = cen.shape[1]
    total, mass = added(ref, width)
    new = (total + prior * cen[...].astype(f32)) / (mass + prior)
    new = new.astype(bf16)
    tail = halves(mass)
    for k in range(out.shape[0]):
        out[k, :, :width] = new
        out[k, :, width:] = tail


def call(kernel, outs, args, specs=None, flops=0, moved=0):
    return pl.pallas_call(
        kernel,
        out_shape=outs,
        in_specs=specs or vmem(len(args)),
        out_specs=jax.tree.map(lambda _: pl.BlockSpec(memory_space=pltpu.VMEM), outs),
        compiler_params=params(),
        cost_estimate=pl.CostEstimate(flops=flops, bytes_accessed=moved, transcendentals=0),
    )(*args)


def shards(points, coarse_ids, lists, owner_map, centroids):
    narrow = ("y", "c")
    parts = lax.axis_size(narrow)
    zs, xs = lax.axis_size("z"), lax.axis_size("x")
    n = lax.axis_index(narrow)
    count, width = points.shape
    rows = centroids.shape[0] // parts
    size = rows * zs
    padded = width + lane
    sds = jax.ShapeDtypeStruct

    own = lax.dynamic_slice(centroids, (n * rows, 0), (rows, width))
    column = lax.all_gather(own, "z", axis=0, tiled=True)
    copies = jnp.broadcast_to(column, (xs, size, width))
    means = lax.all_to_all(copies, "x", 0, 0, tiled=True).reshape(xs * size, width)

    place = jnp.stack([coarse_ids[0], n]).astype(i32)
    mask = call(
        mask_kernel,
        sds((lane, lane), f32),
        (place, lists, owner_map.reshape(-1, lane)),
        [pl.BlockSpec(memory_space=pltpu.SMEM)] + vmem(2),
        moved=4 << 20,
    )
    turned = call(turn_kernel, sds((width, count), bf16), (points,), moved=8 << 20)
    flops = 2 * xs * size * count * width
    expo, stat = call(
        score_kernel,
        (sds((xs * size, count), f32), sds((2, count), f32)),
        (means, turned, mask),
        flops=flops,
        moved=16 << 20,
    )
    shared = lax.all_to_all(jnp.broadcast_to(stat, (parts, 2, count)), narrow, 0, 0, tiled=True)
    sums = call(
        sums_kernel,
        sds((xs * size, padded), bf16),
        (expo, stat, shared, points),
        flops=flops,
        moved=16 << 20,
    )
    got = lax.all_to_all(sums.reshape(xs, size, padded), "x", 0, 0, tiled=True)
    sums = call(add_kernel, sds((size, padded), bf16), (got,))
    got = lax.all_to_all(sums.reshape(zs, rows, padded), "z", 0, 0, tiled=True)
    table = call(last_kernel, sds((parts, rows, padded), bf16), (got, own))
    whole = lax.all_to_all(table, narrow, 0, 0, tiled=True).reshape(parts * rows, padded).astype(f32)
    return whole[:, :width], whole[:, width] + whole[:, width + 1]


def solution(mesh):
    chips = Mesh(mesh.devices.reshape(16, 4, 4, 2), ("z", "x", "y", "c"))
    wide = ("z", "x")
    return jax.shard_map(
        shards,
        mesh=chips,
        in_specs=(P(wide, None), P(wide), P(), P(), P(wide, None)),
        out_specs=(P(wide, None), P(wide)),
        check_vma=False,
    )
```

time: 181 us -> 175 us (0.967)
  blocking collectives: 27.1 us -> 134 us
  starting transfers between devices: 80.3 us -> 4.7 us
  waiting for transfers between devices: 47.4 us -> 13.1 us
  Pallas kernels: 17.4 us -> 13.6 us
    all_to_all x1 -> x4, blocking collectives: 9.74 us -> 102 us  [the longest x1 39.1 us: shards(): got = lax.all_to_all(sums.reshape(zs, rows, padded), 'z', 0, 0, tiled=True)]
    ppermute x18 -> x0, starting transfers between devices: 80.3 us -> none  [shifted(): return lax.ppermute(a, axis, [(i, (i + by) % n) for i in range(n)])]
    ppermute x18 -> x0, waiting for transfers between devices: 47.4 us -> none  [shifted(): return lax.ppermute(a, axis, [(i, (i + by) % n) for i in range(n)])]
    all_gather x1, blocking collectives: 17.4 us -> 31.8 us  [shards(): column = lax.all_gather(own, 'z', axis=0, tiled=True)]
    all_to_all x0 -> x1, waiting for transfers between devices: none -> 13.1 us  [shards(): lax.all_to_all(copies, 'x', 0, 0, tiled=True).reshape(xs * size, width)]
    all_to_all x0 -> x1, starting transfers between devices: none -> 4.7 us  [shards(): lax.all_to_all(copies, 'x', 0, 0, tiled=True).reshape(xs * size, width)]
    pallas_call x12 -> x6, Pallas kernels: 17.4 us -> 13.6 us  [call(): pl.pallas_call(kernel, out_shape=outs, in_specs=specs or vmem(len(args)),...]
    unnamed x14 -> x12, local copies, waits for them, and re-layouts: 4.36 us -> 4.49 us
  transfers between devices with their start and end apart: 18 -> 1, of which waited for: 9 -> 1; matrix products, arithmetic and copies ran while one was open for 0% -> 0% of each run, Pallas kernels for 7% -> 1%
where the time goes in v2:
time: 175 us; the launch traced here: 174 us
  blocking collectives  134 us (77%)
  Pallas kernels  13.6 us (8%)
  waiting for transfers between devices  13.1 us (7%)
  local copies, waits for them, and re-layouts  7.01 us (4%)
  starting transfers between devices  4.7 us (3%)
    all_to_all x1, blocking collectives, shards(): got = lax.all_to_all(sums.reshape(zs, rows, padded), 'z', 0, 0, tiled=True)  39.1 us
    all_gather x1, blocking collectives, shards(): column = lax.all_gather(own, 'z', axis=0, tiled=True)  31.8 us
    all_to_all x1, blocking collectives, shards(): got = lax.all_to_all(sums.reshape(xs, size, padded), 'x', 0, 0, tiled=True)  30.7 us
    all_to_all x1, blocking collectives, shards(): lax.all_to_all(jnp.broadcast_to(stat, (parts, 2, count)), narrow, 0, 0, t...  18.7 us
    pallas_call x6, Pallas kernels, call(): pl.pallas_call(kernel, out_shape=outs, in_specs=specs or vmem(len(args)),...  13.6 us
    all_to_all x1, blocking collectives, shards(): lax.all_to_all(table, narrow, 0, 0, tiled=True)  13.4 us
    all_to_all x1, waiting for transfers between devices, shards(): lax.all_to_all(copies, 'x', 0, 0, tiled=True).reshape(xs * size, width)  13.1 us
    all_to_all x1, starting transfers between devices, shards(): lax.all_to_all(copies, 'x', 0, 0, tiled=True).reshape(xs * size, width)  4.7 us
  transfers between devices with their start and end apart: 1, of which 1 were waited for; matrix products, arithmetic and copies ran while one was open for 0% of the time, Pallas kernels for 1%

profile of v2, /device:TPU:1, one launch (start us, length us, event | category | flops | bytes accessed | tf_op | source)
XLA Modules:
  0.0 174.3 jit_solution(3727887031113970798)
XLA Ops:
  0.6 0.0 copy-start
  0.7 0.9 copy-done
  1.6 31.8 %all_gather.3 = bf16[256,1024]{1,0:T(8,128)(2,1)S(1)} all-gather(bf16[16,1024]{1,0:T(8,128)(2,1)S(1)} %constant_dynamic-slice_fusion.cen), channel_id=1, replica_groups=mesh['z'=16,'x'=4,'y'=4,'c'=2] {'z'}, dimensions={0}, use_global_device_ids=true | all-gather | bytes 557056 | tf_op jit(solution)/shard_map/all_gather | solution.py:167
  33.4 1.6 broadcast_in_dim.6
  35.0 0.0 copy-start.1
  35.0 4.7 %all-to-all-start = ((bf16[4,256,1024]{2,1,0:T(8,128)(2,1)}), bf16[4,256,1024]{2,1,0:T(8,128)(2,1)}, u32[]{:S(2)}, u32[]{:S(2)}) async-start(bf16[4,256,1024]{2,1,0:T(8,128)(2,1)} %broadcast_in_dim.6), calls=%async_computation | async-start | bytes 4194304 | tf_op jit(solution)/shard_map/all_to_all | solution.py:169
  40.4 0.0 copy-done.1
  40.4 0.0 copy-start.4
  40.4 0.0 copy-start.5
  40.4 0.9 shard_map.68.turned_ref
  41.3 0.0 copy-start.2
  41.3 1.6 copy-done.2
  42.9 0.1 pad_add_fusion.place_ref
  43.0 0.0 copy-done.4
  43.0 0.0 copy-done.5
  43.0 1.5 shard_map.69.mask_ref
  44.5 13.1 %all-to-all-done = bf16[4,256,1024]{2,1,0:T(8,128)(2,1)} async-done(((bf16[4,256,1024]{2,1,0:T(8,128)(2,1)}), bf16[4,256,1024]{2,1,0:T(8,128)(2,1)}, u32[]{:S(2)}, u32[]{:S(2)}) %all-to-all-start) | async-done | bytes 2097184 | tf_op jit(solution)/shard_map/all_to_all | solution.py:169
  57.6 0.0 copy-start.3
  57.6 1.9 %copy-done.3 = bf16[1024,1536]{1,0:T(8,128)(2,1)S(1)} copy-done((bf16[1024,1536]{1,0:T(8,128)(2,1)S(1)}, bf16[1024,1536]{1,0:T(8,128)(2,1)}, u32[]{:S(2)}) %copy-start.3) | copy-done | bytes 3145752
  59.5 6.8 %shard_map.70 = (f32[1024,1536]{1,0:T(8,128)S(1)}, f32[2,1536]{1,0:T(2,128)S(1)}) custom-call(bf16[1024,1024]{1,0:T(8,128)(2,1)} %bitcast.means_ref, bf16[1024,1536]{1,0:T(8,128)(2,1)S(1)} %copy-done.3, f32[128,128]{1,0:T(8,128)S(1)} %shard_map.69.mask_ref), custom_call_target="tpu_custom_call" | custom-call | flops 3221225472 | bytes 16777216 | tf_op jit(solution)/shard_map/pallas_call | solution.py:145
  66.4 18.7 %all_to_all.25.all_ref = f32[8,2,1536]{2,1,0:T(2,128)S(1)} all-to-all(f32[8,2,1536]{2,1,0:T(2,128)S(1)} %broadcast_in_dim.7), channel_id=1, replica_groups=mesh['z'=16,'x'=4,'y'=4,'c'=2] {'y','c'}, dimensions={0} | all-to-all | bytes 196608 | tf_op jit(solution)/shard_map/all_to_all | solution.py:188
  85.1 3.6 %shard_map.71 = bf16[1024,1152]{1,0:T(8,128)(2,1)S(1)} custom-call(f32[1024,1536]{1,0:T(8,128)S(1)} %get-tuple-element.4.expo_ref, f32[2,1536]{1,0:T(2,128)S(1)} %get-tuple-element.5.stat_ref, f32[8,2,1536]{2,1,0:T(2,128)S(1)} %all_to_all.25.all_ref, bf16[1536,1024]{1,0:T(8,128)(2,1)S(1)} %copy-done.1), custom_call_target="tpu_custom_call" | custom-call | flops 3221225472 | bytes 16777216 | tf_op jit(solution)/shard_map/pallas_call | solution.py:145
  88.7 30.7 %all_to_all.26.ref = bf16[4,256,1152]{2,1,0:T(8,128)(2,1)S(1)} all-to-all(bf16[4,256,1152]{2,1,0:T(8,128)(2,1)S(1)} %bitcast.8), channel_id=1, replica_groups=mesh['z'=16,'x'=4,'y'=4,'c'=2] {'x'}, dimensions={0} | all-to-all | bytes 4718592 | tf_op jit(solution)/shard_map/all_to_all | solution.py:196
  119.4 0.6 shard_map.72
  120.0 39.1 %all_to_all.27.ref = bf16[16,16,1152]{2,1,0:T(8,128)(2,1)S(1)} all-to-all(bf16[16,16,1152]{2,1,0:T(8,128)(2,1)S(1)} %bitcast.9), channel_id=1, replica_groups=mesh['z'=16,'x'=4,'y'=4,'c'=2] {'z'}, dimensions={0} | all-to-all | bytes 1179648 | tf_op jit(solution)/shard_map/all_to_all | solution.py:198
  159.1 0.2 shard_map.73
  159.3 13.4 %all_to_all.28 = bf16[8,16,1152]{2,1,0:T(8,128)(2,1)S(1)} all-to-all(bf16[8,16,1152]{2,1,0:T(8,128)(2,1)S(1)} %shard_map.73), channel_id=1, replica_groups=mesh['z'=16,'x'=4,'y'=4,'c'=2] {'y','c'}, dimensions={0} | all-to-all | bytes 589824 | tf_op jit(solution)/shard_map/all_to_all | solution.py:200
  172.7 0.1 bitcast_convert_fusion
  172.8 0.7 fusion
  173.5 0.8 slice.12
  (2 shorter events, 0.0 us)
Async XLA Ops:
  0.6 1.0 copy-start
  35.0 5.4 %copy-start.1 = (bf16[1536,1024]{1,0:T(8,128)(2,1)S(1)}, bf16[1536,1024]{1,0:T(8,128)(2,1)}, u32[]{:S(2)}) copy-start(bf16[1536,1024]{1,0:T(8,128)(2,1)} %points_ref.3) | copy-start | bytes 9437188
  35.0 22.6 %all-to-all-start = ((bf16[4,256,1024]{2,1,0:T(8,128)(2,1)}), bf16[4,256,1024]{2,1,0:T(8,128)(2,1)}, u32[]{:S(2)}, u32[]{:S(2)}) async-start(bf16[4,256,1024]{2,1,0:T(8,128)(2,1)} %broadcast_in_dim.6), calls=%async_computation | async-start | bytes 4194304 | tf_op jit(solution)/shard_map/all_to_all | solution.py:169
  40.4 2.6 %copy-start.4 = (s32[16,2048]{1,0:T(8,128)S(1)}, s32[16,2048]{1,0:T(8,128)}, u32[]{:S(2)}) copy-start(s32[16,2048]{1,0:T(8,128)} %lists_ref.1) | copy-start | bytes 393220
  40.4 2.6 %copy-start.5 = (s32[8192]{0:T(1024)S(1)}, s32[8192]{0:T(1024)}, u32[]{:S(2)}) copy-start(s32[8192]{0:T(1024)} %param.8) | copy-start | bytes 98308
  41.3 1.7 copy-start.2
  57.6 1.9 %copy-start.3 = (bf16[1024,1536]{1,0:T(8,128)(2,1)S(1)}, bf16[1024,1536]{1,0:T(8,128)(2,1)}, u32[]{:S(2)}) copy-start(bf16[1024,1536]{1,0:T(8,128)(2,1)} %copy-done.2) | copy-start | bytes 9437188

commit v3 on v2

v3 whole, which is shorter than its diff:
```python
import functools

import jax
import jax.numpy as jnp
from jax import lax
from jax.experimental import pallas as pl
from jax.experimental.pallas import tpu as pltpu
from jax.sharding import Mesh, PartitionSpec as P

temper = 0.1
prior = 0.01
gone = -3e38
f32 = jnp.float32
bf16 = jnp.bfloat16
i32 = jnp.int32
lane = 128


def vmem(n):
    return [pl.BlockSpec(memory_space=pltpu.VMEM)] * n


def params():
    return pltpu.CompilerParams(vmem_limit_bytes=20 * 1024 * 1024)


def mask_kernel(place_ref, other_ref, lists_ref, owner_ref, mask_ref):
    n, x = place_ref[1], place_ref[2]
    count = lists_ref.shape[1]
    blocks = owner_ref.shape[0]
    in_block = lax.broadcasted_iota(i32, (lane, count), 0)
    of_blocks = lax.broadcasted_iota(i32, (blocks, count), 0)
    rows = owner_ref[...]
    tables = [(rows >> 7).astype(f32).astype(bf16), (rows & 127).astype(f32).astype(bf16)]
    mask = jnp.zeros(mask_ref.shape, f32)
    for slab, cluster in enumerate((place_ref[0], other_ref[0])):
        ids = lists_ref[pl.ds(cluster, 1), :]
        which = (of_blocks == (ids >> 7)).astype(bf16)
        here = in_block == (ids & 127)
        owner, inner = (
            jnp.sum(
                jnp.where(
                    here,
                    lax.dot_general(
                        table, which, (((0,), (0,)), ((), ())), preferred_element_type=f32
                    ),
                    0.0,
                ),
                axis=0,
                keepdims=True,
            ).astype(i32)
            for table in tables
        )
        column = owner & 3
        row = (owner >> 2) * 16 + (inner & 15)
        block = (row >> 7) + jnp.where(column == x, 0, 2) + 4 * slab
        mine = ((inner >> 4) == n) & ((column == x) | (column == 3 - x))
        left = (in_block == (row & 127)).astype(bf16)
        right = (in_block == jnp.where(mine, block, lane)).astype(bf16)
        mask = mask + lax.dot_general(
            left, right, (((1,), (1,)), ((), ())), preferred_element_type=f32
        )
    mask_ref[...] = mask


def turn_kernel(*refs):
    turned_ref = refs[-1]
    step = 256
    base = 0
    for points_ref in refs[:-1]:
        for c in range(points_ref.shape[0] // step):
            at = slice(c * step, (c + 1) * step)
            turned_ref[:, base : base + step] = points_ref[at, :].T
            base += step


def squares(means_ref):
    wide = means_ref[...].astype(f32)
    return jnp.sum(wide * wide, axis=1, keepdims=True) * (-1.0 / temper)


def listed_rows(mask_ref, first, rows):
    picked = [mask_ref[:, first + i : first + i + 1] for i in range(rows // lane)]
    return jnp.concatenate(picked) > 0.5


def scored(means_ref, turned_ref, bias, listed, at):
    dots = jnp.dot(means_ref[...], turned_ref[:, at], preferred_element_type=f32)
    t = jnp.where(listed, dots * (2.0 / temper) + bias, gone)
    top = jnp.max(t, axis=0, keepdims=True)
    expo = jnp.exp(t - top)
    return expo, top, jnp.sum(expo, axis=0, keepdims=True)


def own_kernel(slab, means_ref, turned_ref, mask_ref, expo_ref, stat_ref):
    bias = squares(means_ref)
    listed = listed_rows(mask_ref, 4 * slab, means_ref.shape[0])
    step = 256
    for c in range(turned_ref.shape[1] // step):
        at = slice(c * step, (c + 1) * step)
        expo_ref[:, at], stat_ref[0:1, at], stat_ref[1:2, at] = scored(
            means_ref, turned_ref, bias, listed, at
        )


def rest_kernel(
    place_ref,
    means_ref,
    turned_a,
    turned_b,
    mask_ref,
    stat_a,
    stat_b,
    expo_a,
    expo_b,
    stat_c,
    stat_d,
    both_ref,
):
    bias = squares(means_ref)
    me, core = place_ref[3], place_ref[4]
    count = turned_a.shape[1]
    step = 256
    half = count // 2
    for slab, turned_ref, old_ref, expo_ref, stat_ref in (
        (0, turned_a, stat_a, expo_a, stat_c),
        (1, turned_b, stat_b, expo_b, stat_d),
    ):
        listed = listed_rows(mask_ref, 4 * slab + 2, means_ref.shape[0])
        for c in range(count // step):
            at = slice(c * step, (c + 1) * step)
            expo_ref[:, at], top, total = scored(means_ref, turned_ref, bias, listed, at)
            stat_ref[0:1, at] = top
            stat_ref[1:2, at] = total
            before = old_ref[0:1, at]
            join = jnp.maximum(top, before)
            total = total * jnp.exp(top - join) + old_ref[1:2, at] * jnp.exp(before - join)
            if slab == 0:
                start, which = c * step, me
            else:
                shift = half * core
                start = c * step + (shift if c * step < half else -shift)
                start, which = pl.multiple_of(start, lane), 1 - me
            both_ref[which, 0:1, pl.ds(start, step)] = join
            both_ref[which, 1:2, pl.ds(start, step)] = total


def sums_kernel(
    place_ref,
    expo_a,
    expo_b,
    stat_a,
    stat_b,
    all_ref,
    points_ref,
    first_ref,
    second_ref,
    out_ref,
    norm_ref,
):
    me, core = place_ref[3], place_ref[4]
    half = first_ref.shape[0]
    width = points_ref.shape[1]
    for slab, which in enumerate((me, 1 - me)):
        tops = all_ref[:, which, 0, :]
        top = jnp.max(tops, axis=0, keepdims=True)
        total = jnp.sum(all_ref[:, which, 1, :] * jnp.exp(tops - top), axis=0, keepdims=True)
        norm_ref[slab, 0:1, :] = top
        norm_ref[slab, 1:2, :] = total

    def shares(expo, stat, top, total):
        return (expo * (jnp.exp(stat - top) / total)).astype(bf16)

    parts = [shares(expo_a[...], stat_a[0:1, :], norm_ref[0, 0:1, :], norm_ref[0, 1:2, :])]
    for h in range(2):
        from_ = pl.ds(pl.multiple_of((core if h == 0 else 1 - core) * half, lane), half)
        at = slice(h * half, (h + 1) * half)
        parts.append(
            shares(
                expo_b[:, at], stat_b[0:1, at], norm_ref[1, 0:1, from_], norm_ref[1, 1:2, from_]
            )
        )
    step = 256
    for c in range(width // step):
        at = slice(c * step, (c + 1) * step)
        total = None
        for part, ref in zip(parts, (points_ref, first_ref, second_ref)):
            more = jnp.dot(part, ref[:, at], preferred_element_type=f32)
            total = more if total is None else total + more
        out_ref[:, at] = total.astype(bf16)
    mass = sum(jnp.sum(part.astype(f32), axis=1, keepdims=True) for part in parts)
    out_ref[:, width:] = halves(mass)


def added(pieces, width):
    total = pieces[0].astype(f32)
    for piece in pieces[1:]:
        total = total + piece.astype(f32)
    return total[:, :width], total[:, width : width + 1] + total[:, width + 1 : width + 2]


def halves(mass):
    high = mass.astype(bf16).astype(f32)
    lanes = lax.broadcasted_iota(i32, (mass.shape[0], lane), 1)
    return jnp.where(lanes == 0, high, jnp.where(lanes == 1, mass - high, 0.0)).astype(bf16)


def add_kernel(a, b, out):
    width = a.shape[1] - lane
    total, mass = added([a[...], b[...]], width)
    out[:, :width] = total.astype(bf16)
    out[:, width:] = halves(mass)


def last_kernel(ref, cen, out):
    width = cen.shape[1]
    total, mass = added([ref[k] for k in range(ref.shape[0])], width)
    new = (total + prior * cen[...].astype(f32)) / (mass + prior)
    new = new.astype(bf16)
    tail = halves(mass)
    for k in range(out.shape[0]):
        out[k, :, :width] = new
        out[k, :, width:] = tail


def call(kernel, outs, args, specs=None, flops=0, moved=0, scratch=()):
    return pl.pallas_call(
        kernel,
        out_shape=outs,
        in_specs=specs or vmem(len(args)),
        out_specs=jax.tree.map(lambda _: pl.BlockSpec(memory_space=pltpu.VMEM), outs),
        scratch_shapes=scratch,
        compiler_params=params(),
        cost_estimate=pl.CostEstimate(flops=flops, bytes_accessed=moved, transcendentals=0),
    )(*args)


def shards(points, coarse_ids, lists, owner_map, centroids):
    narrow = ("y", "c")
    across = ("xh", "xl")
    parts = lax.axis_size(narrow)
    zs = lax.axis_size("z")
    n, x = lax.axis_index(narrow), lax.axis_index(across)
    me, core = lax.axis_index("xl"), lax.axis_index("c")
    count, width = points.shape
    rows = centroids.shape[0] // parts
    size = rows * zs
    padded = width + lane
    sds = jax.ShapeDtypeStruct
    smem = [pl.BlockSpec(memory_space=pltpu.SMEM)]
    swap = [(0, 1), (1, 0)]
    outer = [(0, 3), (3, 0), (1, 2), (2, 1)]

    half = lax.dynamic_slice(points, (core * (count // 2), 0), (count // 2, width))
    first = lax.ppermute(half, "xl", swap)
    other = lax.ppermute(coarse_ids, "xl", swap)
    own = lax.dynamic_slice(centroids, (n * rows, 0), (rows, width))
    column = lax.all_gather(own, "z", axis=0, tiled=True)
    first, other, column = lax.optimization_barrier((first, other, column))
    second = lax.ppermute(first, "c", swap)
    beyond = lax.ppermute(column, across, outer)

    place = jnp.stack([coarse_ids[0], n, x, me, core]).astype(i32)
    mask = call(
        mask_kernel,
        sds((lane, lane), f32),
        (place, other, lists, owner_map.reshape(-1, lane)),
        smem * 2 + vmem(2),
        moved=8 << 20,
    )
    flops = 2 * size * count * width
    turned_a = call(turn_kernel, sds((width, count), bf16), (points,), moved=8 << 20)
    turned_b = call(turn_kernel, sds((width, count), bf16), (first, second), moved=8 << 20)
    expo = sds((size, count), f32)
    stat = sds((2, count), f32)
    (expo_a, stat_a), (expo_b, stat_b) = (
        call(
            functools.partial(own_kernel, slab),
            (expo, stat),
            (column, turned, mask),
            flops=flops,
            moved=6 << 20,
        )
        for slab, turned in enumerate((turned_a, turned_b))
    )
    expo_c, expo_d, stat_c, stat_d, both = call(
        rest_kernel,
        (expo, expo, stat, stat, sds((2, 2, count), f32)),
        (place, beyond, turned_a, turned_b, mask, stat_a, stat_b),
        smem + vmem(6),
        flops=2 * flops,
        moved=12 << 20,
    )
    pool = ("xl",) + narrow
    copies = jnp.broadcast_to(both, (2 * parts, 2, 2, count))
    shared = lax.all_to_all(copies, pool, 0, 0, tiled=True)

    def sums(expo_a, expo_b, stat_a, stat_b):
        return call(
            sums_kernel,
            sds((size, padded), bf16),
            (place, expo_a, expo_b, stat_a, stat_b, shared, points, first, second),
            smem + vmem(8),
            flops=2 * flops,
            moved=10 << 20,
            scratch=[pltpu.VMEM((2, 2, count), f32)],
        )

    away = lax.ppermute(sums(expo_c, expo_d, stat_c, stat_d), across, outer)
    kept = sums(expo_a, expo_b, stat_a, stat_b)
    added_up = call(add_kernel, sds((size, padded), bf16), (kept, away))
    got = lax.all_to_all(added_up.reshape(zs, rows, padded), "z", 0, 0, tiled=True)
    table = call(last_kernel, sds((parts, rows, padded), bf16), (got, own))
    whole = lax.all_to_all(table, narrow, 0, 0, tiled=True).reshape(parts * rows, padded).astype(f32)
    return whole[:, :width], whole[:, width] + whole[:, width + 1]


def solution(mesh):
    chips = Mesh(mesh.devices.reshape(16, 2, 2, 4, 2), ("z", "xh", "xl", "y", "c"))
    wide = ("z", "xh", "xl")
    return jax.shard_map(
        shards,
        mesh=chips,
        in_specs=(P(wide, None), P(wide), P(), P(), P(wide, None)),
        out_specs=(P(wide, None), P(wide)),
        check_vma=False,
    )
```

time: 175 us -> 169 us (0.966)
  blocking collectives: 134 us -> 101 us
  starting transfers between devices: 4.7 us -> 23 us
  Pallas kernels: 13.6 us -> 23.8 us
  waiting for transfers between devices: 13.1 us -> 10 us
    all_to_all x3 -> x2, blocking collectives: 88.5 us -> 51.1 us  [the longest x1 38.2 us: shards(): lax.all_to_all(added_up.reshape(zs, rows, padded), 'z', 0, 0, tiled=True)]
    ppermute x0 -> x5, starting transfers between devices: none -> 23 us  [the longest x1 9.95 us: shards(): second = lax.ppermute(first, 'c', swap)]
    all_to_all x1 -> x0, waiting for transfers between devices: 13.1 us -> none  [shards(): lax.all_to_all(copies, 'x', 0, 0, tiled=True).reshape(xs * size, width)]
    pallas_call x6 -> x10, Pallas kernels: 13.6 us -> 23.8 us  [call(): pl.pallas_call(kernel, out_shape=outs, in_specs=specs or vmem(len(args)),...]
    ppermute x0 -> x5, waiting for transfers between devices: none -> 10 us  [the longest x1 10 us: shards(): away = lax.ppermute(sums(expo_c, expo_d, stat_c, stat_d), across, outer)]
    all_to_all x1 -> x0, starting transfers between devices: 4.7 us -> none  [shards(): lax.all_to_all(copies, 'x', 0, 0, tiled=True).reshape(xs * size, width)]
    dynamic_slice x0 -> x1, local copies, waits for them, and re-layouts: none -> 2.85 us  [shards(): lax.dynamic_slice(points, (core * (count // 2), 0), (count // 2, width))]
    all_gather x1, blocking collectives: 31.8 us -> 34.3 us  [shards(): column = lax.all_gather(own, 'z', axis=0, tiled=True)]
  transfers between devices with their start and end apart: 1 -> 5, of which waited for: 1 -> 1; matrix products, arithmetic and copies ran while one was open for 0% -> 0% of each run, Pallas kernels for 1% -> 9%
where the time goes in v3:
time: 169 us
  blocking collectives  101 us (60%)
  Pallas kernels  23.8 us (14%)
  starting transfers between devices  23 us (14%)
  waiting for transfers between devices  10 us (6%)
  local copies, waits for them, and re-layouts  8.33 us (5%)
    all_to_all x1, blocking collectives, shards(): lax.all_to_all(added_up.reshape(zs, rows, padded), 'z', 0, 0, tiled=True)  38.2 us
    all_gather x1, blocking collectives, shards(): column = lax.all_gather(own, 'z', axis=0, tiled=True)  34.3 us
    pallas_call x10, Pallas kernels, call(): pl.pallas_call(kernel, out_shape=outs, in_specs=specs or vmem(len(args)),...  23.8 us
    all_to_all x1, blocking collectives, shards(): lax.all_to_all(table, narrow, 0, 0, tiled=True)  15.7 us
    all_to_all x1, blocking collectives, shards(): shared = lax.all_to_all(copies, pool, 0, 0, tiled=True)  13 us
    ppermute x1, waiting for transfers between devices, shards(): away = lax.ppermute(sums(expo_c, expo_d, stat_c, stat_d), across, outer)  10 us
    ppermute x1, starting transfers between devices, shards(): second = lax.ppermute(first, 'c', swap)  9.95 us
    unnamed x14, local copies, waits for them, and re-layouts  4.43 us
  transfers between devices with their start and end apart: 5, of which 1 were waited for; matrix products, arithmetic and copies ran while one was open for 0% of the time, Pallas kernels for 9%

profile of v3, /device:TPU:1, one launch (start us, length us, event | category | flops | bytes accessed | tf_op | source)
XLA Modules:
  0.0 168.6 jit_solution(6975544267864077918)
XLA Ops:
  0.6 0.0 copy-start
  0.7 0.0 copy-start.1
  0.7 2.9 %constant_dynamic-slice_fusion.1 = bf16[768,1024]{1,0:T(8,128)(2,1)} fusion(bf16[1536,1024]{1,0:T(8,128)(2,1)} %points_ref.3, s32[]{:T(128)S(6)} %select_n.6), kind=kLoop, calls=%fused_computation.4 | loop fusion | bytes 3145732 | tf_op jit(solution)/shard_map/dynamic_slice | solution.py:254
  3.5 3.9 %collective-permute-start = (bf16[768,1024]{1,0:T(8,128)(2,1)}, bf16[768,1024]{1,0:T(8,128)(2,1)}, u32[]{:S(2)}, u32[]{:S(2)}) collective-permute-start(bf16[768,1024]{1,0:T(8,128)(2,1)} %constant_dynamic-slice_fusion.1), channel_id=1, source_target_pairs={{0,8},{8,0},{1,9},{9,1},{2,10},{10,2},{3,11},{11,3},{4,12},{12,4},... | collective-permute-start | bytes 4718600 | tf_op jit(solution)/shard_map/ppermute | solution.py:255
  7.5 1.9 %collective-permute-start.1 = (s32[1]{0:T(128)}, s32[1]{0:T(128)}, u32[]{:S(2)}, u32[]{:S(2)}) collective-permute-start(s32[1]{0:T(128)} %param.6), channel_id=1, source_target_pairs={{0,8},{8,0},{1,9},{9,1},{2,10},{10,2},{3,11},{11,3},{4,12},{12,4},... | collective-permute-start | bytes 20 | tf_op jit(solution)/shard_map/ppermute | solution.py:256
  9.4 0.0 copy-done
  9.4 34.3 %all_gather.3.means_ref = bf16[256,1024]{1,0:T(8,128)(2,1)} all-gather(bf16[16,1024]{1,0:T(8,128)(2,1)S(1)} %constant_dynamic-slice_fusion.cen), channel_id=1, replica_groups=mesh['z'=16,'xh'=2,'xl'=2,'y'=4,'c'=2] {'z'}, dimensions={0}, use_global_device_ids=true | all-gather | bytes 557056 | tf_op jit(solution)/shard_map/all_gather | solution.py:258
  43.7 0.0 collective-permute-done.1.other_ref
  43.7 0.0 collective-permute-done.refs_0_.first_ref
  43.7 9.9 %collective-permute-start.2 = (bf16[768,1024]{1,0:T(8,128)(2,1)}, bf16[768,1024]{1,0:T(8,128)(2,1)}, u32[]{:S(2)}, u32[]{:S(2)}) collective-permute-start(bf16[768,1024]{1,0:T(8,128)(2,1)} %collective-permute-done.refs_0_.first_ref), channel_id=1, source_target_pairs={{0,1},{1,0},{2,3},{3,2},{4,5},{5,4},{6,7},{7,6},{8,9},{9,8},{10,11... | collective-permute-start | bytes 4718600 | tf_op jit(solution)/shard_map/ppermute | solution.py:260
  53.7 4.4 %collective-permute-start.3 = (bf16[256,1024]{1,0:T(8,128)(2,1)}, bf16[256,1024]{1,0:T(8,128)(2,1)}, u32[]{:S(2)}, u32[]{:S(2)}) collective-permute-start(bf16[256,1024]{1,0:T(8,128)(2,1)} %all_gather.3.means_ref), channel_id=1, source_target_pairs={{0,24},{24,0},{8,16},{16,8},{1,25},{25,1},{9,17},{17,9},{2,26},{26... | collective-permute-start | bytes 1572872 | tf_op jit(solution)/shard_map/ppermute | solution.py:261
  58.7 0.0 copy-done.1
  58.8 0.0 copy-start.6
  58.8 0.9 shard_map.68.turned_ref.turned_a
  59.6 0.0 copy-start.2
  59.6 1.6 copy-done.2
  61.3 0.1 stack.19.place_ref
  61.3 0.0 copy-done.6
  61.3 0.0 copy-start.5
  61.3 0.9 copy-done.5
  62.2 3.0 %shard_map.69.mask_ref = f32[128,128]{1,0:T(8,128)S(1)} custom-call(s32[5]{0:T(128)S(1)} %stack.19.place_ref, s32[1]{0:T(128)} %collective-permute-done.1.other_ref, s32[16,2048]{1,0:T(8,128)S(1)} %copy-done.5, s32[64,128]{1,0:T(8,128)S(1)} %bitcast.10), custom_call_target="tpu_custom_call" | custom-call | bytes 8388608 | tf_op jit(solution)/shard_map/pallas_call | solution.py:227
  65.2 0.0 copy-start.3
  65.2 1.9 %copy-done.3 = bf16[1024,1536]{1,0:T(8,128)(2,1)S(1)} copy-done((bf16[1024,1536]{1,0:T(8,128)(2,1)S(1)}, bf16[1024,1536]{1,0:T(8,128)(2,1)}, u32[]{:S(2)}) %copy-start.3) | copy-done | bytes 3145752
  67.1 2.5 %shard_map.70 = (f32[256,1536]{1,0:T(8,128)S(1)}, f32[2,1536]{1,0:T(2,128)S(1)}) custom-call(bf16[256,1024]{1,0:T(8,128)(2,1)} %all_gather.3.means_ref, bf16[1024,1536]{1,0:T(8,128)(2,1)S(1)} %copy-done.3, f32[128,128]{1,0:T(8,128)S(1)} %shard_map.69.mask_ref), custom_call_target="tpu_custom_call" | custom-call | flops 805306368 | bytes 6291456 | tf_op jit(solution)/shard_map/pallas_call | solution.py:227
  69.6 0.0 collective-permute-done.2.refs_1_.second_ref
  69.6 2.7 %shard_map.71.turned_ref.turned_b = bf16[1024,1536]{1,0:T(8,128)(2,1)S(1)} custom-call(bf16[768,1024]{1,0:T(8,128)(2,1)} %collective-permute-done.refs_0_.first_ref, bf16[768,1024]{1,0:T(8,128)(2,1)} %collective-permute-done.2.refs_1_.second_ref), custom_call_target="tpu_custom_call" | custom-call | bytes 8388608 | tf_op jit(solution)/shard_map/pallas_call | solution.py:227
  72.3 0.0 copy-start.4
  72.3 2.6 %shard_map.72 = (f32[256,1536]{1,0:T(8,128)S(1)}, f32[2,1536]{1,0:T(2,128)S(1)}) custom-call(bf16[256,1024]{1,0:T(8,128)(2,1)} %all_gather.3.means_ref, bf16[1024,1536]{1,0:T(8,128)(2,1)S(1)} %shard_map.71.turned_ref.turned_b, f32[128,128]{1,0:T(8,128)S(1)} %shard_map.69.mask_ref), custom_call_target="tpu_custom_call" | custom-call | flops 805306368 | bytes 6291456 | tf_op jit(solution)/shard_map/pallas_call | solution.py:227
  75.0 0.0 collective-permute-done.3.means_ref
  75.0 0.0 copy-done.4
  75.0 3.8 %shard_map.73 = (f32[256,1536]{1,0:T(8,128)S(1)}, f32[256,1536]{1,0:T(8,128)S(1)}, f32[2,1536]{1,0:T(2,128)S(1)}, f32[2,1536]{1,0:T(2,128)S(1)}, f32[2,2,1536]{2,1,0:T(2,128)S(1)}) custom-call(s32[5]{0:T(128)S(1)} %stack.19.place_ref, bf16[256,1024]{1,0:T(8,128)(2,1)} %collective-permute-done.3.means_ref, bf16[1024,1536]{1,0:T(8,128)(2,1)S(1)} %copy-done.4, ...), custom_call_target="tpu_custom_call" | custom-call | flops 1610612736 | bytes 12582912 | tf_op jit(solution)/shard_map/pallas_call | solution.py:227
  78.8 0.1 broadcast_in_dim.3
  78.9 13.0 %all_to_all.15.all_ref = f32[16,2,2,1536]{3,2,1,0:T(2,128)S(1)} all-to-all(f32[16,2,2,1536]{3,2,1,0:T(2,128)S(1)} %broadcast_in_dim.3), channel_id=1, replica_groups=mesh['z'=16,'xh'=2,'xl'=2,'y'=4,'c'=2] {'xl','y','c'}, dimensions={0} | all-to-all | bytes 786432 | tf_op jit(solution)/shard_map/all_to_all | solution.py:296
  91.9 3.9 %shard_map.75 = bf16[256,1152]{1,0:T(8,128)(2,1)S(1)} custom-call(s32[5]{0:T(128)S(1)} %stack.19.place_ref, f32[256,1536]{1,0:T(8,128)S(1)} %get-tuple-element.22.expo_a, f32[256,1536]{1,0:T(8,128)S(1)} %get-tuple-element.23.expo_b, f32[2,1536]{1,0:T(2,128)S(1)} %get-tuple-element.24.stat_a, f32[2,1536]{1,0:T(2,128)S(1)} %get-tuple-element.25.stat_b, ...), custom_call_target="tpu_custom_call" | custom-call | flops 1610612736 | bytes 10485760 | tf_op jit(solution)/shard_map/pallas_call | solution.py:227
  95.7 2.9 %collective-permute-start.4 = (bf16[256,1152]{1,0:T(8,128)(2,1)S(1)}, bf16[256,1152]{1,0:T(8,128)(2,1)S(1)}, u32[]{:S(2)}, u32[]{:S(2)}) collective-permute-start(bf16[256,1152]{1,0:T(8,128)(2,1)S(1)} %shard_map.75), channel_id=1, source_target_pairs={{0,24},{24,0},{8,16},{16,8},{1,25},{25,1},{9,17},{17,9},{2,26},{26... | collective-permute-start | bytes 1769480 | tf_op jit(solution)/shard_map/ppermute | solution.py:309
  98.6 3.9 %shard_map.74.a = bf16[256,1152]{1,0:T(8,128)(2,1)S(1)} custom-call(s32[5]{0:T(128)S(1)} %stack.19.place_ref, f32[256,1536]{1,0:T(8,128)S(1)} %get-tuple-element.16.expo_a, f32[256,1536]{1,0:T(8,128)S(1)} %get-tuple-element.18.expo_b, f32[2,1536]{1,0:T(2,128)S(1)} %get-tuple-element.19.stat_a, f32[2,1536]{1,0:T(2,128)S(1)} %get-tuple-element.20.stat_b, ...), custom_call_target="tpu_custom_call" | custom-call | flops 1610612736 | bytes 10485760 | tf_op jit(solution)/shard_map/pallas_call | solution.py:227
  102.5 10.0 %collective-permute-done.4.b = bf16[256,1152]{1,0:T(8,128)(2,1)S(1)} collective-permute-done((bf16[256,1152]{1,0:T(8,128)(2,1)S(1)}, bf16[256,1152]{1,0:T(8,128)(2,1)S(1)}, u32[]{:S(2)}, u32[]{:S(2)}) %collective-permute-start.4) | collective-permute-done | bytes 589856 | tf_op jit(solution)/shard_map/ppermute | solution.py:309
  112.5 0.4 shard_map.76
  112.9 38.2 %all_to_all.16.ref = bf16[16,16,1152]{2,1,0:T(8,128)(2,1)S(1)} all-to-all(bf16[16,16,1152]{2,1,0:T(8,128)(2,1)S(1)} %bitcast.9), channel_id=1, replica_groups=mesh['z'=16,'xh'=2,'xl'=2,'y'=4,'c'=2] {'z'}, dimensions={0} | all-to-all | bytes 1179648 | tf_op jit(solution)/shard_map/all_to_all | solution.py:312
  151.1 0.2 shard_map.77
  151.3 15.7 %all_to_all.17 = bf16[8,16,1152]{2,1,0:T(8,128)(2,1)S(1)} all-to-all(bf16[8,16,1152]{2,1,0:T(8,128)(2,1)S(1)} %shard_map.77), channel_id=1, replica_groups=mesh['z'=16,'xh'=2,'xl'=2,'y'=4,'c'=2] {'y','c'}, dimensions={0} | all-to-all | bytes 589824 | tf_op jit(solution)/shard_map/all_to_all | solution.py:314
  167.0 0.1 bitcast_convert_fusion
  167.1 0.8 slice.12
  167.9 0.7 fusion
  (1 shorter events, 0.0 us)
Async XLA Ops:
  0.6 8.8 %copy-start = (bf16[128,1024]{1,0:T(8,128)(2,1)S(1)}, bf16[128,1024]{1,0:T(8,128)(2,1)}, u32[]{:S(2)}) copy-start(bf16[128,1024]{1,0:T(8,128)(2,1)} %param.9) | copy-start | bytes 786436
  0.7 58.1 %copy-start.1 = (bf16[1536,1024]{1,0:T(8,128)(2,1)S(1)}, bf16[1536,1024]{1,0:T(8,128)(2,1)}, u32[]{:S(2)}) copy-start(bf16[1536,1024]{1,0:T(8,128)(2,1)} %points_ref.3) | copy-start | bytes 9437188
  3.5 40.2 %collective-permute-start = (bf16[768,1024]{1,0:T(8,128)(2,1)}, bf16[768,1024]{1,0:T(8,128)(2,1)}, u32[]{:S(2)}, u32[]{:S(2)}) collective-permute-start(bf16[768,1024]{1,0:T(8,128)(2,1)} %constant_dynamic-slice_fusion.1), channel_id=1, source_target_pairs={{0,8},{8,0},{1,9},{9,1},{2,10},{10,2},{3,11},{11,3},{4,12},{12,4},... | collective-permute-start | bytes 4718600 | tf_op jit(solution)/shard_map/ppermute | solution.py:255
  7.5 36.3 %collective-permute-start.1 = (s32[1]{0:T(128)}, s32[1]{0:T(128)}, u32[]{:S(2)}, u32[]{:S(2)}) collective-permute-start(s32[1]{0:T(128)} %param.6), channel_id=1, source_target_pairs={{0,8},{8,0},{1,9},{9,1},{2,10},{10,2},{3,11},{11,3},{4,12},{12,4},... | collective-permute-start | bytes 20 | tf_op jit(solution)/shard_map/ppermute | solution.py:256
  43.7 25.8 %collective-permute-start.2 = (bf16[768,1024]{1,0:T(8,128)(2,1)}, bf16[768,1024]{1,0:T(8,128)(2,1)}, u32[]{:S(2)}, u32[]{:S(2)}) collective-permute-start(bf16[768,1024]{1,0:T(8,128)(2,1)} %collective-permute-done.refs_0_.first_ref), channel_id=1, source_target_pairs={{0,1},{1,0},{2,3},{3,2},{4,5},{5,4},{6,7},{7,6},{8,9},{9,8},{10,11... | collective-permute-start | bytes 4718600 | tf_op jit(solution)/shard_map/ppermute | solution.py:260
  53.7 21.3 %collective-permute-start.3 = (bf16[256,1024]{1,0:T(8,128)(2,1)}, bf16[256,1024]{1,0:T(8,128)(2,1)}, u32[]{:S(2)}, u32[]{:S(2)}) collective-permute-start(bf16[256,1024]{1,0:T(8,128)(2,1)} %all_gather.3.means_ref), channel_id=1, source_target_pairs={{0,24},{24,0},{8,16},{16,8},{1,25},{25,1},{9,17},{17,9},{2,26},{26... | collective-permute-start | bytes 1572872 | tf_op jit(solution)/shard_map/ppermute | solution.py:261
  58.8 2.6 %copy-start.6 = (s32[8192]{0:T(1024)S(1)}, s32[8192]{0:T(1024)}, u32[]{:S(2)}) copy-start(s32[8192]{0:T(1024)} %param.8) | copy-start | bytes 98308
  59.6 1.6 copy-start.2
  61.3 0.9 copy-start.5
  65.2 1.9 %copy-start.3 = (bf16[1024,1536]{1,0:T(8,128)(2,1)S(1)}, bf16[1024,1536]{1,0:T(8,128)(2,1)}, u32[]{:S(2)}) copy-start(bf16[1024,1536]{1,0:T(8,128)(2,1)} %copy-done.2) | copy-start | bytes 9437188
  72.3 2.7 %copy-start.4 = (bf16[1024,1536]{1,0:T(8,128)(2,1)S(1)}, bf16[1024,1536]{1,0:T(8,128)(2,1)}, u32[]{:S(2)}) copy-start(bf16[1024,1536]{1,0:T(8,128)(2,1)} %copy-done.2) | copy-start | bytes 9437188
  95.7 16.8 %collective-permute-start.4 = (bf16[256,1152]{1,0:T(8,128)(2,1)S(1)}, bf16[256,1152]{1,0:T(8,128)(2,1)S(1)}, u32[]{:S(2)}, u32[]{:S(2)}) collective-permute-start(bf16[256,1152]{1,0:T(8,128)(2,1)S(1)} %shard_map.75), channel_id=1, source_target_pairs={{0,24},{24,0},{8,16},{16,8},{1,25},{25,1},{9,17},{17,9},{2,26},{26... | collective-permute-start | bytes 1769480 | tf_op jit(solution)/shard_map/ppermute | solution.py:309

commit v4 on v3

--- a/solution.py
+++ b/solution.py
@@ -26,6 +26,8 @@
 
 def mask_kernel(place_ref, other_ref, lists_ref, owner_ref, mask_ref):
     n, x = place_ref[1], place_ref[2]
+    of_lists = lax.broadcasted_iota(i32, lists_ref.shape, 0)
+    neighbour = other_ref[0:1, 0:1].astype(f32).astype(i32)
     count = lists_ref.shape[1]
     blocks = owner_ref.shape[0]
     in_block = lax.broadcasted_iota(i32, (lane, count), 0)
@@ -33,8 +35,10 @@
     rows = owner_ref[...]
     tables = [(rows >> 7).astype(f32).astype(bf16), (rows & 127).astype(f32).astype(bf16)]
     mask = jnp.zeros(mask_ref.shape, f32)
-    for slab, cluster in enumerate((place_ref[0], other_ref[0])):
-        ids = lists_ref[pl.ds(cluster, 1), :]
+    for slab, cluster in enumerate((place_ref[0], neighbour)):
+        ids = jnp.sum(
+            jnp.where(of_lists == cluster, lists_ref[...], 0), axis=0, keepdims=True
+        )
         which = (of_blocks == (ids >> 7)).astype(bf16)
         here = in_block == (ids & 127)
         owner, inner = (
@@ -63,15 +67,16 @@
     mask_ref[...] = mask
 
 
-def turn_kernel(*refs):
-    turned_ref = refs[-1]
-    step = 256
-    base = 0
-    for points_ref in refs[:-1]:
-        for c in range(points_ref.shape[0] // step):
-            at = slice(c * step, (c + 1) * step)
-            turned_ref[:, base : base + step] = points_ref[at, :].T
-            base += step
+def cut_kernel(place_ref, points_ref, half_ref, id_ref, sem, id_sem):
+    rows = points_ref.shape[0] // 2
+    start = pl.multiple_of(place_ref[4] * rows, rows)
+    copy = pltpu.make_async_copy(points_ref.at[pl.ds(start, rows)], half_ref.at[pl.ds(0, rows)], sem)
+    copy.start()
+    id_ref[...] = jnp.full(id_ref.shape, place_ref[0].astype(f32), f32).astype(bf16)
+    last = pltpu.make_async_copy(id_ref, half_ref.at[pl.ds(rows, 16)], id_sem)
+    last.start()
+    last.wait()
+    copy.wait()
 
 
 def squares(means_ref):
@@ -84,30 +89,42 @@
     return jnp.concatenate(picked) > 0.5
 
 
-def scored(means_ref, turned_ref, bias, listed, at):
-    dots = jnp.dot(means_ref[...], turned_ref[:, at], preferred_element_type=f32)
+def scored(means_ref, points, bias, listed):
+    dots = lax.dot_general(
+        means_ref[...], points, (((1,), (1,)), ((), ())), preferred_element_type=f32
+    )
     t = jnp.where(listed, dots * (2.0 / temper) + bias, gone)
     top = jnp.max(t, axis=0, keepdims=True)
     expo = jnp.exp(t - top)
     return expo, top, jnp.sum(expo, axis=0, keepdims=True)
 
 
-def own_kernel(slab, means_ref, turned_ref, mask_ref, expo_ref, stat_ref):
+def blocks_of(count, *refs):
+    step = 256
+    rows = count // len(refs)
+    for c in range(count // step):
+        start = c * step
+        ref = refs[start // rows]
+        start %= rows
+        yield slice(c * step, (c + 1) * step), ref, slice(start, start + step)
+
+
+def own_kernel(slab, means_ref, mask_ref, *refs):
+    *points, expo_ref, stat_ref = refs
     bias = squares(means_ref)
     listed = listed_rows(mask_ref, 4 * slab, means_ref.shape[0])
-    step = 256
-    for c in range(turned_ref.shape[1] // step):
-        at = slice(c * step, (c + 1) * step)
+    for at, ref, rows in blocks_of(expo_ref.shape[1], *points):
         expo_ref[:, at], stat_ref[0:1, at], stat_ref[1:2, at] = scored(
-            means_ref, turned_ref, bias, listed, at
+            means_ref, ref[rows, :], bias, listed
         )
 
 
 def rest_kernel(
     place_ref,
     means_ref,
-    turned_a,
-    turned_b,
+    points_ref,
+    first_ref,
+    second_ref,
     mask_ref,
     stat_a,
     stat_b,
@@ -119,30 +136,28 @@
 ):
     bias = squares(means_ref)
     me, core = place_ref[3], place_ref[4]
-    count = turned_a.shape[1]
-    step = 256
+    count = points_ref.shape[0]
     half = count // 2
-    for slab, turned_ref, old_ref, expo_ref, stat_ref in (
-        (0, turned_a, stat_a, expo_a, stat_c),
-        (1, turned_b, stat_b, expo_b, stat_d),
+    for slab, points, old_ref, expo_ref, stat_ref in (
+        (0, (points_ref,), stat_a, expo_a, stat_c),
+        (1, (first_ref, second_ref), stat_b, expo_b, stat_d),
     ):
         listed = listed_rows(mask_ref, 4 * slab + 2, means_ref.shape[0])
-        for c in range(count // step):
-            at = slice(c * step, (c + 1) * step)
-            expo_ref[:, at], top, total = scored(means_ref, turned_ref, bias, listed, at)
+        for at, ref, rows in blocks_of(count, *points):
+            expo_ref[:, at], top, total = scored(means_ref, ref[rows, :], bias, listed)
             stat_ref[0:1, at] = top
             stat_ref[1:2, at] = total
             before = old_ref[0:1, at]
             join = jnp.maximum(top, before)
             total = total * jnp.exp(top - join) + old_ref[1:2, at] * jnp.exp(before - join)
             if slab == 0:
-                start, which = c * step, me
+                start, which = at.start, me
             else:
                 shift = half * core
-                start = c * step + (shift if c * step < half else -shift)
+                start = at.start + (shift if at.start < half else -shift)
                 start, which = pl.multiple_of(start, lane), 1 - me
-            both_ref[which, 0:1, pl.ds(start, step)] = join
-            both_ref[which, 1:2, pl.ds(start, step)] = total
+            both_ref[which, 0:1, pl.ds(start, 256)] = join
+            both_ref[which, 1:2, pl.ds(start, 256)] = total
 
 
 def sums_kernel(
@@ -159,7 +174,7 @@
     norm_ref,
 ):
     me, core = place_ref[3], place_ref[4]
-    half = first_ref.shape[0]
+    half = points_ref.shape[0] // 2
     width = points_ref.shape[1]
     for slab, which in enumerate((me, 1 - me)):
         tops = all_ref[:, which, 0, :]
@@ -185,7 +200,7 @@
         at = slice(c * step, (c + 1) * step)
         total = None
         for part, ref in zip(parts, (points_ref, first_ref, second_ref)):
-            more = jnp.dot(part, ref[:, at], preferred_element_type=f32)
+            more = jnp.dot(part, ref[: part.shape[1], at], preferred_element_type=f32)
             total = more if total is None else total + more
         out_ref[:, at] = total.astype(bf16)
     mass = sum(jnp.sum(part.astype(f32), axis=1, keepdims=True) for part in parts)
@@ -223,12 +238,23 @@
         out[k, :, width:] = tail
 
 
-def call(kernel, outs, args, specs=None, flops=0, moved=0, scratch=()):
+def out_kernel(ref, table_ref, mass_ref):
+    parts, rows, padded = ref.shape
+    width = padded - lane
+    tails = []
+    for k in range(parts):
+        table_ref[k * rows : (k + 1) * rows, :] = ref[k, :, :width].astype(f32)
+        tails.append(ref[k, :, width:].astype(f32))
+    tail = jnp.concatenate(tails).T
+    mass_ref[...] = tail[0:1, :] + tail[1:2, :]
+
+
+def call(kernel, outs, args, specs=None, flops=0, moved=0, scratch=(), home=pltpu.VMEM):
     return pl.pallas_call(
         kernel,
         out_shape=outs,
         in_specs=specs or vmem(len(args)),
-        out_specs=jax.tree.map(lambda _: pl.BlockSpec(memory_space=pltpu.VMEM), outs),
+        out_specs=jax.tree.map(lambda _: pl.BlockSpec(memory_space=home), outs),
         scratch_shapes=scratch,
         compiler_params=params(),
         cost_estimate=pl.CostEstimate(flops=flops, bytes_accessed=moved, transcendentals=0),
@@ -251,43 +277,52 @@
     swap = [(0, 1), (1, 0)]
     outer = [(0, 3), (3, 0), (1, 2), (2, 1)]
 
-    half = lax.dynamic_slice(points, (core * (count // 2), 0), (count // 2, width))
+    place = jnp.stack([coarse_ids[0], n, x, me, core]).astype(i32)
+    half = call(
+        cut_kernel,
+        sds((count // 2 + 16, width), bf16),
+        (place, points),
+        smem + [pl.BlockSpec(memory_space=pltpu.HBM)],
+        moved=3 << 20,
+        scratch=[
+            pltpu.VMEM((16, width), bf16),
+            pltpu.SemaphoreType.DMA,
+            pltpu.SemaphoreType.DMA,
+        ],
+        home=pl.ANY,
+    )
     first = lax.ppermute(half, "xl", swap)
-    other = lax.ppermute(coarse_ids, "xl", swap)
     own = lax.dynamic_slice(centroids, (n * rows, 0), (rows, width))
     column = lax.all_gather(own, "z", axis=0, tiled=True)
-    first, other, column = lax.optimization_barrier((first, other, column))
+    first, column = lax.optimization_barrier((first, column))
+    beyond = lax.ppermute(column, across, outer)
     second = lax.ppermute(first, "c", swap)
-    beyond = lax.ppermute(column, across, outer)
-
-    place = jnp.stack([coarse_ids[0], n, x, me, core]).astype(i32)
+
     mask = call(
         mask_kernel,
         sds((lane, lane), f32),
-        (place, other, lists, owner_map.reshape(-1, lane)),
-        smem * 2 + vmem(2),
+        (place, first[count // 2 :, :lane], lists, owner_map.reshape(-1, lane)),
+        smem + vmem(3),
         moved=8 << 20,
     )
     flops = 2 * size * count * width
-    turned_a = call(turn_kernel, sds((width, count), bf16), (points,), moved=8 << 20)
-    turned_b = call(turn_kernel, sds((width, count), bf16), (first, second), moved=8 << 20)
     expo = sds((size, count), f32)
     stat = sds((2, count), f32)
     (expo_a, stat_a), (expo_b, stat_b) = (
         call(
             functools.partial(own_kernel, slab),
             (expo, stat),
-            (column, turned, mask),
+            (column, mask) + slabs,
             flops=flops,
             moved=6 << 20,
         )
-        for slab, turned in enumerate((turned_a, turned_b))
+        for slab, slabs in enumerate(((points,), (first, second)))
     )
     expo_c, expo_d, stat_c, stat_d, both = call(
         rest_kernel,
         (expo, expo, stat, stat, sds((2, 2, count), f32)),
-        (place, beyond, turned_a, turned_b, mask, stat_a, stat_b),
-        smem + vmem(6),
+        (place, beyond, points, first, second, mask, stat_a, stat_b),
+        smem + vmem(7),
         flops=2 * flops,
         moved=12 << 20,
     )
@@ -311,8 +346,11 @@
     added_up = call(add_kernel, sds((size, padded), bf16), (kept, away))
     got = lax.all_to_all(added_up.reshape(zs, rows, padded), "z", 0, 0, tiled=True)
     table = call(last_kernel, sds((parts, rows, padded), bf16), (got, own))
-    whole = lax.all_to_all(table, narrow, 0, 0, tiled=True).reshape(parts * rows, padded).astype(f32)
-    return whole[:, :width], whole[:, width] + whole[:, width + 1]
+    whole = lax.all_to_all(table, narrow, 0, 0, tiled=True)
+    new_table, masses = call(
+        out_kernel, (sds((parts * rows, width), f32), sds((1, parts * rows), f32)), (whole,)
+    )
+    return new_table, masses[0]
 
 
 def solution(mesh):

time: 169 us -> 166 us (0.982)
  local copies, waits for them, and re-layouts: 8.33 us -> 3.55 us
  blocking collectives: 101 us -> 105 us
  waiting for transfers between devices: 10 us -> 13.8 us
  Pallas kernels: 23.8 us -> 20.9 us
    all_to_all x1, blocking collectives: 38.2 us -> 44.5 us  [shards(): lax.all_to_all(added_up.reshape(zs, rows, padded), 'z', 0, 0, tiled=True)]
    ppermute x1, waiting for transfers between devices: 0.01 us -> 4.75 us  [shards(): beyond = lax.ppermute(column, across, outer)]
    pallas_call x10, Pallas kernels: 23.8 us -> 20.9 us  [call(): pl.pallas_call(kernel, out_shape=outs, in_specs=specs or vmem(len(args)),...]
    dynamic_slice x1 -> x0, local copies, waits for them, and re-layouts: 2.85 us -> none  [shards(): lax.dynamic_slice(points, (core * (count // 2), 0), (count // 2, width))]
    all_gather x1, blocking collectives: 34.3 us -> 31.9 us  [shards(): column = lax.all_gather(own, 'z', axis=0, tiled=True)]
    ppermute x1 -> x0, starting transfers between devices: 1.92 us -> none  [shards(): other = lax.ppermute(coarse_ids, 'xl', swap)]
    unnamed x14 -> x10, local copies, waits for them, and re-layouts: 4.43 us -> 2.66 us
  transfers between devices with their start and end apart: 5 -> 4, of which waited for: 1 -> 2; matrix products, arithmetic and copies ran while one was open for 0% -> 0% of each run, Pallas kernels for 9% -> 6%
where the time goes in v4:
time: 166 us
  blocking collectives  105 us (63%)
  starting transfers between devices  21.4 us (13%)
  Pallas kernels  20.9 us (13%)
  waiting for transfers between devices  13.8 us (8%)
  local copies, waits for them, and re-layouts  3.55 us (2%)
    all_to_all x1, blocking collectives, shards(): lax.all_to_all(added_up.reshape(zs, rows, padded), 'z', 0, 0, tiled=True)  44.5 us
    all_gather x1, blocking collectives, shards(): column = lax.all_gather(own, 'z', axis=0, tiled=True)  31.9 us
    pallas_call x10, Pallas kernels, call(): pl.pallas_call(kernel, out_shape=outs, in_specs=specs or vmem(len(args)),...  20.9 us
    all_to_all x1, blocking collectives, shards(): whole = lax.all_to_all(table, narrow, 0, 0, tiled=True)  14.9 us
    all_to_all x1, blocking collectives, shards(): shared = lax.all_to_all(copies, pool, 0, 0, tiled=True)  13.5 us
    ppermute x1, starting transfers between devices, shards(): second = lax.ppermute(first, 'c', swap)  9.44 us
    ppermute x1, waiting for transfers between devices, shards(): away = lax.ppermute(sums(expo_c, expo_d, stat_c, stat_d), across, outer)  9.03 us
    ppermute x1, waiting for transfers between devices, shards(): beyond = lax.ppermute(column, across, outer)  4.75 us
  transfers between devices with their start and end apart: 4, of which 2 were waited for; matrix products, arithmetic and copies ran while one was open for 0% of the time, Pallas kernels for 6%

profile of v4, /device:TPU:1, one launch (start us, length us, event | category | flops | bytes accessed | tf_op | source)
XLA Modules:
  0.0 165.9 jit_solution(2164939011603407940)
XLA Ops:
  0.6 0.0 copy-start
  1.3 0.1 stack.19.place_ref
  1.4 0.0 copy-start.1
  1.4 1.9 %copy-done.1 = bf16[1536,1024]{1,0:T(8,128)(2,1)S(1)} copy-done((bf16[1536,1024]{1,0:T(8,128)(2,1)S(1)}, bf16[1536,1024]{1,0:T(8,128)(2,1)}, u32[]{:S(2)}) %copy-start.1) | copy-done | bytes 3145752
  3.3 0.0 copy-start.3
  3.3 0.0 copy-start.2
  3.3 1.7 %shard_map.68 = bf16[784,1024]{1,0:T(8,128)(2,1)} custom-call(s32[5]{0:T(128)S(1)} %stack.19.place_ref, bf16[1536,1024]{1,0:T(8,128)(2,1)S(1)} %copy-done.1), custom_call_target="tpu_custom_call" | custom-call | bytes 3145728 | tf_op jit(solution)/shard_map/pallas_call | solution.py:253
  5.1 4.0 %collective-permute-start = (bf16[784,1024]{1,0:T(8,128)(2,1)}, bf16[784,1024]{1,0:T(8,128)(2,1)}, u32[]{:S(2)}, u32[]{:S(2)}) collective-permute-start(bf16[784,1024]{1,0:T(8,128)(2,1)} %shard_map.68), channel_id=1, source_target_pairs={{0,8},{8,0},{1,9},{9,1},{2,10},{10,2},{3,11},{11,3},{4,12},{12,4},... | collective-permute-start | bytes 4816904 | tf_op jit(solution)/shard_map/ppermute | solution.py:294
  9.0 0.0 copy-done
  9.1 31.9 %all_gather.3.means_ref = bf16[256,1024]{1,0:T(8,128)(2,1)S(1)} all-gather(bf16[16,1024]{1,0:T(8,128)(2,1)S(1)} %constant_dynamic-slice_fusion.cen), channel_id=1, replica_groups=mesh['z'=16,'xh'=2,'xl'=2,'y'=4,'c'=2] {'z'}, dimensions={0}, use_global_device_ids=true | all-gather | bytes 557056 | tf_op jit(solution)/shard_map/all_gather | solution.py:296
  41.0 0.0 collective-permute-done.refs_0_.first_ref
  41.0 9.4 %collective-permute-start.1 = (bf16[784,1024]{1,0:T(8,128)(2,1)}, bf16[784,1024]{1,0:T(8,128)(2,1)S(1)}, u32[]{:S(2)}, u32[]{:S(2)}) collective-permute-start(bf16[784,1024]{1,0:T(8,128)(2,1)} %collective-permute-done.refs_0_.first_ref), channel_id=1, source_target_pairs={{0,1},{1,0},{2,3},{3,2},{4,5},{5,4},{6,7},{7,6},{8,9},{9,8},{10,11... | collective-permute-start | bytes 4816904 | tf_op jit(solution)/shard_map/ppermute | solution.py:299
  50.4 3.7 %collective-permute-start.2 = (bf16[256,1024]{1,0:T(8,128)(2,1)S(1)}, bf16[256,1024]{1,0:T(8,128)(2,1)S(1)}, u32[]{:S(2)}, u32[]{:S(2)}) collective-permute-start(bf16[256,1024]{1,0:T(8,128)(2,1)S(1)} %all_gather.3.means_ref), channel_id=1, source_target_pairs={{0,24},{24,0},{8,16},{16,8},{1,25},{25,1},{9,17},{17,9},{2,26},{26... | collective-permute-start | bytes 1572872 | tf_op jit(solution)/shard_map/ppermute | solution.py:298
  54.2 0.7 slice.3.other_ref
  54.9 0.0 copy-done.3
  54.9 0.0 copy-start.4
  54.9 0.8 copy-done.4
  55.6 2.3 %shard_map.69.mask_ref = f32[128,128]{1,0:T(8,128)S(1)} custom-call(s32[5]{0:T(128)S(1)} %stack.19.place_ref, bf16[16,128]{1,0:T(8,128)(2,1)S(1)} %slice.3.other_ref, s32[16,2048]{1,0:T(8,128)S(1)} %copy-done.3, s32[64,128]{1,0:T(8,128)S(1)} %bitcast.8), custom_call_target="tpu_custom_call" | custom-call | bytes 8388608 | tf_op jit(solution)/shard_map/pallas_call | solution.py:253
  57.9 0.0 copy-done.2
  57.9 1.5 shard_map.70
  59.4 0.0 collective-permute-done.1.refs_1_.second_ref
  59.4 2.9 %shard_map.71 = (f32[256,1536]{1,0:T(8,128)S(1)}, f32[2,1536]{1,0:T(2,128)S(1)}) custom-call(bf16[256,1024]{1,0:T(8,128)(2,1)S(1)} %all_gather.3.means_ref, f32[128,128]{1,0:T(8,128)S(1)} %shard_map.69.mask_ref, bf16[784,1024]{1,0:T(8,128)(2,1)} %collective-permute-done.refs_0_.first_ref, bf16[784,1024]{1,0:T(8,128)(2,1)S(1)} %collective-permute-done.1.refs_1_.second_ref), custom_call_target="tpu_custom_call" | custom-call | flops 805306368 | bytes 6291456 | tf_op jit(solution)/shard_map/pallas_call | solution.py:253
  62.3 4.8 %collective-permute-done.2.means_ref = bf16[256,1024]{1,0:T(8,128)(2,1)S(1)} collective-permute-done((bf16[256,1024]{1,0:T(8,128)(2,1)S(1)}, bf16[256,1024]{1,0:T(8,128)(2,1)S(1)}, u32[]{:S(2)}, u32[]{:S(2)}) %collective-permute-start.2) | collective-permute-done | bytes 524320 | tf_op jit(solution)/shard_map/ppermute | solution.py:298
  67.1 4.2 %shard_map.72 = (f32[256,1536]{1,0:T(8,128)S(1)}, f32[256,1536]{1,0:T(8,128)S(1)}, f32[2,1536]{1,0:T(2,128)S(1)}, f32[2,1536]{1,0:T(2,128)S(1)}, f32[2,2,1536]{2,1,0:T(2,128)S(1)}) custom-call(s32[5]{0:T(128)S(1)} %stack.19.place_ref, bf16[256,1024]{1,0:T(8,128)(2,1)S(1)} %collective-permute-done.2.means_ref, bf16[1536,1024]{1,0:T(8,128)(2,1)S(1)} %copy-done.2, ...), custom_call_target="tpu_custom_call" | custom-call | flops 1610612736 | bytes 12582912 | tf_op jit(solution)/shard_map/pallas_call | solution.py:253
  71.2 0.1 broadcast_in_dim.3
  71.4 13.5 %all_to_all.15.all_ref = f32[16,2,2,1536]{3,2,1,0:T(2,128)S(1)} all-to-all(f32[16,2,2,1536]{3,2,1,0:T(2,128)S(1)} %broadcast_in_dim.3), channel_id=1, replica_groups=mesh['z'=16,'xh'=2,'xl'=2,'y'=4,'c'=2] {'xl','y','c'}, dimensions={0} | all-to-all | bytes 786432 | tf_op jit(solution)/shard_map/all_to_all | solution.py:331
  84.8 3.4 %shard_map.74 = bf16[256,1152]{1,0:T(8,128)(2,1)S(1)} custom-call(s32[5]{0:T(128)S(1)} %stack.19.place_ref, f32[256,1536]{1,0:T(8,128)S(1)} %get-tuple-element.22.expo_a, f32[256,1536]{1,0:T(8,128)S(1)} %get-tuple-element.23.expo_b, f32[2,1536]{1,0:T(2,128)S(1)} %get-tuple-element.24.stat_a, f32[2,1536]{1,0:T(2,128)S(1)} %get-tuple-element.25.stat_b, ...), custom_call_target="tpu_custom_call" | custom-call | flops 1610612736 | bytes 10485760 | tf_op jit(solution)/shard_map/pallas_call | solution.py:253
  88.2 4.3 %collective-permute-start.3 = (bf16[256,1152]{1,0:T(8,128)(2,1)S(1)}, bf16[256,1152]{1,0:T(8,128)(2,1)S(1)}, u32[]{:S(2)}, u32[]{:S(2)}) collective-permute-start(bf16[256,1152]{1,0:T(8,128)(2,1)S(1)} %shard_map.74), channel_id=1, source_target_pairs={{0,24},{24,0},{8,16},{16,8},{1,25},{25,1},{9,17},{17,9},{2,26},{26... | collective-permute-start | bytes 1769480 | tf_op jit(solution)/shard_map/ppermute | solution.py:344
  92.5 3.4 %shard_map.73.a = bf16[256,1152]{1,0:T(8,128)(2,1)S(1)} custom-call(s32[5]{0:T(128)S(1)} %stack.19.place_ref, f32[256,1536]{1,0:T(8,128)S(1)} %get-tuple-element.17.expo_a, f32[256,1536]{1,0:T(8,128)S(1)} %get-tuple-element.18.expo_b, f32[2,1536]{1,0:T(2,128)S(1)} %get-tuple-element.19.stat_a, f32[2,1536]{1,0:T(2,128)S(1)} %get-tuple-element.20.stat_b, ...), custom_call_target="tpu_custom_call" | custom-call | flops 1610612736 | bytes 10485760 | tf_op jit(solution)/shard_map/pallas_call | solution.py:253
  96.0 9.0 %collective-permute-done.3.b = bf16[256,1152]{1,0:T(8,128)(2,1)S(1)} collective-permute-done((bf16[256,1152]{1,0:T(8,128)(2,1)S(1)}, bf16[256,1152]{1,0:T(8,128)(2,1)S(1)}, u32[]{:S(2)}, u32[]{:S(2)}) %collective-permute-start.3) | collective-permute-done | bytes 589856 | tf_op jit(solution)/shard_map/ppermute | solution.py:344
  105.0 0.4 shard_map.75
  105.4 44.5 %all_to_all.16.ref = bf16[16,16,1152]{2,1,0:T(8,128)(2,1)S(1)} all-to-all(bf16[16,16,1152]{2,1,0:T(8,128)(2,1)S(1)} %bitcast.7), channel_id=1, replica_groups=mesh['z'=16,'xh'=2,'xl'=2,'y'=4,'c'=2] {'z'}, dimensions={0} | all-to-all | bytes 1179648 | tf_op jit(solution)/shard_map/all_to_all | solution.py:347
  149.9 0.2 shard_map.76
  150.1 14.9 %all_to_all.17.ref = bf16[8,16,1152]{2,1,0:T(8,128)(2,1)S(1)} all-to-all(bf16[8,16,1152]{2,1,0:T(8,128)(2,1)S(1)} %shard_map.76), channel_id=1, replica_groups=mesh['z'=16,'xh'=2,'xl'=2,'y'=4,'c'=2] {'y','c'}, dimensions={0} | all-to-all | bytes 589824 | tf_op jit(solution)/shard_map/all_to_all | solution.py:349
  165.1 0.8 shard_map.77
  (1 shorter events, 0.0 us)
Async XLA Ops:
  0.6 8.4 %copy-start = (bf16[128,1024]{1,0:T(8,128)(2,1)S(1)}, bf16[128,1024]{1,0:T(8,128)(2,1)}, u32[]{:S(2)}) copy-start(bf16[128,1024]{1,0:T(8,128)(2,1)} %param.9) | copy-start | bytes 786436
  1.4 1.9 %copy-start.1 = (bf16[1536,1024]{1,0:T(8,128)(2,1)S(1)}, bf16[1536,1024]{1,0:T(8,128)(2,1)}, u32[]{:S(2)}) copy-start(bf16[1536,1024]{1,0:T(8,128)(2,1)} %points_ref.7) | copy-start | bytes 9437188
  3.3 51.5 %copy-start.3 = (s32[16,2048]{1,0:T(8,128)S(1)}, s32[16,2048]{1,0:T(8,128)}, u32[]{:S(2)}) copy-start(s32[16,2048]{1,0:T(8,128)} %lists_ref.1) | copy-start | bytes 393220
  3.3 54.6 %copy-start.2 = (bf16[1536,1024]{1,0:T(8,128)(2,1)S(1)}, bf16[1536,1024]{1,0:T(8,128)(2,1)}, u32[]{:S(2)}) copy-start(bf16[1536,1024]{1,0:T(8,128)(2,1)} %points_ref.7) | copy-start | bytes 9437188
  5.1 35.9 %collective-permute-start = (bf16[784,1024]{1,0:T(8,128)(2,1)}, bf16[784,1024]{1,0:T(8,128)(2,1)}, u32[]{:S(2)}, u32[]{:S(2)}) collective-permute-start(bf16[784,1024]{1,0:T(8,128)(2,1)} %shard_map.68), channel_id=1, source_target_pairs={{0,8},{8,0},{1,9},{9,1},{2,10},{10,2},{3,11},{11,3},{4,12},{12,4},... | collective-permute-start | bytes 4816904 | tf_op jit(solution)/shard_map/ppermute | solution.py:294
  41.0 18.4 %collective-permute-start.1 = (bf16[784,1024]{1,0:T(8,128)(2,1)}, bf16[784,1024]{1,0:T(8,128)(2,1)S(1)}, u32[]{:S(2)}, u32[]{:S(2)}) collective-permute-start(bf16[784,1024]{1,0:T(8,128)(2,1)} %collective-permute-done.refs_0_.first_ref), channel_id=1, source_target_pairs={{0,1},{1,0},{2,3},{3,2},{4,5},{5,4},{6,7},{7,6},{8,9},{9,8},{10,11... | collective-permute-start | bytes 4816904 | tf_op jit(solution)/shard_map/ppermute | solution.py:299
  50.4 16.6 %collective-permute-start.2 = (bf16[256,1024]{1,0:T(8,128)(2,1)S(1)}, bf16[256,1024]{1,0:T(8,128)(2,1)S(1)}, u32[]{:S(2)}, u32[]{:S(2)}) collective-permute-start(bf16[256,1024]{1,0:T(8,128)(2,1)S(1)} %all_gather.3.means_ref), channel_id=1, source_target_pairs={{0,24},{24,0},{8,16},{16,8},{1,25},{25,1},{9,17},{17,9},{2,26},{26... | collective-permute-start | bytes 1572872 | tf_op jit(solution)/shard_map/ppermute | solution.py:298
  54.9 0.8 copy-start.4
  88.2 16.8 %collective-permute-start.3 = (bf16[256,1152]{1,0:T(8,128)(2,1)S(1)}, bf16[256,1152]{1,0:T(8,128)(2,1)S(1)}, u32[]{:S(2)}, u32[]{:S(2)}) collective-permute-start(bf16[256,1152]{1,0:T(8,128)(2,1)S(1)} %shard_map.74), channel_id=1, source_target_pairs={{0,24},{24,0},{8,16},{16,8},{1,25},{25,1},{9,17},{17,9},{2,26},{26... | collective-permute-start | bytes 1769480 | tf_op jit(solution)/shard_map/ppermute | solution.py:344

commit v5 on v4

--- a/solution.py
+++ b/solution.py
@@ -10,6 +10,7 @@
 temper = 0.1
 prior = 0.01
 gone = -3e38
+near = (0, 1, 2, -1)
 f32 = jnp.float32
 bf16 = jnp.bfloat16
 i32 = jnp.int32
@@ -156,8 +157,7 @@
                 shift = half * core
                 start = at.start + (shift if at.start < half else -shift)
                 start, which = pl.multiple_of(start, lane), 1 - me
-            both_ref[which, 0:1, pl.ds(start, 256)] = join
-            both_ref[which, 1:2, pl.ds(start, 256)] = total
+            both_ref[pl.ds(which, 1), pl.ds(start, 256)] = join + jnp.log(total)
 
 
 def sums_kernel(
@@ -177,24 +177,19 @@
     half = points_ref.shape[0] // 2
     width = points_ref.shape[1]
     for slab, which in enumerate((me, 1 - me)):
-        tops = all_ref[:, which, 0, :]
-        top = jnp.max(tops, axis=0, keepdims=True)
-        total = jnp.sum(all_ref[:, which, 1, :] * jnp.exp(tops - top), axis=0, keepdims=True)
-        norm_ref[slab, 0:1, :] = top
-        norm_ref[slab, 1:2, :] = total
-
-    def shares(expo, stat, top, total):
-        return (expo * (jnp.exp(stat - top) / total)).astype(bf16)
-
-    parts = [shares(expo_a[...], stat_a[0:1, :], norm_ref[0, 0:1, :], norm_ref[0, 1:2, :])]
+        each = [all_ref[k, pl.ds(which, 1), :] for k in range(all_ref.shape[0])]
+        top = functools.reduce(jnp.maximum, each)
+        total = functools.reduce(jnp.add, [jnp.exp(one - top) for one in each])
+        norm_ref[slab] = top + jnp.log(total)
+
+    def shares(expo, stat, norm):
+        return (expo * jnp.exp(stat - norm)).astype(bf16)
+
+    parts = [shares(expo_a[...], stat_a[0:1, :], norm_ref[0])]
     for h in range(2):
         from_ = pl.ds(pl.multiple_of((core if h == 0 else 1 - core) * half, lane), half)
         at = slice(h * half, (h + 1) * half)
-        parts.append(
-            shares(
-                expo_b[:, at], stat_b[0:1, at], norm_ref[1, 0:1, from_], norm_ref[1, 1:2, from_]
-            )
-        )
+        parts.append(shares(expo_b[:, at], stat_b[0:1, at], norm_ref[1, :, from_]))
     step = 256
     for c in range(width // step):
         at = slice(c * step, (c + 1) * step)
@@ -220,9 +215,22 @@
     return jnp.where(lanes == 0, high, jnp.where(lanes == 1, mass - high, 0.0)).astype(bf16)
 
 
-def add_kernel(a, b, out):
+def cross_kernel(place_ref, a, b, *rest):
+    outs, total_ref = rest[:-1], rest[-1]
     width = a.shape[1] - lane
     total, mass = added([a[...], b[...]], width)
+    total_ref[:, :width] = total.astype(bf16)
+    total_ref[:, width:] = halves(mass)
+    for d, out in zip(near, outs):
+        zl = (place_ref[5] + d) & 3
+        for zh in range(4):
+            at = pl.ds(pl.multiple_of((zh * 4 + zl) * 16, 16), 16)
+            out[zh * 16 : (zh + 1) * 16, :] = total_ref[at, :]
+
+
+def near_kernel(a, b, c, d, out):
+    width = a.shape[1] - lane
+    total, mass = added([a[...], b[...], c[...], d[...]], width)
     out[:, :width] = total.astype(bf16)
     out[:, width:] = halves(mass)
 
@@ -265,7 +273,7 @@
     narrow = ("y", "c")
     across = ("xh", "xl")
     parts = lax.axis_size(narrow)
-    zs = lax.axis_size("z")
+    zs = lax.axis_size(("zh", "zl"))
     n, x = lax.axis_index(narrow), lax.axis_index(across)
     me, core = lax.axis_index("xl"), lax.axis_index("c")
     count, width = points.shape
@@ -277,7 +285,7 @@
     swap = [(0, 1), (1, 0)]
     outer = [(0, 3), (3, 0), (1, 2), (2, 1)]
 
-    place = jnp.stack([coarse_ids[0], n, x, me, core]).astype(i32)
+    place = jnp.stack([coarse_ids[0], n, x, me, core, lax.axis_index("zl")]).astype(i32)
     half = call(
         cut_kernel,
         sds((count // 2 + 16, width), bf16),
@@ -293,7 +301,7 @@
     )
     first = lax.ppermute(half, "xl", swap)
     own = lax.dynamic_slice(centroids, (n * rows, 0), (rows, width))
-    column = lax.all_gather(own, "z", axis=0, tiled=True)
+    column = lax.all_gather(own, ("zh", "zl"), axis=0, tiled=True)
     first, column = lax.optimization_barrier((first, column))
     beyond = lax.ppermute(column, across, outer)
     second = lax.ppermute(first, "c", swap)
@@ -320,14 +328,14 @@
     )
     expo_c, expo_d, stat_c, stat_d, both = call(
         rest_kernel,
-        (expo, expo, stat, stat, sds((2, 2, count), f32)),
+        (expo, expo, stat, stat, sds((2, count), f32)),
         (place, beyond, points, first, second, mask, stat_a, stat_b),
         smem + vmem(7),
         flops=2 * flops,
         moved=12 << 20,
     )
     pool = ("xl",) + narrow
-    copies = jnp.broadcast_to(both, (2 * parts, 2, 2, count))
+    copies = jnp.broadcast_to(both, (2 * parts, 2, count))
     shared = lax.all_to_all(copies, pool, 0, 0, tiled=True)
 
     def sums(expo_a, expo_b, stat_a, stat_b):
@@ -338,13 +346,25 @@
             smem + vmem(8),
             flops=2 * flops,
             moved=10 << 20,
-            scratch=[pltpu.VMEM((2, 2, count), f32)],
+            scratch=[pltpu.VMEM((2, 1, count), f32)],
         )
 
     away = lax.ppermute(sums(expo_c, expo_d, stat_c, stat_d), across, outer)
     kept = sums(expo_a, expo_b, stat_a, stat_b)
-    added_up = call(add_kernel, sds((size, padded), bf16), (kept, away))
-    got = lax.all_to_all(added_up.reshape(zs, rows, padded), "z", 0, 0, tiled=True)
+    deep = ("zh", "zl")
+    group = sds((size // 4, padded), bf16)
+    cuts = call(
+        cross_kernel,
+        (group,) * 4,
+        (place, kept, away),
+        smem + vmem(2),
+        scratch=[pltpu.VMEM((size, padded), bf16)],
+    )
+    got = [cuts[0]] + [
+        lax.ppermute(cuts[k], deep, [(i, (i + near[k]) % zs) for i in range(zs)]) for k in (1, 2, 3)
+    ]
+    summed = call(near_kernel, group, tuple(got))
+    got = lax.all_to_all(summed.reshape(4, rows, padded), "zh", 0, 0, tiled=True)
     table = call(last_kernel, sds((parts, rows, padded), bf16), (got, own))
     whole = lax.all_to_all(table, narrow, 0, 0, tiled=True)
     new_table, masses = call(
@@ -354,8 +374,8 @@
 
 
 def solution(mesh):
-    chips = Mesh(mesh.devices.reshape(16, 2, 2, 4, 2), ("z", "xh", "xl", "y", "c"))
-    wide = ("z", "xh", "xl")
+    chips = Mesh(mesh.devices.reshape(4, 4, 2, 2, 4, 2), ("zh", "zl", "xh", "xl", "y", "c"))
+    wide = ("zh", "zl", "xh", "xl")
     return jax.shard_map(
         shards,
         mesh=chips,

time: 166 us -> 159 us (0.958)
  blocking collectives: 105 us -> 80.1 us
  starting transfers between devices: 21.4 us -> 33.7 us
  waiting for transfers between devices: 13.8 us -> 18.7 us
    all_to_all x1, blocking collectives: 44.5 us -> 22.8 us  [shards(): lax.all_to_all(summed.reshape(4, rows, padded), 'zh', 0, 0, tiled=True)]
    ppermute x0 -> x3, starting transfers between devices: none -> 12.4 us  [shards(): lax.ppermute(cuts[k], deep, [(i, (i + near[k]) % zs) for i in range(zs)])]
    ppermute x0 -> x3, waiting for transfers between devices: none -> 4.23 us  [shards(): lax.ppermute(cuts[k], deep, [(i, (i + near[k]) % zs) for i in range(zs)])]
    all_to_all x1, blocking collectives: 13.5 us -> 11.7 us  [shards(): shared = lax.all_to_all(copies, pool, 0, 0, tiled=True)]
    pallas_call x10 -> x11, Pallas kernels: 20.9 us -> 21.3 us  [call(): pl.pallas_call(kernel, out_shape=outs, in_specs=specs or vmem(len(args)),...]
  transfers between devices with their start and end apart: 4 -> 7, of which waited for: 2 -> 3; matrix products, arithmetic and copies ran while one was open for 0% -> 0% of each run, Pallas kernels for 6% -> 6%
where the time goes in v5:
time: 159 us
  blocking collectives  80.1 us (50%)
  starting transfers between devices  33.7 us (21%)
  Pallas kernels  21.3 us (13%)
  waiting for transfers between devices  18.7 us (12%)
  local copies, waits for them, and re-layouts  3.5 us (2%)
    all_gather x1, blocking collectives, shards(): column = lax.all_gather(own, ('zh', 'zl'), axis=0, tiled=True)  31.9 us
    all_to_all x1, blocking collectives, shards(): lax.all_to_all(summed.reshape(4, rows, padded), 'zh', 0, 0, tiled=True)  22.8 us
    pallas_call x11, Pallas kernels, call(): pl.pallas_call(kernel, out_shape=outs, in_specs=specs or vmem(len(args)),...  21.3 us
    all_to_all x1, blocking collectives, shards(): whole = lax.all_to_all(table, narrow, 0, 0, tiled=True)  13.6 us
    ppermute x3, starting transfers between devices, shards(): lax.ppermute(cuts[k], deep, [(i, (i + near[k]) % zs) for i in range(zs)])  12.4 us
    all_to_all x1, blocking collectives, shards(): shared = lax.all_to_all(copies, pool, 0, 0, tiled=True)  11.7 us
    ppermute x1, waiting for transfers between devices, shards(): away = lax.ppermute(sums(expo_c, expo_d, stat_c, stat_d), across, outer)  9.7 us
    ppermute x1, starting transfers between devices, shards(): second = lax.ppermute(first, 'c', swap)  9.44 us
  transfers between devices with their start and end apart: 7, of which 3 were waited for; matrix products, arithmetic and copies ran while one was open for 0% of the time, Pallas kernels for 6%

profile of v5, /device:TPU:1, one launch (start us, length us, event | category | flops | bytes accessed | tf_op | source)
XLA Modules:
  0.0 158.8 jit_solution(71367528170035291)
XLA Ops:
  0.6 0.0 copy-start
  1.3 0.1 stack.23.place_ref
  1.4 0.0 copy-start.1
  1.4 1.9 %copy-done.1 = bf16[1536,1024]{1,0:T(8,128)(2,1)S(1)} copy-done((bf16[1536,1024]{1,0:T(8,128)(2,1)S(1)}, bf16[1536,1024]{1,0:T(8,128)(2,1)}, u32[]{:S(2)}) %copy-start.1) | copy-done | bytes 3145752
  3.3 0.0 copy-start.3
  3.3 0.0 copy-start.2
  3.3 1.7 %shard_map.68 = bf16[784,1024]{1,0:T(8,128)(2,1)} custom-call(s32[6]{0:T(128)S(1)} %stack.23.place_ref, bf16[1536,1024]{1,0:T(8,128)(2,1)S(1)} %copy-done.1), custom_call_target="tpu_custom_call" | custom-call | bytes 3145728 | tf_op jit(solution)/shard_map/pallas_call | solution.py:261
  5.1 4.0 %collective-permute-start = (bf16[784,1024]{1,0:T(8,128)(2,1)}, bf16[784,1024]{1,0:T(8,128)(2,1)}, u32[]{:S(2)}, u32[]{:S(2)}) collective-permute-start(bf16[784,1024]{1,0:T(8,128)(2,1)} %shard_map.68), channel_id=1, source_target_pairs={{0,8},{8,0},{1,9},{9,1},{2,10},{10,2},{3,11},{11,3},{4,12},{12,4},... | collective-permute-start | bytes 4816904 | tf_op jit(solution)/shard_map/ppermute | solution.py:302
  9.0 0.0 copy-done
  9.1 31.9 %all_gather.3.means_ref = bf16[256,1024]{1,0:T(8,128)(2,1)S(1)} all-gather(bf16[16,1024]{1,0:T(8,128)(2,1)S(1)} %constant_dynamic-slice_fusion.cen), channel_id=1, replica_groups=mesh['zh'=4,'zl'=4,'xh'=2,'xl'=2,'y'=4,'c'=2] {'zh','zl'}, dimensions={0}, use_global_device_ids=true | all-gather | bytes 557056 | tf_op jit(solution)/shard_map/all_gather | solution.py:304
  41.0 0.0 collective-permute-done.refs_0_.first_ref
  41.0 9.4 %collective-permute-start.1 = (bf16[784,1024]{1,0:T(8,128)(2,1)}, bf16[784,1024]{1,0:T(8,128)(2,1)S(1)}, u32[]{:S(2)}, u32[]{:S(2)}) collective-permute-start(bf16[784,1024]{1,0:T(8,128)(2,1)} %collective-permute-done.refs_0_.first_ref), channel_id=1, source_target_pairs={{0,1},{1,0},{2,3},{3,2},{4,5},{5,4},{6,7},{7,6},{8,9},{9,8},{10,11... | collective-permute-start | bytes 4816904 | tf_op jit(solution)/shard_map/ppermute | solution.py:307
  50.4 3.7 %collective-permute-start.2 = (bf16[256,1024]{1,0:T(8,128)(2,1)S(1)}, bf16[256,1024]{1,0:T(8,128)(2,1)S(1)}, u32[]{:S(2)}, u32[]{:S(2)}) collective-permute-start(bf16[256,1024]{1,0:T(8,128)(2,1)S(1)} %all_gather.3.means_ref), channel_id=1, source_target_pairs={{0,24},{24,0},{8,16},{16,8},{1,25},{25,1},{9,17},{17,9},{2,26},{26... | collective-permute-start | bytes 1572872 | tf_op jit(solution)/shard_map/ppermute | solution.py:306
  54.2 0.7 slice.3.other_ref
  54.9 0.0 copy-done.3
  54.9 0.0 copy-start.4
  54.9 0.8 copy-done.4
  55.6 2.3 %shard_map.69.mask_ref = f32[128,128]{1,0:T(8,128)S(1)} custom-call(s32[6]{0:T(128)S(1)} %stack.23.place_ref, bf16[16,128]{1,0:T(8,128)(2,1)S(1)} %slice.3.other_ref, s32[16,2048]{1,0:T(8,128)S(1)} %copy-done.3, s32[64,128]{1,0:T(8,128)S(1)} %bitcast.9), custom_call_target="tpu_custom_call" | custom-call | bytes 8388608 | tf_op jit(solution)/shard_map/pallas_call | solution.py:261
  57.9 0.0 copy-done.2
  57.9 1.5 shard_map.70
  59.4 0.0 collective-permute-done.1.refs_1_.second_ref
  59.4 2.9 %shard_map.71 = (f32[256,1536]{1,0:T(8,128)S(1)}, f32[2,1536]{1,0:T(2,128)S(1)}) custom-call(bf16[256,1024]{1,0:T(8,128)(2,1)S(1)} %all_gather.3.means_ref, f32[128,128]{1,0:T(8,128)S(1)} %shard_map.69.mask_ref, bf16[784,1024]{1,0:T(8,128)(2,1)} %collective-permute-done.refs_0_.first_ref, bf16[784,1024]{1,0:T(8,128)(2,1)S(1)} %collective-permute-done.1.refs_1_.second_ref), custom_call_target="tpu_custom_call" | custom-call | flops 805306368 | bytes 6291456 | tf_op jit(solution)/shard_map/pallas_call | solution.py:261
  62.3 4.8 %collective-permute-done.2.means_ref = bf16[256,1024]{1,0:T(8,128)(2,1)S(1)} collective-permute-done((bf16[256,1024]{1,0:T(8,128)(2,1)S(1)}, bf16[256,1024]{1,0:T(8,128)(2,1)S(1)}, u32[]{:S(2)}, u32[]{:S(2)}) %collective-permute-start.2) | collective-permute-done | bytes 524320 | tf_op jit(solution)/shard_map/ppermute | solution.py:306
  67.1 4.1 %shard_map.72 = (f32[256,1536]{1,0:T(8,128)S(1)}, f32[256,1536]{1,0:T(8,128)S(1)}, f32[2,1536]{1,0:T(2,128)S(1)}, f32[2,1536]{1,0:T(2,128)S(1)}, f32[2,1536]{1,0:T(2,128)S(1)}) custom-call(s32[6]{0:T(128)S(1)} %stack.23.place_ref, bf16[256,1024]{1,0:T(8,128)(2,1)S(1)} %collective-permute-done.2.means_ref, bf16[1536,1024]{1,0:T(8,128)(2,1)S(1)} %copy-done.2, ...), custom_call_target="tpu_custom_call" | custom-call | flops 1610612736 | bytes 12582912 | tf_op jit(solution)/shard_map/pallas_call | solution.py:261
  71.2 0.1 broadcast_in_dim.3
  71.3 11.7 %all_to_all.15.all_ref = f32[16,2,1536]{2,1,0:T(2,128)S(1)} all-to-all(f32[16,2,1536]{2,1,0:T(2,128)S(1)} %broadcast_in_dim.3), channel_id=1, replica_groups=mesh['zh'=4,'zl'=4,'xh'=2,'xl'=2,'y'=4,'c'=2] {'xl','y','c'}, dimensions={0} | all-to-all | bytes 393216 | tf_op jit(solution)/shard_map/all_to_all | solution.py:339
  83.0 3.3 %shard_map.74 = bf16[256,1152]{1,0:T(8,128)(2,1)S(1)} custom-call(s32[6]{0:T(128)S(1)} %stack.23.place_ref, f32[256,1536]{1,0:T(8,128)S(1)} %get-tuple-element.26.expo_a, f32[256,1536]{1,0:T(8,128)S(1)} %get-tuple-element.27.expo_b, f32[2,1536]{1,0:T(2,128)S(1)} %get-tuple-element.28.stat_a, f32[2,1536]{1,0:T(2,128)S(1)} %get-tuple-element.29.stat_b, ...), custom_call_target="tpu_custom_call" | custom-call | flops 1610612736 | bytes 10485760 | tf_op jit(solution)/shard_map/pallas_call | solution.py:261
  86.4 4.1 %collective-permute-start.3 = (bf16[256,1152]{1,0:T(8,128)(2,1)S(1)}, bf16[256,1152]{1,0:T(8,128)(2,1)S(1)}, u32[]{:S(2)}, u32[]{:S(2)}) collective-permute-start(bf16[256,1152]{1,0:T(8,128)(2,1)S(1)} %shard_map.74), channel_id=1, source_target_pairs={{0,24},{24,0},{8,16},{16,8},{1,25},{25,1},{9,17},{17,9},{2,26},{26... | collective-permute-start | bytes 1769480 | tf_op jit(solution)/shard_map/ppermute | solution.py:352
  90.5 3.3 %shard_map.73.a = bf16[256,1152]{1,0:T(8,128)(2,1)S(1)} custom-call(s32[6]{0:T(128)S(1)} %stack.23.place_ref, f32[256,1536]{1,0:T(8,128)S(1)} %get-tuple-element.21.expo_a, f32[256,1536]{1,0:T(8,128)S(1)} %get-tuple-element.22.expo_b, f32[2,1536]{1,0:T(2,128)S(1)} %get-tuple-element.23.stat_a, f32[2,1536]{1,0:T(2,128)S(1)} %get-tuple-element.24.stat_b, ...), custom_call_target="tpu_custom_call" | custom-call | flops 1610612736 | bytes 10485760 | tf_op jit(solution)/shard_map/pallas_call | solution.py:261
  93.8 9.7 %collective-permute-done.3.b = bf16[256,1152]{1,0:T(8,128)(2,1)S(1)} collective-permute-done((bf16[256,1152]{1,0:T(8,128)(2,1)S(1)}, bf16[256,1152]{1,0:T(8,128)(2,1)S(1)}, u32[]{:S(2)}, u32[]{:S(2)}) %collective-permute-start.3) | collective-permute-done | bytes 589856 | tf_op jit(solution)/shard_map/ppermute | solution.py:352
  103.5 0.9 shard_map.75
  104.4 1.9 %collective-permute-start.4 = (bf16[64,1152]{1,0:T(8,128)(2,1)S(1)}, bf16[64,1152]{1,0:T(8,128)(2,1)S(1)}, u32[]{:S(2)}, u32[]{:S(2)}) collective-permute-start(bf16[64,1152]{1,0:T(8,128)(2,1)S(1)} %get-tuple-element.31), channel_id=1, source_target_pairs={{0,32},{32,64},{64,96},{96,128},{128,160},{160,192},{192,224},{224... | collective-permute-start | bytes 442376 | tf_op jit(solution)/shard_map/ppermute | solution.py:364
  106.3 4.0 %collective-permute-start.5 = (bf16[64,1152]{1,0:T(8,128)(2,1)S(1)}, bf16[64,1152]{1,0:T(8,128)(2,1)S(1)}, u32[]{:S(2)}, u32[]{:S(2)}) collective-permute-start(bf16[64,1152]{1,0:T(8,128)(2,1)S(1)} %get-tuple-element.32), channel_id=1, source_target_pairs={{0,64},{32,96},{64,128},{96,160},{128,192},{160,224},{192,256},{22... | collective-permute-start | bytes 442376 | tf_op jit(solution)/shard_map/ppermute | solution.py:364
  110.4 6.5 %collective-permute-start.6 = (bf16[64,1152]{1,0:T(8,128)(2,1)S(1)}, bf16[64,1152]{1,0:T(8,128)(2,1)S(1)}, u32[]{:S(2)}, u32[]{:S(2)}) collective-permute-start(bf16[64,1152]{1,0:T(8,128)(2,1)S(1)} %get-tuple-element.33), channel_id=1, source_target_pairs={{0,480},{32,0},{64,32},{96,64},{128,96},{160,128},{192,160},{224,1... | collective-permute-start | bytes 442376 | tf_op jit(solution)/shard_map/ppermute | solution.py:364
  116.9 0.0 collective-permute-done.4.b
  116.9 4.2 %collective-permute-done.5.c = bf16[64,1152]{1,0:T(8,128)(2,1)S(1)} collective-permute-done((bf16[64,1152]{1,0:T(8,128)(2,1)S(1)}, bf16[64,1152]{1,0:T(8,128)(2,1)S(1)}, u32[]{:S(2)}, u32[]{:S(2)}) %collective-permute-start.5) | collective-permute-done | bytes 147488 | tf_op jit(solution)/shard_map/ppermute | solution.py:364
  121.1 0.0 collective-permute-done.6.d
  121.1 0.2 shard_map.76
  121.4 22.8 %all_to_all.16.ref = bf16[4,16,1152]{2,1,0:T(8,128)(2,1)S(1)} all-to-all(bf16[4,16,1152]{2,1,0:T(8,128)(2,1)S(1)} %bitcast.8), channel_id=1, replica_groups=mesh['zh'=4,'zl'=4,'xh'=2,'xl'=2,'y'=4,'c'=2] {'zh'}, dimensions={0} | all-to-all | bytes 294912 | tf_op jit(solution)/shard_map/all_to_all | solution.py:367
  144.2 0.2 shard_map.77
  144.4 13.6 %all_to_all.17.ref = bf16[8,16,1152]{2,1,0:T(8,128)(2,1)S(1)} all-to-all(bf16[8,16,1152]{2,1,0:T(8,128)(2,1)S(1)} %shard_map.77), channel_id=1, replica_groups=mesh['zh'=4,'zl'=4,'xh'=2,'xl'=2,'y'=4,'c'=2] {'y','c'}, dimensions={0} | all-to-all | bytes 589824 | tf_op jit(solution)/shard_map/all_to_all | solution.py:369
  157.9 0.8 shard_map.78
  (1 shorter events, 0.0 us)
Async XLA Ops:
  0.6 8.4 %copy-start = (bf16[128,1024]{1,0:T(8,128)(2,1)S(1)}, bf16[128,1024]{1,0:T(8,128)(2,1)}, u32[]{:S(2)}) copy-start(bf16[128,1024]{1,0:T(8,128)(2,1)} %param.9) | copy-start | bytes 786436
  1.4 1.9 %copy-start.1 = (bf16[1536,1024]{1,0:T(8,128)(2,1)S(1)}, bf16[1536,1024]{1,0:T(8,128)(2,1)}, u32[]{:S(2)}) copy-start(bf16[1536,1024]{1,0:T(8,128)(2,1)} %points_ref.7) | copy-start | bytes 9437188
  3.3 51.5 %copy-start.3 = (s32[16,2048]{1,0:T(8,128)S(1)}, s32[16,2048]{1,0:T(8,128)}, u32[]{:S(2)}) copy-start(s32[16,2048]{1,0:T(8,128)} %lists_ref.1) | copy-start | bytes 393220
  3.3 54.6 %copy-start.2 = (bf16[1536,1024]{1,0:T(8,128)(2,1)S(1)}, bf16[1536,1024]{1,0:T(8,128)(2,1)}, u32[]{:S(2)}) copy-start(bf16[1536,1024]{1,0:T(8,128)(2,1)} %points_ref.7) | copy-start | bytes 9437188
  5.1 35.9 %collective-permute-start = (bf16[784,1024]{1,0:T(8,128)(2,1)}, bf16[784,1024]{1,0:T(8,128)(2,1)}, u32[]{:S(2)}, u32[]{:S(2)}) collective-permute-start(bf16[784,1024]{1,0:T(8,128)(2,1)} %shard_map.68), channel_id=1, source_target_pairs={{0,8},{8,0},{1,9},{9,1},{2,10},{10,2},{3,11},{11,3},{4,12},{12,4},... | collective-permute-start | bytes 4816904 | tf_op jit(solution)/shard_map/ppermute | solution.py:302
  41.0 18.4 %collective-permute-start.1 = (bf16[784,1024]{1,0:T(8,128)(2,1)}, bf16[784,1024]{1,0:T(8,128)(2,1)S(1)}, u32[]{:S(2)}, u32[]{:S(2)}) collective-permute-start(bf16[784,1024]{1,0:T(8,128)(2,1)} %collective-permute-done.refs_0_.first_ref), channel_id=1, source_target_pairs={{0,1},{1,0},{2,3},{3,2},{4,5},{5,4},{6,7},{7,6},{8,9},{9,8},{10,11... | collective-permute-start | bytes 4816904 | tf_op jit(solution)/shard_map/ppermute | solution.py:307
  50.4 16.6 %collective-permute-start.2 = (bf16[256,1024]{1,0:T(8,128)(2,1)S(1)}, bf16[256,1024]{1,0:T(8,128)(2,1)S(1)}, u32[]{:S(2)}, u32[]{:S(2)}) collective-permute-start(bf16[256,1024]{1,0:T(8,128)(2,1)S(1)} %all_gather.3.means_ref), channel_id=1, source_target_pairs={{0,24},{24,0},{8,16},{16,8},{1,25},{25,1},{9,17},{17,9},{2,26},{26... | collective-permute-start | bytes 1572872 | tf_op jit(solution)/shard_map/ppermute | solution.py:306
  54.9 0.8 copy-start.4
  86.4 17.2 %collective-permute-start.3 = (bf16[256,1152]{1,0:T(8,128)(2,1)S(1)}, bf16[256,1152]{1,0:T(8,128)(2,1)S(1)}, u32[]{:S(2)}, u32[]{:S(2)}) collective-permute-start(bf16[256,1152]{1,0:T(8,128)(2,1)S(1)} %shard_map.74), channel_id=1, source_target_pairs={{0,24},{24,0},{8,16},{16,8},{1,25},{25,1},{9,17},{17,9},{2,26},{26... | collective-permute-start | bytes 1769480 | tf_op jit(solution)/shard_map/ppermute | solution.py:352
  104.4 12.5 %collective-permute-start.4 = (bf16[64,1152]{1,0:T(8,128)(2,1)S(1)}, bf16[64,1152]{1,0:T(8,128)(2,1)S(1)}, u32[]{:S(2)}, u32[]{:S(2)}) collective-permute-start(bf16[64,1152]{1,0:T(8,128)(2,1)S(1)} %get-tuple-element.31), channel_id=1, source_target_pairs={{0,32},{32,64},{64,96},{96,128},{128,160},{160,192},{192,224},{224... | collective-permute-start | bytes 442376 | tf_op jit(solution)/shard_map/ppermute | solution.py:364
  106.3 14.8 %collective-permute-start.5 = (bf16[64,1152]{1,0:T(8,128)(2,1)S(1)}, bf16[64,1152]{1,0:T(8,128)(2,1)S(1)}, u32[]{:S(2)}, u32[]{:S(2)}) collective-permute-start(bf16[64,1152]{1,0:T(8,128)(2,1)S(1)} %get-tuple-element.32), channel_id=1, source_target_pairs={{0,64},{32,96},{64,128},{96,160},{128,192},{160,224},{192,256},{22... | collective-permute-start | bytes 442376 | tf_op jit(solution)/shard_map/ppermute | solution.py:364
  110.4 10.7 %collective-permute-start.6 = (bf16[64,1152]{1,0:T(8,128)(2,1)S(1)}, bf16[64,1152]{1,0:T(8,128)(2,1)S(1)}, u32[]{:S(2)}, u32[]{:S(2)}) collective-permute-start(bf16[64,1152]{1,0:T(8,128)(2,1)S(1)} %get-tuple-element.33), channel_id=1, source_target_pairs={{0,480},{32,0},{64,32},{96,64},{128,96},{160,128},{192,160},{224,1... | collective-permute-start | bytes 442376 | tf_op jit(solution)/shard_map/ppermute | solution.py:364

commit v6 on v5

v6 whole, which is shorter than its diff:
```python
import functools

import jax
import jax.numpy as jnp
from jax import lax
from jax.experimental import pallas as pl
from jax.experimental.pallas import tpu as pltpu
from jax.sharding import Mesh, PartitionSpec as P

temper = 0.1
prior = 0.01
gone = -3e38
near = (0, 1, 2, -1)
f32 = jnp.float32
bf16 = jnp.bfloat16
i32 = jnp.int32
lane = 128


def vmem(n):
    return [pl.BlockSpec(memory_space=pltpu.VMEM)] * n


def params():
    return pltpu.CompilerParams(vmem_limit_bytes=20 * 1024 * 1024)


def mask_kernel(place_ref, lists_ref, owner_ref, *refs):
    *other, mask_ref = refs
    n, me, zl = place_ref[1], place_ref[2], place_ref[4]
    count = lists_ref.shape[1]
    blocks = owner_ref.shape[0]
    in_block = lax.broadcasted_iota(i32, (lane, count), 0)
    of_blocks = lax.broadcasted_iota(i32, (blocks, count), 0)
    of_lists = lax.broadcasted_iota(i32, lists_ref.shape, 0)
    cluster = other[0][0:1, 0:1].astype(f32).astype(i32) if other else place_ref[0]
    ids = jnp.sum(jnp.where(of_lists == cluster, lists_ref[...], 0), axis=0, keepdims=True)
    which = (of_blocks == (ids >> 7)).astype(bf16)
    here = in_block == (ids & 127)
    rows = owner_ref[...]

    def pick(table):
        found = lax.dot_general(
            table.astype(f32).astype(bf16),
            which,
            (((0,), (0,)), ((), ())),
            preferred_element_type=f32,
        )
        return jnp.sum(jnp.where(here, found, 0.0), axis=0, keepdims=True).astype(i32)

    owner = pick(rows >> 7)
    inner = pick(rows & 127)
    row = ((owner >> 1) & 1) * 64 + (owner >> 4) * 16 + (inner & 15)
    mine = ((inner >> 4) == n) & ((owner & 1) == me)
    block = jnp.where(mine, ((owner >> 2) - zl) & 3, lane)
    left = (in_block == row).astype(bf16)
    right = (in_block == block).astype(bf16)
    mask_ref[...] = lax.dot_general(
        left, right, (((1,), (1,)), ((), ())), preferred_element_type=f32
    )


def cut_kernel(place_ref, points_ref, half_ref, id_ref, sem, id_sem):
    rows = points_ref.shape[0] // 2
    start = pl.multiple_of(place_ref[3] * rows, rows)
    copy = pltpu.make_async_copy(points_ref.at[pl.ds(start, rows)], half_ref.at[pl.ds(0, rows)], sem)
    copy.start()
    id_ref[...] = jnp.full(id_ref.shape, place_ref[0].astype(f32), f32).astype(bf16)
    last = pltpu.make_async_copy(id_ref, half_ref.at[pl.ds(rows, 16)], id_sem)
    last.start()
    last.wait()
    copy.wait()


def squares(means):
    wide = means.astype(f32)
    return jnp.sum(wide * wide, axis=1, keepdims=True) * (-1.0 / temper)


def listed_rows(mask_ref, first, rows):
    picked = [mask_ref[:, first + i : first + i + 1] for i in range(rows // lane)]
    return jnp.concatenate(picked) > 0.5


def scored(means, points, bias, listed):
    dots = lax.dot_general(
        means, points, (((1,), (1,)), ((), ())), preferred_element_type=f32
    )
    t = jnp.where(listed, dots * (2.0 / temper) + bias, gone)
    top = jnp.max(t, axis=0, keepdims=True)
    expo = jnp.exp(t - top)
    return expo, top, jnp.sum(expo, axis=0, keepdims=True)


def blocks_of(count, *refs):
    step = 256
    rows = count // len(refs)
    for c in range(count // step):
        start = c * step
        ref = refs[start // rows]
        start %= rows
        yield slice(c * step, (c + 1) * step), ref, slice(start, start + step)


def score_kernel(*refs):
    *pieces, mask_ref, points_ref, expo_ref, stat_ref = refs
    means = jnp.concatenate([piece[...] for piece in pieces])
    bias = squares(means)
    listed = listed_rows(mask_ref, 0, means.shape[0])
    for at, ref, rows in blocks_of(expo_ref.shape[1], points_ref):
        expo_ref[:, at], stat_ref[0:1, at], stat_ref[1:2, at] = scored(
            means, ref[rows, :], bias, listed
        )


def other_kernel(place_ref, old_ref, *refs):
    *pieces, mask_ref, first_ref, second_ref, expo_ref, stat_ref, both_ref = refs
    means = jnp.concatenate([piece[...] for piece in pieces])
    bias = squares(means)
    listed = listed_rows(mask_ref, 0, means.shape[0])
    me, core = place_ref[2], place_ref[3]
    count = expo_ref.shape[1]
    half = count // 2
    both_ref[pl.ds(me, 1), :] = old_ref[0:1, :] + jnp.log(old_ref[1:2, :])
    for at, ref, rows in blocks_of(count, first_ref, second_ref):
        expo_ref[:, at], top, total = scored(means, ref[rows, :], bias, listed)
        stat_ref[0:1, at] = top
        stat_ref[1:2, at] = total
        start = pl.multiple_of(at.start + (half * core if at.start < half else -half * core), lane)
        both_ref[pl.ds(1 - me, 1), pl.ds(start, 256)] = top + jnp.log(total)


def sums_kernel(
    groups,
    place_ref,
    all_ref,
    points_ref,
    first_ref,
    second_ref,
    expo_a,
    stat_a,
    expo_b,
    stat_b,
    one_ref,
    two_ref,
    norm_ref,
):
    me, core = place_ref[2], place_ref[3]
    half = points_ref.shape[0] // 2
    width = points_ref.shape[1]
    for slab, which in enumerate((me, 1 - me)):
        each = [all_ref[k, pl.ds(which, 1), :] for k in range(all_ref.shape[0])]
        top = functools.reduce(jnp.maximum, each)
        total = functools.reduce(jnp.add, [jnp.exp(one - top) for one in each])
        norm_ref[slab] = top + jnp.log(total)

    def shares(expo, stat, lanes, norm):
        scale = jnp.exp(stat[0:1, lanes] - norm)
        rows = [expo[j * lane : (j + 1) * lane, lanes] for j in groups]
        return jnp.concatenate([(row * scale).astype(bf16) for row in rows])

    parts = [shares(expo_a, stat_a, slice(None), norm_ref[0])]
    for h in range(2):
        from_ = pl.ds(pl.multiple_of((core if h == 0 else 1 - core) * half, lane), half)
        at = slice(h * half, (h + 1) * half)
        parts.append(shares(expo_b, stat_b, at, norm_ref[1, :, from_]))
    step = 256
    for c in range(width // step):
        at = slice(c * step, (c + 1) * step)
        total = None
        for part, ref in zip(parts, (points_ref, first_ref, second_ref)):
            more = jnp.dot(part, ref[: part.shape[1], at], preferred_element_type=f32)
            total = more if total is None else total + more
        total = total.astype(bf16)
        one_ref[:, at] = total[:lane]
        two_ref[:, at] = total[lane:]
    mass = sum(jnp.sum(part.astype(f32), axis=1, keepdims=True) for part in parts)
    tail = halves(mass)
    one_ref[:, width:] = tail[:lane]
    two_ref[:, width:] = tail[lane:]


def added(pieces, width):
    total = pieces[0].astype(f32)
    for piece in pieces[1:]:
        total = total + piece.astype(f32)
    return total[:, :width], total[:, width : width + 1] + total[:, width + 1 : width + 2]


def halves(mass):
    high = mass.astype(bf16).astype(f32)
    lanes = lax.broadcasted_iota(i32, (mass.shape[0], lane), 1)
    return jnp.where(lanes == 0, high, jnp.where(lanes == 1, mass - high, 0.0)).astype(bf16)


def near_kernel(a, b, c, d, out):
    width = a.shape[1] - lane
    total, mass = added([a[...], b[...], c[...], d[...]], width)
    out[:, :width] = total.astype(bf16)
    out[:, width:] = halves(mass)


def last_kernel(ref, cen, out):
    width = cen.shape[1]
    total, mass = added([ref[k] for k in range(ref.shape[0])], width)
    new = (total + prior * cen[...].astype(f32)) / (mass + prior)
    new = new.astype(bf16)
    tail = halves(mass)
    for k in range(out.shape[0]):
        out[k, :, :width] = new
        out[k, :, width:] = tail


def out_kernel(ref, table_ref, mass_ref):
    parts, rows, padded = ref.shape
    width = padded - lane
    tails = []
    for k in range(parts):
        table_ref[k * rows : (k + 1) * rows, :] = ref[k, :, :width].astype(f32)
        tails.append(ref[k, :, width:].astype(f32))
    tail = jnp.concatenate(tails).T
    mass_ref[...] = tail[0:1, :] + tail[1:2, :]


def call(kernel, outs, args, specs=None, flops=0, moved=0, scratch=(), home=pltpu.VMEM):
    return pl.pallas_call(
        kernel,
        out_shape=outs,
        in_specs=specs or vmem(len(args)),
        out_specs=jax.tree.map(lambda _: pl.BlockSpec(memory_space=home), outs),
        scratch_shapes=scratch,
        compiler_params=params(),
        cost_estimate=pl.CostEstimate(flops=flops, bytes_accessed=moved, transcendentals=0),
    )(*args)


def shards(points, coarse_ids, lists, owner_map, centroids):
    narrow, deep, far = ("y", "c"), ("zh", "zl"), ("xh", "zh")
    parts, zs, peers = (lax.axis_size(a) for a in (narrow, deep, far))
    n = lax.axis_index(narrow)
    count, width = points.shape
    rows = centroids.shape[0] // parts
    size = rows * peers
    padded = width + lane
    sds = jax.ShapeDtypeStruct
    smem = [pl.BlockSpec(memory_space=pltpu.SMEM)]
    swap = [(0, 1), (1, 0)]

    def along(a, by):
        return lax.ppermute(a, deep, [(i, (i + by) % zs) for i in range(zs)])

    place = jnp.stack(
        [coarse_ids[0], n, lax.axis_index("xl"), lax.axis_index("c"), lax.axis_index("zl")]
    ).astype(i32)
    half = call(
        cut_kernel,
        sds((count // 2 + 16, width), bf16),
        (place, points),
        smem + [pl.BlockSpec(memory_space=pltpu.HBM)],
        moved=3 << 20,
        scratch=[
            pltpu.VMEM((16, width), bf16),
            pltpu.SemaphoreType.DMA,
            pltpu.SemaphoreType.DMA,
        ],
        home=pl.ANY,
    )
    first = lax.ppermute(half, "xl", swap)
    own = lax.dynamic_slice(centroids, (n * rows, 0), (rows, width))
    copies = jnp.broadcast_to(own, (peers, rows, width))
    group = lax.all_to_all(copies, far, 0, 0, tiled=True).reshape(size, width)
    pieces = [group] + [along(group, -d) for d in near[1:]]
    first, *pieces = lax.optimization_barrier((first, *pieces))
    second = lax.ppermute(first, "c", swap)
    flops = 2 * len(near) * size * count * width
    stat = sds((2, count), f32)
    expo = sds((len(near) * size, count), f32)

    def listed(*other):
        return call(
            mask_kernel,
            sds((lane, lane), f32),
            (place, lists, owner_map.reshape(-1, lane)) + other,
            smem + vmem(2 + len(other)),
            moved=8 << 20,
        )

    expo_a, stat_a = call(
        score_kernel, (expo, stat), (*pieces, listed(), points), flops=flops, moved=6 << 20
    )
    mask = listed(first[count // 2 :, :lane])
    expo_b, stat_b, both = call(
        other_kernel,
        (expo, stat, sds((2, count), f32)),
        (place, stat_a, *pieces, mask, first, second),
        smem + vmem(8),
        flops=flops,
        moved=6 << 20,
    )
    pool = ("xl",) + narrow
    copies = jnp.broadcast_to(both, (2 * parts, 2, count))
    shared = lax.all_to_all(copies, pool, 0, 0, tiled=True)

    def sums(*groups):
        return call(
            functools.partial(sums_kernel, groups),
            (sds((size, padded), bf16),) * 2,
            (place, shared, points, first, second, expo_a, stat_a, expo_b, stat_b),
            smem + vmem(8),
            flops=flops,
            moved=10 << 20,
            scratch=[pltpu.VMEM((2, 1, count), f32)],
        )

    two, one = sums(2, 1)
    three, kept = sums(3, 0)
    got = [kept, along(one, near[1]), along(two, near[2]), along(three, near[3])]
    summed = call(near_kernel, sds((size, padded), bf16), tuple(got))
    got = lax.all_to_all(summed.reshape(peers, rows, padded), far, 0, 0, tiled=True)
    table = call(last_kernel, sds((parts, rows, padded), bf16), (got, own))
    whole = lax.all_to_all(table, narrow, 0, 0, tiled=True)
    new_table, masses = call(
        out_kernel, (sds((parts * rows, width), f32), sds((1, parts * rows), f32)), (whole,)
    )
    return new_table, masses[0]


def solution(mesh):
    chips = Mesh(mesh.devices.reshape(4, 4, 2, 2, 4, 2), ("zh", "zl", "xh", "xl", "y", "c"))
    wide = ("zh", "zl", "xh", "xl")
    return jax.shard_map(
        shards,
        mesh=chips,
        in_specs=(P(wide, None), P(wide), P(), P(), P(wide, None)),
        out_specs=(P(wide, None), P(wide)),
        check_vma=False,
    )
```

time: 159 us -> 172 us (1.082)
  the two profiles are of different devices: /device:TPU:1 before, /device:TPU:33 now
where the time goes in v6:
time: 172 us
  blocking collectives  94.2 us (55%)
  starting transfers between devices  35 us (20%)
  Pallas kernels  19.2 us (11%)
  waiting for transfers between devices  18.3 us (11%)
  local copies, waits for them, and re-layouts  3.51 us (2%)
    all_to_all x1, blocking collectives, shards(): group = lax.all_to_all(copies, far, 0, 0, tiled=True).reshape(size, width)  39.8 us
    all_to_all x1, blocking collectives, shards(): lax.all_to_all(summed.reshape(peers, rows, padded), far, 0, 0, tiled=True)  30.3 us
    ppermute x6, starting transfers between devices, along(): return lax.ppermute(a, deep, [(i, (i + by) % zs) for i in range(zs)])  25.2 us
    pallas_call x10, Pallas kernels, call(): pl.pallas_call(kernel, out_shape=outs, in_specs=specs or vmem(len(args)),...  19.2 us
    ppermute x6, waiting for transfers between devices, along(): return lax.ppermute(a, deep, [(i, (i + by) % zs) for i in range(zs)])  18.3 us
    all_to_all x1, blocking collectives, shards(): whole = lax.all_to_all(table, narrow, 0, 0, tiled=True)  13 us
    all_to_all x1, blocking collectives, shards(): shared = lax.all_to_all(copies, pool, 0, 0, tiled=True)  11.1 us
    ppermute x1, starting transfers between devices, shards(): second = lax.ppermute(first, 'c', swap)  6.65 us
  transfers between devices with their start and end apart: 8, of which 3 were waited for; matrix products, arithmetic and copies ran while one was open for 0% of the time, Pallas kernels for 5%

profile of v6, /device:TPU:33, one launch (start us, length us, event | category | flops | bytes accessed | tf_op | source)
XLA Modules:
  0.0 171.8 jit_solution(7303348675303048934)
XLA Ops:
  0.6 0.0 copy-start
  1.3 0.1 stack.19.place_ref
  1.4 0.0 copy-start.1
  1.4 1.9 %copy-done.1 = bf16[1536,1024]{1,0:T(8,128)(2,1)S(1)} copy-done((bf16[1536,1024]{1,0:T(8,128)(2,1)S(1)}, bf16[1536,1024]{1,0:T(8,128)(2,1)}, u32[]{:S(2)}) %copy-start.1) | copy-done | bytes 3145752
  3.3 0.0 copy-start.3
  3.3 0.0 copy-start.2
  3.3 1.8 %shard_map.68 = bf16[784,1024]{1,0:T(8,128)(2,1)} custom-call(s32[5]{0:T(128)S(1)} %stack.19.place_ref, bf16[1536,1024]{1,0:T(8,128)(2,1)S(1)} %copy-done.1), custom_call_target="tpu_custom_call" | custom-call | bytes 3145728 | tf_op jit(solution)/shard_map/pallas_call | solution.py:226
  5.1 3.1 %collective-permute-start = (bf16[784,1024]{1,0:T(8,128)(2,1)}, bf16[784,1024]{1,0:T(8,128)(2,1)}, u32[]{:S(2)}, u32[]{:S(2)}) collective-permute-start(bf16[784,1024]{1,0:T(8,128)(2,1)} %shard_map.68), channel_id=1, source_target_pairs={{0,8},{8,0},{1,9},{9,1},{2,10},{10,2},{3,11},{11,3},{4,12},{12,4},... | collective-permute-start | bytes 4816904 | tf_op jit(solution)/shard_map/ppermute | solution.py:268
  8.2 0.0 copy-done
  8.3 39.8 %all_to_all.20 = bf16[8,16,1024]{2,1,0:T(8,128)(2,1)S(1)} all-to-all(bf16[8,16,1024]{2,1,0:T(8,128)(2,1)S(1)} %broadcast_in_dim.6), channel_id=1, replica_groups=mesh['zh'=4,'zl'=4,'xh'=2,'xl'=2,'y'=4,'c'=2] {'xh','zh'}, dimensions={0} | all-to-all | bytes 524288 | tf_op jit(solution)/shard_map/all_to_all | solution.py:271
  48.1 1.9 %collective-permute-start.1 = (bf16[128,1024]{1,0:T(8,128)(2,1)S(1)}, bf16[128,1024]{1,0:T(8,128)(2,1)S(1)}, u32[]{:S(2)}, u32[]{:S(2)}) collective-permute-start(bf16[128,1024]{1,0:T(8,128)(2,1)S(1)} %bitcast.9), channel_id=1, source_target_pairs={{0,480},{32,0},{64,32},{96,64},{128,96},{160,128},{192,160},{224,1... | collective-permute-start | bytes 786440 | tf_op jit(solution)/shard_map/ppermute | solution.py:250
  50.0 11.2 %collective-permute-start.2 = (bf16[128,1024]{1,0:T(8,128)(2,1)S(1)}, bf16[128,1024]{1,0:T(8,128)(2,1)S(1)}, u32[]{:S(2)}, u32[]{:S(2)}) collective-permute-start(bf16[128,1024]{1,0:T(8,128)(2,1)S(1)} %bitcast.10), channel_id=1, source_target_pairs={{0,448},{32,480},{64,0},{96,32},{128,64},{160,96},{192,128},{224,1... | collective-permute-start | bytes 786440 | tf_op jit(solution)/shard_map/ppermute | solution.py:250
  61.2 2.6 %collective-permute-start.3 = (bf16[128,1024]{1,0:T(8,128)(2,1)S(1)}, bf16[128,1024]{1,0:T(8,128)(2,1)S(1)}, u32[]{:S(2)}, u32[]{:S(2)}) collective-permute-start(bf16[128,1024]{1,0:T(8,128)(2,1)S(1)} %bitcast.11), channel_id=1, source_target_pairs={{0,32},{32,64},{64,96},{96,128},{128,160},{160,192},{192,224},{224... | collective-permute-start | bytes 786440 | tf_op jit(solution)/shard_map/ppermute | solution.py:250
  63.8 0.0 collective-permute-done.1.refs_1_
  63.8 3.4 %collective-permute-done.2.refs_2_ = bf16[128,1024]{1,0:T(8,128)(2,1)S(1)} collective-permute-done((bf16[128,1024]{1,0:T(8,128)(2,1)S(1)}, bf16[128,1024]{1,0:T(8,128)(2,1)S(1)}, u32[]{:S(2)}, u32[]{:S(2)}) %collective-permute-start.2) | collective-permute-done | bytes 262176 | tf_op jit(solution)/shard_map/ppermute | solution.py:250
  67.2 1.4 collective-permute-done.3.refs_3_
  68.6 0.0 collective-permute-done.refs_5_.first_ref
  68.6 6.6 %collective-permute-start.4 = (bf16[784,1024]{1,0:T(8,128)(2,1)}, bf16[784,1024]{1,0:T(8,128)(2,1)S(1)}, u32[]{:S(2)}, u32[]{:S(2)}) collective-permute-start(bf16[784,1024]{1,0:T(8,128)(2,1)} %collective-permute-done.refs_5_.first_ref), channel_id=1, source_target_pairs={{0,1},{1,0},{2,3},{3,2},{4,5},{5,4},{6,7},{7,6},{8,9},{9,8},{10,11... | collective-permute-start | bytes 4816904 | tf_op jit(solution)/shard_map/ppermute | solution.py:274
  75.2 0.0 copy-done.3
  75.2 0.0 copy-start.4
  75.3 0.7 copy-done.4
  76.0 1.5 shard_map.69.refs_4_
  77.5 0.7 slice.3.refs_0_
  78.2 1.5 shard_map.71.refs_4_
  79.7 0.0 copy-done.2
  79.8 2.5 %shard_map.70 = (f32[512,1536]{1,0:T(8,128)S(1)}, f32[2,1536]{1,0:T(2,128)S(1)}) custom-call(bf16[128,1024]{1,0:T(8,128)(2,1)S(1)} %bitcast.12, bf16[128,1024]{1,0:T(8,128)(2,1)S(1)} %collective-permute-done.1.refs_1_, bf16[128,1024]{1,0:T(8,128)(2,1)S(1)} %collective-permute-done.2.refs_2_, bf16[128,1024]{1,0:T(8,128)(2,1)S(1)} %collective-permute-done.3.refs_3_, ...), custom_call_target="tpu_custom_call" | custom-call | flops 1610612736 | bytes 6291456 | tf_op jit(solution)/shard_map/pallas_call | solution.py:226
  82.3 0.0 collective-permute-done.4.refs_6_.second_ref
  82.3 3.9 %shard_map.72 = (f32[512,1536]{1,0:T(8,128)S(1)}, f32[2,1536]{1,0:T(2,128)S(1)}, f32[2,1536]{1,0:T(2,128)S(1)}) custom-call(s32[5]{0:T(128)S(1)} %stack.19.place_ref, f32[2,1536]{1,0:T(2,128)S(1)} %get-tuple-element.22.old_ref.stat_a, bf16[128,1024]{1,0:T(8,128)(2,1)S(1)} %bitcast.13, bf16[128,1024]{1,0:T(8,128)(2,1)S(1)} %collective-permute-done.1.refs_1_, ...), custom_call_target="tpu_custom_call" | custom-call | flops 1610612736 | bytes 6291456 | tf_op jit(solution)/shard_map/pallas_call | solution.py:226
  86.2 0.1 broadcast_in_dim.7
  86.3 11.1 %all_to_all.21.all_ref = f32[16,2,1536]{2,1,0:T(2,128)S(1)} all-to-all(f32[16,2,1536]{2,1,0:T(2,128)S(1)} %broadcast_in_dim.7), channel_id=1, replica_groups=mesh['zh'=4,'zl'=4,'xh'=2,'xl'=2,'y'=4,'c'=2] {'xl','y','c'}, dimensions={0} | all-to-all | bytes 393216 | tf_op jit(solution)/shard_map/all_to_all | solution.py:302
  97.4 3.3 %shard_map.74 = (bf16[128,1152]{1,0:T(8,128)(2,1)S(1)}, bf16[128,1152]{1,0:T(8,128)(2,1)S(1)}) custom-call(s32[5]{0:T(128)S(1)} %stack.19.place_ref, f32[16,2,1536]{2,1,0:T(2,128)S(1)} %all_to_all.21.all_ref, bf16[1536,1024]{1,0:T(8,128)(2,1)S(1)} %copy-done.2, bf16[784,1024]{1,0:T(8,128)(2,1)} %collective-permute-done.refs_5_.first_ref, ...), custom_call_target="tpu_custom_call" | custom-call | flops 1610612736 | bytes 10485760 | tf_op jit(solution)/shard_map/pallas_call | solution.py:226
  100.7 2.7 %collective-permute-start.5 = (bf16[128,1152]{1,0:T(8,128)(2,1)S(1)}, bf16[128,1152]{1,0:T(8,128)(2,1)S(1)}, u32[]{:S(2)}, u32[]{:S(2)}) collective-permute-start(bf16[128,1152]{1,0:T(8,128)(2,1)S(1)} %get-tuple-element.29), channel_id=1, source_target_pairs={{0,32},{32,64},{64,96},{96,128},{128,160},{160,192},{192,224},{224... | collective-permute-start | bytes 884744 | tf_op jit(solution)/shard_map/ppermute | solution.py:250
  103.4 4.9 %collective-permute-start.6 = (bf16[128,1152]{1,0:T(8,128)(2,1)S(1)}, bf16[128,1152]{1,0:T(8,128)(2,1)S(1)}, u32[]{:S(2)}, u32[]{:S(2)}) collective-permute-start(bf16[128,1152]{1,0:T(8,128)(2,1)S(1)} %get-tuple-element.30), channel_id=1, source_target_pairs={{0,64},{32,96},{64,128},{96,160},{128,192},{160,224},{192,256},{22... | collective-permute-start | bytes 884744 | tf_op jit(solution)/shard_map/ppermute | solution.py:250
  108.3 3.3 %shard_map.73 = (bf16[128,1152]{1,0:T(8,128)(2,1)S(1)}, bf16[128,1152]{1,0:T(8,128)(2,1)S(1)}) custom-call(s32[5]{0:T(128)S(1)} %stack.19.place_ref, f32[16,2,1536]{2,1,0:T(2,128)S(1)} %all_to_all.21.all_ref, bf16[1536,1024]{1,0:T(8,128)(2,1)S(1)} %copy-done.2, bf16[784,1024]{1,0:T(8,128)(2,1)} %collective-permute-done.refs_5_.first_ref, ...), custom_call_target="tpu_custom_call" | custom-call | flops 1610612736 | bytes 10485760 | tf_op jit(solution)/shard_map/pallas_call | solution.py:226
  111.6 1.9 %collective-permute-start.7 = (bf16[128,1152]{1,0:T(8,128)(2,1)S(1)}, bf16[128,1152]{1,0:T(8,128)(2,1)S(1)}, u32[]{:S(2)}, u32[]{:S(2)}) collective-permute-start(bf16[128,1152]{1,0:T(8,128)(2,1)S(1)} %get-tuple-element.31), channel_id=1, source_target_pairs={{0,480},{32,0},{64,32},{96,64},{128,96},{160,128},{192,160},{224,1... | collective-permute-start | bytes 884744 | tf_op jit(solution)/shard_map/ppermute | solution.py:250
  113.6 0.0 collective-permute-done.5.b
  113.6 13.6 %collective-permute-done.6.c = bf16[128,1152]{1,0:T(8,128)(2,1)S(1)} collective-permute-done((bf16[128,1152]{1,0:T(8,128)(2,1)S(1)}, bf16[128,1152]{1,0:T(8,128)(2,1)S(1)}, u32[]{:S(2)}, u32[]{:S(2)}) %collective-permute-start.6) | collective-permute-done | bytes 294944 | tf_op jit(solution)/shard_map/ppermute | solution.py:250
  127.1 0.0 collective-permute-done.7.d
  127.1 0.3 shard_map.75
  127.4 30.3 %all_to_all.22.ref = bf16[8,16,1152]{2,1,0:T(8,128)(2,1)S(1)} all-to-all(bf16[8,16,1152]{2,1,0:T(8,128)(2,1)S(1)} %bitcast.8), channel_id=1, replica_groups=mesh['zh'=4,'zl'=4,'xh'=2,'xl'=2,'y'=4,'c'=2] {'xh','zh'}, dimensions={0} | all-to-all | bytes 589824 | tf_op jit(solution)/shard_map/all_to_all | solution.py:319
  157.8 0.2 shard_map.76
  157.9 13.0 %all_to_all.23.ref = bf16[8,16,1152]{2,1,0:T(8,128)(2,1)S(1)} all-to-all(bf16[8,16,1152]{2,1,0:T(8,128)(2,1)S(1)} %shard_map.76), channel_id=1, replica_groups=mesh['zh'=4,'zl'=4,'xh'=2,'xl'=2,'y'=4,'c'=2] {'y','c'}, dimensions={0} | all-to-all | bytes 589824 | tf_op jit(solution)/shard_map/all_to_all | solution.py:321
  170.9 0.8 shard_map.77
  (2 shorter events, 0.0 us)
Async XLA Ops:
  0.6 7.6 %copy-start = (bf16[128,1024]{1,0:T(8,128)(2,1)S(1)}, bf16[128,1024]{1,0:T(8,128)(2,1)}, u32[]{:S(2)}) copy-start(bf16[128,1024]{1,0:T(8,128)(2,1)} %param.9) | copy-start | bytes 786436
  1.4 1.9 %copy-start.1 = (bf16[1536,1024]{1,0:T(8,128)(2,1)S(1)}, bf16[1536,1024]{1,0:T(8,128)(2,1)}, u32[]{:S(2)}) copy-start(bf16[1536,1024]{1,0:T(8,128)(2,1)} %points_ref.5) | copy-start | bytes 9437188
  3.3 71.9 %copy-start.3 = (s32[16,2048]{1,0:T(8,128)S(1)}, s32[16,2048]{1,0:T(8,128)}, u32[]{:S(2)}) copy-start(s32[16,2048]{1,0:T(8,128)} %lists_ref.3) | copy-start | bytes 393220
  3.3 76.4 %copy-start.2 = (bf16[1536,1024]{1,0:T(8,128)(2,1)S(1)}, bf16[1536,1024]{1,0:T(8,128)(2,1)}, u32[]{:S(2)}) copy-start(bf16[1536,1024]{1,0:T(8,128)(2,1)} %points_ref.5) | copy-start | bytes 9437188
  5.1 63.5 %collective-permute-start = (bf16[784,1024]{1,0:T(8,128)(2,1)}, bf16[784,1024]{1,0:T(8,128)(2,1)}, u32[]{:S(2)}, u32[]{:S(2)}) collective-permute-start(bf16[784,1024]{1,0:T(8,128)(2,1)} %shard_map.68), channel_id=1, source_target_pairs={{0,8},{8,0},{1,9},{9,1},{2,10},{10,2},{3,11},{11,3},{4,12},{12,4},... | collective-permute-start | bytes 4816904 | tf_op jit(solution)/shard_map/ppermute | solution.py:268
  48.1 15.7 %collective-permute-start.1 = (bf16[128,1024]{1,0:T(8,128)(2,1)S(1)}, bf16[128,1024]{1,0:T(8,128)(2,1)S(1)}, u32[]{:S(2)}, u32[]{:S(2)}) collective-permute-start(bf16[128,1024]{1,0:T(8,128)(2,1)S(1)} %bitcast.9), channel_id=1, source_target_pairs={{0,480},{32,0},{64,32},{96,64},{128,96},{160,128},{192,160},{224,1... | collective-permute-start | bytes 786440 | tf_op jit(solution)/shard_map/ppermute | solution.py:250
  50.0 17.2 %collective-permute-start.2 = (bf16[128,1024]{1,0:T(8,128)(2,1)S(1)}, bf16[128,1024]{1,0:T(8,128)(2,1)S(1)}, u32[]{:S(2)}, u32[]{:S(2)}) collective-permute-start(bf16[128,1024]{1,0:T(8,128)(2,1)S(1)} %bitcast.10), channel_id=1, source_target_pairs={{0,448},{32,480},{64,0},{96,32},{128,64},{160,96},{192,128},{224,1... | collective-permute-start | bytes 786440 | tf_op jit(solution)/shard_map/ppermute | solution.py:250
  61.2 7.4 %collective-permute-start.3 = (bf16[128,1024]{1,0:T(8,128)(2,1)S(1)}, bf16[128,1024]{1,0:T(8,128)(2,1)S(1)}, u32[]{:S(2)}, u32[]{:S(2)}) collective-permute-start(bf16[128,1024]{1,0:T(8,128)(2,1)S(1)} %bitcast.11), channel_id=1, source_target_pairs={{0,32},{32,64},{64,96},{96,128},{128,160},{160,192},{192,224},{224... | collective-permute-start | bytes 786440 | tf_op jit(solution)/shard_map/ppermute | solution.py:250
  68.6 13.7 %collective-permute-start.4 = (bf16[784,1024]{1,0:T(8,128)(2,1)}, bf16[784,1024]{1,0:T(8,128)(2,1)S(1)}, u32[]{:S(2)}, u32[]{:S(2)}) collective-permute-start(bf16[784,1024]{1,0:T(8,128)(2,1)} %collective-permute-done.refs_5_.first_ref), channel_id=1, source_target_pairs={{0,1},{1,0},{2,3},{3,2},{4,5},{5,4},{6,7},{7,6},{8,9},{9,8},{10,11... | collective-permute-start | bytes 4816904 | tf_op jit(solution)/shard_map/ppermute | solution.py:274
  75.2 0.8 copy-start.4
  100.7 12.9 %collective-permute-start.5 = (bf16[128,1152]{1,0:T(8,128)(2,1)S(1)}, bf16[128,1152]{1,0:T(8,128)(2,1)S(1)}, u32[]{:S(2)}, u32[]{:S(2)}) collective-permute-start(bf16[128,1152]{1,0:T(8,128)(2,1)S(1)} %get-tuple-element.29), channel_id=1, source_target_pairs={{0,32},{32,64},{64,96},{96,128},{128,160},{160,192},{192,224},{224... | collective-permute-start | bytes 884744 | tf_op jit(solution)/shard_map/ppermute | solution.py:250
  103.4 23.7 %collective-permute-start.6 = (bf16[128,1152]{1,0:T(8,128)(2,1)S(1)}, bf16[128,1152]{1,0:T(8,128)(2,1)S(1)}, u32[]{:S(2)}, u32[]{:S(2)}) collective-permute-start(bf16[128,1152]{1,0:T(8,128)(2,1)S(1)} %get-tuple-element.30), channel_id=1, source_target_pairs={{0,64},{32,96},{64,128},{96,160},{128,192},{160,224},{192,256},{22... | collective-permute-start | bytes 884744 | tf_op jit(solution)/shard_map/ppermute | solution.py:250
  111.6 15.5 %collective-permute-start.7 = (bf16[128,1152]{1,0:T(8,128)(2,1)S(1)}, bf16[128,1152]{1,0:T(8,128)(2,1)S(1)}, u32[]{:S(2)}, u32[]{:S(2)}) collective-permute-start(bf16[128,1152]{1,0:T(8,128)(2,1)S(1)} %get-tuple-element.31), channel_id=1, source_target_pairs={{0,480},{32,0},{64,32},{96,64},{128,96},{160,128},{192,160},{224,1... | collective-permute-start | bytes 884744 | tf_op jit(solution)/shard_map/ppermute | solution.py:250

commit v7 on v6

--- a/solution.py
+++ b/solution.py
@@ -27,7 +27,7 @@
 
 def mask_kernel(place_ref, lists_ref, owner_ref, *refs):
     *other, mask_ref = refs
-    n, me, zl = place_ref[1], place_ref[2], place_ref[4]
+    n, zl, x = place_ref[1], place_ref[4], place_ref[5]
     count = lists_ref.shape[1]
     blocks = owner_ref.shape[0]
     in_block = lax.broadcasted_iota(i32, (lane, count), 0)
@@ -51,7 +51,7 @@
     owner = pick(rows >> 7)
     inner = pick(rows & 127)
     row = ((owner >> 1) & 1) * 64 + (owner >> 4) * 16 + (inner & 15)
-    mine = ((inner >> 4) == n) & ((owner & 1) == me)
+    mine = ((inner >> 4) == n) & (((owner & 3) == x) | ((owner & 3) == 3 - x))
     block = jnp.where(mine, ((owner >> 2) - zl) & 3, lane)
     left = (in_block == row).astype(bf16)
     right = (in_block == block).astype(bf16)
@@ -235,8 +235,10 @@
 
 
 def shards(points, coarse_ids, lists, owner_map, centroids):
-    narrow, deep, far = ("y", "c"), ("zh", "zl"), ("xh", "zh")
-    parts, zs, peers = (lax.axis_size(a) for a in (narrow, deep, far))
+    narrow, deep, far = ("y", "c"), ("zh", "zl"), ("zh", "xh", "xl")
+    parts, zs = lax.axis_size(narrow), lax.axis_size(deep)
+    teams = [[4 * zh + x for x in pair for zh in range(4)] for pair in ((0, 3), (1, 2))]
+    peers = len(teams[0])
     n = lax.axis_index(narrow)
     count, width = points.shape
     rows = centroids.shape[0] // parts
@@ -249,9 +251,11 @@
     def along(a, by):
         return lax.ppermute(a, deep, [(i, (i + by) % zs) for i in range(zs)])
 
-    place = jnp.stack(
-        [coarse_ids[0], n, lax.axis_index("xl"), lax.axis_index("c"), lax.axis_index("zl")]
-    ).astype(i32)
+    def team_exchange(a):
+        return lax.all_to_all(a, far, 0, 0, axis_index_groups=teams, tiled=True)
+
+    where = [lax.axis_index(a) for a in ("xl", "c", "zl", ("xh", "xl"))]
+    place = jnp.stack([coarse_ids[0], n, *where]).astype(i32)
     half = call(
         cut_kernel,
         sds((count // 2 + 16, width), bf16),
@@ -268,10 +272,8 @@
     first = lax.ppermute(half, "xl", swap)
     own = lax.dynamic_slice(centroids, (n * rows, 0), (rows, width))
     copies = jnp.broadcast_to(own, (peers, rows, width))
-    group = lax.all_to_all(copies, far, 0, 0, tiled=True).reshape(size, width)
+    group = team_exchange(copies).reshape(size, width)
     pieces = [group] + [along(group, -d) for d in near[1:]]
-    first, *pieces = lax.optimization_barrier((first, *pieces))
-    second = lax.ppermute(first, "c", swap)
     flops = 2 * len(near) * size * count * width
     stat = sds((2, count), f32)
     expo = sds((len(near) * size, count), f32)
@@ -285,8 +287,10 @@
             moved=8 << 20,
         )
 
+    first, mask, *pieces = lax.optimization_barrier((first, listed(), *pieces))
+    second = lax.ppermute(first, "c", swap)
     expo_a, stat_a = call(
-        score_kernel, (expo, stat), (*pieces, listed(), points), flops=flops, moved=6 << 20
+        score_kernel, (expo, stat), (*pieces, mask, points), flops=flops, moved=6 << 20
     )
     mask = listed(first[count // 2 :, :lane])
     expo_b, stat_b, both = call(
@@ -316,7 +320,7 @@
     three, kept = sums(3, 0)
     got = [kept, along(one, near[1]), along(two, near[2]), along(three, near[3])]
     summed = call(near_kernel, sds((size, padded), bf16), tuple(got))
-    got = lax.all_to_all(summed.reshape(peers, rows, padded), far, 0, 0, tiled=True)
+    got = team_exchange(summed.reshape(peers, rows, padded))
     table = call(last_kernel, sds((parts, rows, padded), bf16), (got, own))
     whole = lax.all_to_all(table, narrow, 0, 0, tiled=True)
     new_table, masses = call(

time: 172 us -> 157 us (0.913)
  the two profiles are of different devices: /device:TPU:33 before, /device:TPU:1 now
where the time goes in v7:
time: 157 us; the launch traced here: 154 us
  blocking collectives  82.5 us (53%)
  starting transfers between devices  33 us (21%)
  Pallas kernels  19.2 us (12%)
  waiting for transfers between devices  14.3 us (9%)
  local copies, waits for them, and re-layouts  3.51 us (2%)
    all_to_all x2, blocking collectives, team_exchange(): return lax.all_to_all(a, far, 0, 0, axis_index_groups=teams, tiled=True)  56.2 us
    ppermute x6, starting transfers between devices, along(): return lax.ppermute(a, deep, [(i, (i + by) % zs) for i in range(zs)])  23.5 us
    pallas_call x10, Pallas kernels, call(): pl.pallas_call(kernel, out_shape=outs, in_specs=specs or vmem(len(args)),...  19.2 us
    all_to_all x1, blocking collectives, shards(): whole = lax.all_to_all(table, narrow, 0, 0, tiled=True)  15.2 us
    ppermute x6, waiting for transfers between devices, along(): return lax.ppermute(a, deep, [(i, (i + by) % zs) for i in range(zs)])  14.3 us
    all_to_all x1, blocking collectives, shards(): shared = lax.all_to_all(copies, pool, 0, 0, tiled=True)  11.1 us
    ppermute x1, starting transfers between devices, shards(): second = lax.ppermute(first, 'c', swap)  5.55 us
    ppermute x1, starting transfers between devices, shards(): first = lax.ppermute(half, 'xl', swap)  3.95 us
  transfers between devices with their start and end apart: 8, of which 3 were waited for; matrix products, arithmetic and copies ran while one was open for 0% of the time, Pallas kernels for 6%

profile of v7, /device:TPU:1, one launch (start us, length us, event | category | flops | bytes accessed | tf_op | source)
XLA Modules:
  0.0 154.0 jit_solution(14498145347623880990)
XLA Ops:
  0.6 0.0 copy-start
  1.3 0.1 stack.23.place_ref
  1.4 0.0 copy-start.1
  1.4 1.9 %copy-done.1 = bf16[1536,1024]{1,0:T(8,128)(2,1)S(1)} copy-done((bf16[1536,1024]{1,0:T(8,128)(2,1)S(1)}, bf16[1536,1024]{1,0:T(8,128)(2,1)}, u32[]{:S(2)}) %copy-start.1) | copy-done | bytes 3145752
  3.3 0.0 copy-start.3
  3.3 0.0 copy-start.2
  3.3 1.8 %shard_map.68 = bf16[784,1024]{1,0:T(8,128)(2,1)} custom-call(s32[6]{0:T(128)S(1)} %stack.23.place_ref, bf16[1536,1024]{1,0:T(8,128)(2,1)S(1)} %copy-done.1), custom_call_target="tpu_custom_call" | custom-call | bytes 3145728 | tf_op jit(solution)/shard_map/pallas_call | solution.py:226
  5.1 4.0 %collective-permute-start = (bf16[784,1024]{1,0:T(8,128)(2,1)}, bf16[784,1024]{1,0:T(8,128)(2,1)}, u32[]{:S(2)}, u32[]{:S(2)}) collective-permute-start(bf16[784,1024]{1,0:T(8,128)(2,1)} %shard_map.68), channel_id=1, source_target_pairs={{0,8},{8,0},{1,9},{9,1},{2,10},{10,2},{3,11},{11,3},{4,12},{12,4},... | collective-permute-start | bytes 4816904 | tf_op jit(solution)/shard_map/ppermute | solution.py:272
  9.0 0.0 copy-done
  9.1 30.8 %all_to_all.20 = bf16[8,16,1024]{2,1,0:T(8,128)(2,1)S(1)} all-to-all(bf16[8,16,1024]{2,1,0:T(8,128)(2,1)S(1)} %broadcast_in_dim.6), channel_id=1, replica_groups={{0,128,256,384,24,152,280,408},{8,136,264,392,16,144,272,400},{1,129,25..., dimensions={0} | all-to-all | bytes 524288 | tf_op jit(solution)/shard_map/all_to_all | solution.py:255
  39.9 3.2 %collective-permute-start.1 = (bf16[128,1024]{1,0:T(8,128)(2,1)S(1)}, bf16[128,1024]{1,0:T(8,128)(2,1)S(1)}, u32[]{:S(2)}, u32[]{:S(2)}) collective-permute-start(bf16[128,1024]{1,0:T(8,128)(2,1)S(1)} %bitcast.10), channel_id=1, source_target_pairs={{0,480},{32,0},{64,32},{96,64},{128,96},{160,128},{192,160},{224,1... | collective-permute-start | bytes 786440 | tf_op jit(solution)/shard_map/ppermute | solution.py:252
  43.1 7.8 %collective-permute-start.2 = (bf16[128,1024]{1,0:T(8,128)(2,1)S(1)}, bf16[128,1024]{1,0:T(8,128)(2,1)S(1)}, u32[]{:S(2)}, u32[]{:S(2)}) collective-permute-start(bf16[128,1024]{1,0:T(8,128)(2,1)S(1)} %bitcast.11), channel_id=1, source_target_pairs={{0,448},{32,480},{64,0},{96,32},{128,64},{160,96},{192,128},{224,1... | collective-permute-start | bytes 786440 | tf_op jit(solution)/shard_map/ppermute | solution.py:252
  51.0 3.4 %collective-permute-start.3 = (bf16[128,1024]{1,0:T(8,128)(2,1)S(1)}, bf16[128,1024]{1,0:T(8,128)(2,1)S(1)}, u32[]{:S(2)}, u32[]{:S(2)}) collective-permute-start(bf16[128,1024]{1,0:T(8,128)(2,1)S(1)} %bitcast.12), channel_id=1, source_target_pairs={{0,32},{32,64},{64,96},{96,128},{128,160},{160,192},{192,224},{224... | collective-permute-start | bytes 786440 | tf_op jit(solution)/shard_map/ppermute | solution.py:252
  54.3 0.0 copy-done.3
  54.3 0.0 copy-start.4
  54.4 0.7 copy-done.4
  55.1 1.5 shard_map.69.refs_4_
  56.6 0.0 collective-permute-done.1.refs_1_
  56.6 8.2 %collective-permute-done.2.refs_2_ = bf16[128,1024]{1,0:T(8,128)(2,1)S(1)} collective-permute-done((bf16[128,1024]{1,0:T(8,128)(2,1)S(1)}, bf16[128,1024]{1,0:T(8,128)(2,1)S(1)}, u32[]{:S(2)}, u32[]{:S(2)}) %collective-permute-start.2) | collective-permute-done | bytes 262176 | tf_op jit(solution)/shard_map/ppermute | solution.py:252
  64.8 0.0 collective-permute-done.3.refs_3_
  64.8 0.0 collective-permute-done.refs_5_.first_ref
  64.8 5.5 %collective-permute-start.4 = (bf16[784,1024]{1,0:T(8,128)(2,1)}, bf16[784,1024]{1,0:T(8,128)(2,1)S(1)}, u32[]{:S(2)}, u32[]{:S(2)}) collective-permute-start(bf16[784,1024]{1,0:T(8,128)(2,1)} %collective-permute-done.refs_5_.first_ref), channel_id=1, source_target_pairs={{0,1},{1,0},{2,3},{3,2},{4,5},{5,4},{6,7},{7,6},{8,9},{9,8},{10,11... | collective-permute-start | bytes 4816904 | tf_op jit(solution)/shard_map/ppermute | solution.py:291
  70.4 0.7 slice.3.refs_0_
  71.1 1.5 shard_map.71.refs_4_
  72.6 0.0 copy-done.2
  72.6 2.5 %shard_map.70 = (f32[512,1536]{1,0:T(8,128)S(1)}, f32[2,1536]{1,0:T(2,128)S(1)}) custom-call(bf16[128,1024]{1,0:T(8,128)(2,1)S(1)} %bitcast.13, bf16[128,1024]{1,0:T(8,128)(2,1)S(1)} %collective-permute-done.1.refs_1_, bf16[128,1024]{1,0:T(8,128)(2,1)S(1)} %collective-permute-done.2.refs_2_, bf16[128,1024]{1,0:T(8,128)(2,1)S(1)} %collective-permute-done.3.refs_3_, ...), custom_call_target="tpu_custom_call" | custom-call | flops 1610612736 | bytes 6291456 | tf_op jit(solution)/shard_map/pallas_call | solution.py:226
  75.1 0.0 collective-permute-done.4.refs_6_.second_ref
  75.1 3.9 %shard_map.72 = (f32[512,1536]{1,0:T(8,128)S(1)}, f32[2,1536]{1,0:T(2,128)S(1)}, f32[2,1536]{1,0:T(2,128)S(1)}) custom-call(s32[6]{0:T(128)S(1)} %stack.23.place_ref, f32[2,1536]{1,0:T(2,128)S(1)} %get-tuple-element.24.old_ref.stat_a, bf16[128,1024]{1,0:T(8,128)(2,1)S(1)} %bitcast.14, bf16[128,1024]{1,0:T(8,128)(2,1)S(1)} %collective-permute-done.1.refs_1_, ...), custom_call_target="tpu_custom_call" | custom-call | flops 1610612736 | bytes 6291456 | tf_op jit(solution)/shard_map/pallas_call | solution.py:226
  79.0 0.1 broadcast_in_dim.7
  79.1 11.1 %all_to_all.21.all_ref = f32[16,2,1536]{2,1,0:T(2,128)S(1)} all-to-all(f32[16,2,1536]{2,1,0:T(2,128)S(1)} %broadcast_in_dim.7), channel_id=1, replica_groups=mesh['zh'=4,'zl'=4,'xh'=2,'xl'=2,'y'=4,'c'=2] {'xl','y','c'}, dimensions={0} | all-to-all | bytes 393216 | tf_op jit(solution)/shard_map/all_to_all | solution.py:306
  90.2 3.3 %shard_map.74 = (bf16[128,1152]{1,0:T(8,128)(2,1)S(1)}, bf16[128,1152]{1,0:T(8,128)(2,1)S(1)}) custom-call(s32[6]{0:T(128)S(1)} %stack.23.place_ref, f32[16,2,1536]{2,1,0:T(2,128)S(1)} %all_to_all.21.all_ref, bf16[1536,1024]{1,0:T(8,128)(2,1)S(1)} %copy-done.2, bf16[784,1024]{1,0:T(8,128)(2,1)} %collective-permute-done.refs_5_.first_ref, ...), custom_call_target="tpu_custom_call" | custom-call | flops 1610612736 | bytes 10485760 | tf_op jit(solution)/shard_map/pallas_call | solution.py:226
  93.5 2.9 %collective-permute-start.5 = (bf16[128,1152]{1,0:T(8,128)(2,1)S(1)}, bf16[128,1152]{1,0:T(8,128)(2,1)S(1)}, u32[]{:S(2)}, u32[]{:S(2)}) collective-permute-start(bf16[128,1152]{1,0:T(8,128)(2,1)S(1)} %get-tuple-element.31), channel_id=1, source_target_pairs={{0,32},{32,64},{64,96},{96,128},{128,160},{160,192},{192,224},{224... | collective-permute-start | bytes 884744 | tf_op jit(solution)/shard_map/ppermute | solution.py:252
  96.4 1.9 %collective-permute-start.6 = (bf16[128,1152]{1,0:T(8,128)(2,1)S(1)}, bf16[128,1152]{1,0:T(8,128)(2,1)S(1)}, u32[]{:S(2)}, u32[]{:S(2)}) collective-permute-start(bf16[128,1152]{1,0:T(8,128)(2,1)S(1)} %get-tuple-element.32), channel_id=1, source_target_pairs={{0,64},{32,96},{64,128},{96,160},{128,192},{160,224},{192,256},{22... | collective-permute-start | bytes 884744 | tf_op jit(solution)/shard_map/ppermute | solution.py:252
  98.3 3.3 %shard_map.73 = (bf16[128,1152]{1,0:T(8,128)(2,1)S(1)}, bf16[128,1152]{1,0:T(8,128)(2,1)S(1)}) custom-call(s32[6]{0:T(128)S(1)} %stack.23.place_ref, f32[16,2,1536]{2,1,0:T(2,128)S(1)} %all_to_all.21.all_ref, bf16[1536,1024]{1,0:T(8,128)(2,1)S(1)} %copy-done.2, bf16[784,1024]{1,0:T(8,128)(2,1)} %collective-permute-done.refs_5_.first_ref, ...), custom_call_target="tpu_custom_call" | custom-call | flops 1610612736 | bytes 10485760 | tf_op jit(solution)/shard_map/pallas_call | solution.py:226
  101.7 4.3 %collective-permute-start.7 = (bf16[128,1152]{1,0:T(8,128)(2,1)S(1)}, bf16[128,1152]{1,0:T(8,128)(2,1)S(1)}, u32[]{:S(2)}, u32[]{:S(2)}) collective-permute-start(bf16[128,1152]{1,0:T(8,128)(2,1)S(1)} %get-tuple-element.33), channel_id=1, source_target_pairs={{0,480},{32,0},{64,32},{96,64},{128,96},{160,128},{192,160},{224,1... | collective-permute-start | bytes 884744 | tf_op jit(solution)/shard_map/ppermute | solution.py:252
  106.0 0.0 collective-permute-done.5.b
  106.0 3.8 %collective-permute-done.6.c = bf16[128,1152]{1,0:T(8,128)(2,1)S(1)} collective-permute-done((bf16[128,1152]{1,0:T(8,128)(2,1)S(1)}, bf16[128,1152]{1,0:T(8,128)(2,1)S(1)}, u32[]{:S(2)}, u32[]{:S(2)}) %collective-permute-start.6) | collective-permute-done | bytes 294944 | tf_op jit(solution)/shard_map/ppermute | solution.py:252
  109.8 2.2 %collective-permute-done.7.d = bf16[128,1152]{1,0:T(8,128)(2,1)S(1)} collective-permute-done((bf16[128,1152]{1,0:T(8,128)(2,1)S(1)}, bf16[128,1152]{1,0:T(8,128)(2,1)S(1)}, u32[]{:S(2)}, u32[]{:S(2)}) %collective-permute-start.7) | collective-permute-done | bytes 294944 | tf_op jit(solution)/shard_map/ppermute | solution.py:252
  112.1 0.3 shard_map.75
  112.4 25.4 %all_to_all.22.ref = bf16[8,16,1152]{2,1,0:T(8,128)(2,1)S(1)} all-to-all(bf16[8,16,1152]{2,1,0:T(8,128)(2,1)S(1)} %bitcast.9), channel_id=1, replica_groups={{0,128,256,384,24,152,280,408},{8,136,264,392,16,144,272,400},{1,129,25..., dimensions={0} | all-to-all | bytes 589824 | tf_op jit(solution)/shard_map/all_to_all | solution.py:255
  137.8 0.2 shard_map.76
  138.0 15.2 %all_to_all.23.ref = bf16[8,16,1152]{2,1,0:T(8,128)(2,1)S(1)} all-to-all(bf16[8,16,1152]{2,1,0:T(8,128)(2,1)S(1)} %shard_map.76), channel_id=1, replica_groups=mesh['zh'=4,'zl'=4,'xh'=2,'xl'=2,'y'=4,'c'=2] {'y','c'}, dimensions={0} | all-to-all | bytes 589824 | tf_op jit(solution)/shard_map/all_to_all | solution.py:325
  153.2 0.8 shard_map.77
  (2 shorter events, 0.0 us)
Async XLA Ops:
  0.6 8.4 %copy-start = (bf16[128,1024]{1,0:T(8,128)(2,1)S(1)}, bf16[128,1024]{1,0:T(8,128)(2,1)}, u32[]{:S(2)}) copy-start(bf16[128,1024]{1,0:T(8,128)(2,1)} %param.9) | copy-start | bytes 786436
  1.4 1.9 %copy-start.1 = (bf16[1536,1024]{1,0:T(8,128)(2,1)S(1)}, bf16[1536,1024]{1,0:T(8,128)(2,1)}, u32[]{:S(2)}) copy-start(bf16[1536,1024]{1,0:T(8,128)(2,1)} %points_ref.5) | copy-start | bytes 9437188
  3.3 51.0 %copy-start.3 = (s32[16,2048]{1,0:T(8,128)S(1)}, s32[16,2048]{1,0:T(8,128)}, u32[]{:S(2)}) copy-start(s32[16,2048]{1,0:T(8,128)} %lists_ref.3) | copy-start | bytes 393220
  3.3 69.3 %copy-start.2 = (bf16[1536,1024]{1,0:T(8,128)(2,1)S(1)}, bf16[1536,1024]{1,0:T(8,128)(2,1)}, u32[]{:S(2)}) copy-start(bf16[1536,1024]{1,0:T(8,128)(2,1)} %points_ref.5) | copy-start | bytes 9437188
  5.1 59.7 %collective-permute-start = (bf16[784,1024]{1,0:T(8,128)(2,1)}, bf16[784,1024]{1,0:T(8,128)(2,1)}, u32[]{:S(2)}, u32[]{:S(2)}) collective-permute-start(bf16[784,1024]{1,0:T(8,128)(2,1)} %shard_map.68), channel_id=1, source_target_pairs={{0,8},{8,0},{1,9},{9,1},{2,10},{10,2},{3,11},{11,3},{4,12},{12,4},... | collective-permute-start | bytes 4816904 | tf_op jit(solution)/shard_map/ppermute | solution.py:272
  39.9 16.7 %collective-permute-start.1 = (bf16[128,1024]{1,0:T(8,128)(2,1)S(1)}, bf16[128,1024]{1,0:T(8,128)(2,1)S(1)}, u32[]{:S(2)}, u32[]{:S(2)}) collective-permute-start(bf16[128,1024]{1,0:T(8,128)(2,1)S(1)} %bitcast.10), channel_id=1, source_target_pairs={{0,480},{32,0},{64,32},{96,64},{128,96},{160,128},{192,160},{224,1... | collective-permute-start | bytes 786440 | tf_op jit(solution)/shard_map/ppermute | solution.py:252
  43.1 21.7 %collective-permute-start.2 = (bf16[128,1024]{1,0:T(8,128)(2,1)S(1)}, bf16[128,1024]{1,0:T(8,128)(2,1)S(1)}, u32[]{:S(2)}, u32[]{:S(2)}) collective-permute-start(bf16[128,1024]{1,0:T(8,128)(2,1)S(1)} %bitcast.11), channel_id=1, source_target_pairs={{0,448},{32,480},{64,0},{96,32},{128,64},{160,96},{192,128},{224,1... | collective-permute-start | bytes 786440 | tf_op jit(solution)/shard_map/ppermute | solution.py:252
  51.0 13.8 %collective-permute-start.3 = (bf16[128,1024]{1,0:T(8,128)(2,1)S(1)}, bf16[128,1024]{1,0:T(8,128)(2,1)S(1)}, u32[]{:S(2)}, u32[]{:S(2)}) collective-permute-start(bf16[128,1024]{1,0:T(8,128)(2,1)S(1)} %bitcast.12), channel_id=1, source_target_pairs={{0,32},{32,64},{64,96},{96,128},{128,160},{160,192},{192,224},{224... | collective-permute-start | bytes 786440 | tf_op jit(solution)/shard_map/ppermute | solution.py:252
  54.3 0.8 copy-start.4
  64.8 10.3 %collective-permute-start.4 = (bf16[784,1024]{1,0:T(8,128)(2,1)}, bf16[784,1024]{1,0:T(8,128)(2,1)S(1)}, u32[]{:S(2)}, u32[]{:S(2)}) collective-permute-start(bf16[784,1024]{1,0:T(8,128)(2,1)} %collective-permute-done.refs_5_.first_ref), channel_id=1, source_target_pairs={{0,1},{1,0},{2,3},{3,2},{4,5},{5,4},{6,7},{7,6},{8,9},{9,8},{10,11... | collective-permute-start | bytes 4816904 | tf_op jit(solution)/shard_map/ppermute | solution.py:291
  93.5 12.5 %collective-permute-start.5 = (bf16[128,1152]{1,0:T(8,128)(2,1)S(1)}, bf16[128,1152]{1,0:T(8,128)(2,1)S(1)}, u32[]{:S(2)}, u32[]{:S(2)}) collective-permute-start(bf16[128,1152]{1,0:T(8,128)(2,1)S(1)} %get-tuple-element.31), channel_id=1, source_target_pairs={{0,32},{32,64},{64,96},{96,128},{128,160},{160,192},{192,224},{224... | collective-permute-start | bytes 884744 | tf_op jit(solution)/shard_map/ppermute | solution.py:252
  96.4 13.4 %collective-permute-start.6 = (bf16[128,1152]{1,0:T(8,128)(2,1)S(1)}, bf16[128,1152]{1,0:T(8,128)(2,1)S(1)}, u32[]{:S(2)}, u32[]{:S(2)}) collective-permute-start(bf16[128,1152]{1,0:T(8,128)(2,1)S(1)} %get-tuple-element.32), channel_id=1, source_target_pairs={{0,64},{32,96},{64,128},{96,160},{128,192},{160,224},{192,256},{22... | collective-permute-start | bytes 884744 | tf_op jit(solution)/shard_map/ppermute | solution.py:252
  101.7 10.4 %collective-permute-start.7 = (bf16[128,1152]{1,0:T(8,128)(2,1)S(1)}, bf16[128,1152]{1,0:T(8,128)(2,1)S(1)}, u32[]{:S(2)}, u32[]{:S(2)}) collective-permute-start(bf16[128,1152]{1,0:T(8,128)(2,1)S(1)} %get-tuple-element.33), channel_id=1, source_target_pairs={{0,480},{32,0},{64,32},{96,64},{128,96},{160,128},{192,160},{224,1... | collective-permute-start | bytes 884744 | tf_op jit(solution)/shard_map/ppermute | solution.py:252

commit v8 on v7

--- a/solution.py
+++ b/solution.py
@@ -141,10 +141,9 @@
     stat_a,
     expo_b,
     stat_b,
-    one_ref,
-    two_ref,
-    norm_ref,
+    *refs,
 ):
+    *out_refs, norm_ref = refs
     me, core = place_ref[2], place_ref[3]
     half = points_ref.shape[0] // 2
     width = points_ref.shape[1]
@@ -172,12 +171,12 @@
             more = jnp.dot(part, ref[: part.shape[1], at], preferred_element_type=f32)
             total = more if total is None else total + more
         total = total.astype(bf16)
-        one_ref[:, at] = total[:lane]
-        two_ref[:, at] = total[lane:]
+        for k, out_ref in enumerate(out_refs):
+            out_ref[:, at] = total[k * lane : (k + 1) * lane]
     mass = sum(jnp.sum(part.astype(f32), axis=1, keepdims=True) for part in parts)
     tail = halves(mass)
-    one_ref[:, width:] = tail[:lane]
-    two_ref[:, width:] = tail[lane:]
+    for k, out_ref in enumerate(out_refs):
+        out_ref[:, width:] = tail[k * lane : (k + 1) * lane]
 
 
 def added(pieces, width):
@@ -273,6 +272,8 @@
     own = lax.dynamic_slice(centroids, (n * rows, 0), (rows, width))
     copies = jnp.broadcast_to(own, (peers, rows, width))
     group = team_exchange(copies).reshape(size, width)
+    first, group = lax.optimization_barrier((first, group))
+    second = lax.ppermute(first, "c", swap)
     pieces = [group] + [along(group, -d) for d in near[1:]]
     flops = 2 * len(near) * size * count * width
     stat = sds((2, count), f32)
@@ -287,8 +288,7 @@
             moved=8 << 20,
         )
 
-    first, mask, *pieces = lax.optimization_barrier((first, listed(), *pieces))
-    second = lax.ppermute(first, "c", swap)
+    mask = listed()
     expo_a, stat_a = call(
         score_kernel, (expo, stat), (*pieces, mask, points), flops=flops, moved=6 << 20
     )
@@ -308,7 +308,7 @@
     def sums(*groups):
         return call(
             functools.partial(sums_kernel, groups),
-            (sds((size, padded), bf16),) * 2,
+            (sds((size, padded), bf16),) * len(groups),
             (place, shared, points, first, second, expo_a, stat_a, expo_b, stat_b),
             smem + vmem(8),
             flops=flops,
@@ -316,8 +316,8 @@
             scratch=[pltpu.VMEM((2, 1, count), f32)],
         )
 
-    two, one = sums(2, 1)
-    three, kept = sums(3, 0)
+    two, one, three = sums(2, 1, 3)
+    (kept,) = sums(0)
     got = [kept, along(one, near[1]), along(two, near[2]), along(three, near[3])]
     summed = call(near_kernel, sds((size, padded), bf16), tuple(got))
     got = team_exchange(summed.reshape(peers, rows, padded))

time: 157 us -> 170 us (1.083)
  the two profiles are of different devices: /device:TPU:1 before, /device:TPU:33 now
where the time goes in v8:
time: 170 us
  blocking collectives  92 us (54%)
  starting transfers between devices  31.4 us (18%)
  waiting for transfers between devices  22.1 us (13%)
  Pallas kernels  19.3 us (11%)
  local copies, waits for them, and re-layouts  3.52 us (2%)
    all_to_all x2, blocking collectives, team_exchange(): return lax.all_to_all(a, far, 0, 0, axis_index_groups=teams, tiled=True)  69.9 us
    ppermute x6, starting transfers between devices, along(): return lax.ppermute(a, deep, [(i, (i + by) % zs) for i in range(zs)])  23.9 us
    ppermute x6, waiting for transfers between devices, along(): return lax.ppermute(a, deep, [(i, (i + by) % zs) for i in range(zs)])  22.1 us
    pallas_call x10, Pallas kernels, call(): pl.pallas_call(kernel, out_shape=outs, in_specs=specs or vmem(len(args)),...  19.3 us
    all_to_all x1, blocking collectives, shards(): shared = lax.all_to_all(copies, pool, 0, 0, tiled=True)  11.4 us
    all_to_all x1, blocking collectives, shards(): whole = lax.all_to_all(table, narrow, 0, 0, tiled=True)  10.6 us
    ppermute x1, starting transfers between devices, shards(): second = lax.ppermute(first, 'c', swap)  4.34 us
  transfers between devices with their start and end apart: 8, of which 3 were waited for; matrix products, arithmetic and copies ran while one was open for 0% of the time, Pallas kernels for 5%

profile of v8, /device:TPU:33, one launch (start us, length us, event | category | flops | bytes accessed | tf_op | source)
XLA Modules:
  0.0 169.8 jit_solution(14283971903715299636)
XLA Ops:
  0.6 0.0 copy-start
  1.3 0.1 stack.23.place_ref
  1.4 0.0 copy-start.1
  1.4 1.9 %copy-done.1 = bf16[1536,1024]{1,0:T(8,128)(2,1)S(1)} copy-done((bf16[1536,1024]{1,0:T(8,128)(2,1)S(1)}, bf16[1536,1024]{1,0:T(8,128)(2,1)}, u32[]{:S(2)}) %copy-start.1) | copy-done | bytes 3145752
  3.3 0.0 copy-start.3
  3.3 0.0 copy-start.2
  3.3 1.7 %shard_map.68 = bf16[784,1024]{1,0:T(8,128)(2,1)} custom-call(s32[6]{0:T(128)S(1)} %stack.23.place_ref, bf16[1536,1024]{1,0:T(8,128)(2,1)S(1)} %copy-done.1), custom_call_target="tpu_custom_call" | custom-call | bytes 3145728 | tf_op jit(solution)/shard_map/pallas_call | solution.py:225
  5.1 3.1 %collective-permute-start = (bf16[784,1024]{1,0:T(8,128)(2,1)}, bf16[784,1024]{1,0:T(8,128)(2,1)}, u32[]{:S(2)}, u32[]{:S(2)}) collective-permute-start(bf16[784,1024]{1,0:T(8,128)(2,1)} %shard_map.68), channel_id=1, source_target_pairs={{0,8},{8,0},{1,9},{9,1},{2,10},{10,2},{3,11},{11,3},{4,12},{12,4},... | collective-permute-start | bytes 4816904 | tf_op jit(solution)/shard_map/ppermute | solution.py:271
  8.2 0.0 copy-done
  8.3 36.8 %all_to_all.20 = bf16[8,16,1024]{2,1,0:T(8,128)(2,1)S(1)} all-to-all(bf16[8,16,1024]{2,1,0:T(8,128)(2,1)S(1)} %broadcast_in_dim.6), channel_id=1, replica_groups={{0,128,256,384,24,152,280,408},{8,136,264,392,16,144,272,400},{1,129,25..., dimensions={0} | all-to-all | bytes 524288 | tf_op jit(solution)/shard_map/all_to_all | solution.py:254
  45.1 0.0 collective-permute-done.refs_5_.first_ref
  45.1 4.3 %collective-permute-start.4 = (bf16[784,1024]{1,0:T(8,128)(2,1)}, bf16[784,1024]{1,0:T(8,128)(2,1)S(1)}, u32[]{:S(2)}, u32[]{:S(2)}) collective-permute-start(bf16[784,1024]{1,0:T(8,128)(2,1)} %collective-permute-done.refs_5_.first_ref), channel_id=1, source_target_pairs={{0,1},{1,0},{2,3},{3,2},{4,5},{5,4},{6,7},{7,6},{8,9},{9,8},{10,11... | collective-permute-start | bytes 4816904 | tf_op jit(solution)/shard_map/ppermute | solution.py:276
  49.5 2.7 %collective-permute-start.3 = (bf16[128,1024]{1,0:T(8,128)(2,1)S(1)}, bf16[128,1024]{1,0:T(8,128)(2,1)S(1)}, u32[]{:S(2)}, u32[]{:S(2)}) collective-permute-start(bf16[128,1024]{1,0:T(8,128)(2,1)S(1)} %bitcast.10), channel_id=1, source_target_pairs={{0,32},{32,64},{64,96},{96,128},{128,160},{160,192},{192,224},{224... | collective-permute-start | bytes 786440 | tf_op jit(solution)/shard_map/ppermute | solution.py:251
  52.2 7.1 %collective-permute-start.2 = (bf16[128,1024]{1,0:T(8,128)(2,1)S(1)}, bf16[128,1024]{1,0:T(8,128)(2,1)S(1)}, u32[]{:S(2)}, u32[]{:S(2)}) collective-permute-start(bf16[128,1024]{1,0:T(8,128)(2,1)S(1)} %bitcast.11), channel_id=1, source_target_pairs={{0,448},{32,480},{64,0},{96,32},{128,64},{160,96},{192,128},{224,1... | collective-permute-start | bytes 786440 | tf_op jit(solution)/shard_map/ppermute | solution.py:251
  59.3 3.4 %collective-permute-start.1 = (bf16[128,1024]{1,0:T(8,128)(2,1)S(1)}, bf16[128,1024]{1,0:T(8,128)(2,1)S(1)}, u32[]{:S(2)}, u32[]{:S(2)}) collective-permute-start(bf16[128,1024]{1,0:T(8,128)(2,1)S(1)} %bitcast.12), channel_id=1, source_target_pairs={{0,480},{32,0},{64,32},{96,64},{128,96},{160,128},{192,160},{224,1... | collective-permute-start | bytes 786440 | tf_op jit(solution)/shard_map/ppermute | solution.py:251
  62.7 0.0 copy-done.3
  62.7 0.0 copy-start.4
  62.7 0.7 copy-done.4
  63.4 1.5 shard_map.69.refs_4_
  65.0 0.7 slice.3.refs_0_
  65.7 1.5 shard_map.71.refs_4_
  67.2 0.0 collective-permute-done.3.refs_3_
  67.2 1.4 collective-permute-done.2.refs_2_
  68.6 5.6 %collective-permute-done.1.refs_1_ = bf16[128,1024]{1,0:T(8,128)(2,1)S(1)} collective-permute-done((bf16[128,1024]{1,0:T(8,128)(2,1)S(1)}, bf16[128,1024]{1,0:T(8,128)(2,1)S(1)}, u32[]{:S(2)}, u32[]{:S(2)}) %collective-permute-start.1) | collective-permute-done | bytes 262176 | tf_op jit(solution)/shard_map/ppermute | solution.py:251
  74.2 0.0 copy-done.2
  74.2 2.5 %shard_map.70 = (f32[512,1536]{1,0:T(8,128)S(1)}, f32[2,1536]{1,0:T(2,128)S(1)}) custom-call(bf16[128,1024]{1,0:T(8,128)(2,1)S(1)} %bitcast.13, bf16[128,1024]{1,0:T(8,128)(2,1)S(1)} %collective-permute-done.1.refs_1_, bf16[128,1024]{1,0:T(8,128)(2,1)S(1)} %collective-permute-done.2.refs_2_, bf16[128,1024]{1,0:T(8,128)(2,1)S(1)} %collective-permute-done.3.refs_3_, ...), custom_call_target="tpu_custom_call" | custom-call | flops 1610612736 | bytes 6291456 | tf_op jit(solution)/shard_map/pallas_call | solution.py:225
  76.7 0.0 collective-permute-done.4.refs_6_.second_ref
  76.7 3.9 %shard_map.72 = (f32[512,1536]{1,0:T(8,128)S(1)}, f32[2,1536]{1,0:T(2,128)S(1)}, f32[2,1536]{1,0:T(2,128)S(1)}) custom-call(s32[6]{0:T(128)S(1)} %stack.23.place_ref, f32[2,1536]{1,0:T(2,128)S(1)} %get-tuple-element.15.old_ref.stat_a, bf16[128,1024]{1,0:T(8,128)(2,1)S(1)} %bitcast.14, bf16[128,1024]{1,0:T(8,128)(2,1)S(1)} %collective-permute-done.1.refs_1_, ...), custom_call_target="tpu_custom_call" | custom-call | flops 1610612736 | bytes 6291456 | tf_op jit(solution)/shard_map/pallas_call | solution.py:225
  80.7 0.1 broadcast_in_dim.7
  80.7 11.4 %all_to_all.21.all_ref = f32[16,2,1536]{2,1,0:T(2,128)S(1)} all-to-all(f32[16,2,1536]{2,1,0:T(2,128)S(1)} %broadcast_in_dim.7), channel_id=1, replica_groups=mesh['zh'=4,'zl'=4,'xh'=2,'xl'=2,'y'=4,'c'=2] {'xl','y','c'}, dimensions={0} | all-to-all | bytes 393216 | tf_op jit(solution)/shard_map/all_to_all | solution.py:306
  92.2 4.2 %shard_map.74 = (bf16[128,1152]{1,0:T(8,128)(2,1)S(1)}, bf16[128,1152]{1,0:T(8,128)(2,1)S(1)}, bf16[128,1152]{1,0:T(8,128)(2,1)S(1)}) custom-call(s32[6]{0:T(128)S(1)} %stack.23.place_ref, f32[16,2,1536]{2,1,0:T(2,128)S(1)} %all_to_all.21.all_ref, bf16[1536,1024]{1,0:T(8,128)(2,1)S(1)} %copy-done.2, ...), custom_call_target="tpu_custom_call" | custom-call | flops 1610612736 | bytes 10485760 | tf_op jit(solution)/shard_map/pallas_call | solution.py:225
  96.4 3.4 %collective-permute-start.5 = (bf16[128,1152]{1,0:T(8,128)(2,1)S(1)}, bf16[128,1152]{1,0:T(8,128)(2,1)S(1)}, u32[]{:S(2)}, u32[]{:S(2)}) collective-permute-start(bf16[128,1152]{1,0:T(8,128)(2,1)S(1)} %get-tuple-element.21), channel_id=1, source_target_pairs={{0,32},{32,64},{64,96},{96,128},{128,160},{160,192},{192,224},{224... | collective-permute-start | bytes 884744 | tf_op jit(solution)/shard_map/ppermute | solution.py:251
  99.8 5.4 %collective-permute-start.6 = (bf16[128,1152]{1,0:T(8,128)(2,1)S(1)}, bf16[128,1152]{1,0:T(8,128)(2,1)S(1)}, u32[]{:S(2)}, u32[]{:S(2)}) collective-permute-start(bf16[128,1152]{1,0:T(8,128)(2,1)S(1)} %get-tuple-element.22), channel_id=1, source_target_pairs={{0,64},{32,96},{64,128},{96,160},{128,192},{160,224},{192,256},{22... | collective-permute-start | bytes 884744 | tf_op jit(solution)/shard_map/ppermute | solution.py:251
  105.2 1.9 %collective-permute-start.7 = (bf16[128,1152]{1,0:T(8,128)(2,1)S(1)}, bf16[128,1152]{1,0:T(8,128)(2,1)S(1)}, u32[]{:S(2)}, u32[]{:S(2)}) collective-permute-start(bf16[128,1152]{1,0:T(8,128)(2,1)S(1)} %get-tuple-element.23), channel_id=1, source_target_pairs={{0,480},{32,0},{64,32},{96,64},{128,96},{160,128},{192,160},{224,1... | collective-permute-start | bytes 884744 | tf_op jit(solution)/shard_map/ppermute | solution.py:251
  107.1 2.6 %shard_map.73.a = bf16[128,1152]{1,0:T(8,128)(2,1)S(1)} custom-call(s32[6]{0:T(128)S(1)} %stack.23.place_ref, f32[16,2,1536]{2,1,0:T(2,128)S(1)} %all_to_all.21.all_ref, bf16[1536,1024]{1,0:T(8,128)(2,1)S(1)} %copy-done.2, bf16[784,1024]{1,0:T(8,128)(2,1)} %collective-permute-done.refs_5_.first_ref, ...), custom_call_target="tpu_custom_call" | custom-call | flops 1610612736 | bytes 10485760 | tf_op jit(solution)/shard_map/pallas_call | solution.py:225
  109.7 0.0 collective-permute-done.5.b
  109.7 15.1 %collective-permute-done.6.c = bf16[128,1152]{1,0:T(8,128)(2,1)S(1)} collective-permute-done((bf16[128,1152]{1,0:T(8,128)(2,1)S(1)}, bf16[128,1152]{1,0:T(8,128)(2,1)S(1)}, u32[]{:S(2)}, u32[]{:S(2)}) %collective-permute-start.6) | collective-permute-done | bytes 294944 | tf_op jit(solution)/shard_map/ppermute | solution.py:251
  124.8 0.0 collective-permute-done.7.d
  124.8 0.3 shard_map.75
  125.1 33.1 %all_to_all.22.ref = bf16[8,16,1152]{2,1,0:T(8,128)(2,1)S(1)} all-to-all(bf16[8,16,1152]{2,1,0:T(8,128)(2,1)S(1)} %bitcast.9), channel_id=1, replica_groups={{0,128,256,384,24,152,280,408},{8,136,264,392,16,144,272,400},{1,129,25..., dimensions={0} | all-to-all | bytes 589824 | tf_op jit(solution)/shard_map/all_to_all | solution.py:254
  158.2 0.2 shard_map.76
  158.4 10.6 %all_to_all.23.ref = bf16[8,16,1152]{2,1,0:T(8,128)(2,1)S(1)} all-to-all(bf16[8,16,1152]{2,1,0:T(8,128)(2,1)S(1)} %shard_map.76), channel_id=1, replica_groups=mesh['zh'=4,'zl'=4,'xh'=2,'xl'=2,'y'=4,'c'=2] {'y','c'}, dimensions={0} | all-to-all | bytes 589824 | tf_op jit(solution)/shard_map/all_to_all | solution.py:325
  169.0 0.8 shard_map.77
  (2 shorter events, 0.0 us)
Async XLA Ops:
  0.6 7.6 %copy-start = (bf16[128,1024]{1,0:T(8,128)(2,1)S(1)}, bf16[128,1024]{1,0:T(8,128)(2,1)}, u32[]{:S(2)}) copy-start(bf16[128,1024]{1,0:T(8,128)(2,1)} %param.9) | copy-start | bytes 786436
  1.4 1.9 %copy-start.1 = (bf16[1536,1024]{1,0:T(8,128)(2,1)S(1)}, bf16[1536,1024]{1,0:T(8,128)(2,1)}, u32[]{:S(2)}) copy-start(bf16[1536,1024]{1,0:T(8,128)(2,1)} %points_ref.5) | copy-start | bytes 9437188
  3.3 59.4 %copy-start.3 = (s32[16,2048]{1,0:T(8,128)S(1)}, s32[16,2048]{1,0:T(8,128)}, u32[]{:S(2)}) copy-start(s32[16,2048]{1,0:T(8,128)} %lists_ref.3) | copy-start | bytes 393220
  3.3 70.9 %copy-start.2 = (bf16[1536,1024]{1,0:T(8,128)(2,1)S(1)}, bf16[1536,1024]{1,0:T(8,128)(2,1)}, u32[]{:S(2)}) copy-start(bf16[1536,1024]{1,0:T(8,128)(2,1)} %points_ref.5) | copy-start | bytes 9437188
  5.1 40.0 %collective-permute-start = (bf16[784,1024]{1,0:T(8,128)(2,1)}, bf16[784,1024]{1,0:T(8,128)(2,1)}, u32[]{:S(2)}, u32[]{:S(2)}) collective-permute-start(bf16[784,1024]{1,0:T(8,128)(2,1)} %shard_map.68), channel_id=1, source_target_pairs={{0,8},{8,0},{1,9},{9,1},{2,10},{10,2},{3,11},{11,3},{4,12},{12,4},... | collective-permute-start | bytes 4816904 | tf_op jit(solution)/shard_map/ppermute | solution.py:271
  45.1 31.6 %collective-permute-start.4 = (bf16[784,1024]{1,0:T(8,128)(2,1)}, bf16[784,1024]{1,0:T(8,128)(2,1)S(1)}, u32[]{:S(2)}, u32[]{:S(2)}) collective-permute-start(bf16[784,1024]{1,0:T(8,128)(2,1)} %collective-permute-done.refs_5_.first_ref), channel_id=1, source_target_pairs={{0,1},{1,0},{2,3},{3,2},{4,5},{5,4},{6,7},{7,6},{8,9},{9,8},{10,11... | collective-permute-start | bytes 4816904 | tf_op jit(solution)/shard_map/ppermute | solution.py:276
  49.5 17.7 %collective-permute-start.3 = (bf16[128,1024]{1,0:T(8,128)(2,1)S(1)}, bf16[128,1024]{1,0:T(8,128)(2,1)S(1)}, u32[]{:S(2)}, u32[]{:S(2)}) collective-permute-start(bf16[128,1024]{1,0:T(8,128)(2,1)S(1)} %bitcast.10), channel_id=1, source_target_pairs={{0,32},{32,64},{64,96},{96,128},{128,160},{160,192},{192,224},{224... | collective-permute-start | bytes 786440 | tf_op jit(solution)/shard_map/ppermute | solution.py:251
  52.2 16.4 %collective-permute-start.2 = (bf16[128,1024]{1,0:T(8,128)(2,1)S(1)}, bf16[128,1024]{1,0:T(8,128)(2,1)S(1)}, u32[]{:S(2)}, u32[]{:S(2)}) collective-permute-start(bf16[128,1024]{1,0:T(8,128)(2,1)S(1)} %bitcast.11), channel_id=1, source_target_pairs={{0,448},{32,480},{64,0},{96,32},{128,64},{160,96},{192,128},{224,1... | collective-permute-start | bytes 786440 | tf_op jit(solution)/shard_map/ppermute | solution.py:251
  59.3 14.9 %collective-permute-start.1 = (bf16[128,1024]{1,0:T(8,128)(2,1)S(1)}, bf16[128,1024]{1,0:T(8,128)(2,1)S(1)}, u32[]{:S(2)}, u32[]{:S(2)}) collective-permute-start(bf16[128,1024]{1,0:T(8,128)(2,1)S(1)} %bitcast.12), channel_id=1, source_target_pairs={{0,480},{32,0},{64,32},{96,64},{128,96},{160,128},{192,160},{224,1... | collective-permute-start | bytes 786440 | tf_op jit(solution)/shard_map/ppermute | solution.py:251
  62.7 0.8 copy-start.4
  96.4 13.3 %collective-permute-start.5 = (bf16[128,1152]{1,0:T(8,128)(2,1)S(1)}, bf16[128,1152]{1,0:T(8,128)(2,1)S(1)}, u32[]{:S(2)}, u32[]{:S(2)}) collective-permute-start(bf16[128,1152]{1,0:T(8,128)(2,1)S(1)} %get-tuple-element.21), channel_id=1, source_target_pairs={{0,32},{32,64},{64,96},{96,128},{128,160},{160,192},{192,224},{224... | collective-permute-start | bytes 884744 | tf_op jit(solution)/shard_map/ppermute | solution.py:251
  99.8 25.0 %collective-permute-start.6 = (bf16[128,1152]{1,0:T(8,128)(2,1)S(1)}, bf16[128,1152]{1,0:T(8,128)(2,1)S(1)}, u32[]{:S(2)}, u32[]{:S(2)}) collective-permute-start(bf16[128,1152]{1,0:T(8,128)(2,1)S(1)} %get-tuple-element.22), channel_id=1, source_target_pairs={{0,64},{32,96},{64,128},{96,160},{128,192},{160,224},{192,256},{22... | collective-permute-start | bytes 884744 | tf_op jit(solution)/shard_map/ppermute | solution.py:251
  105.2 19.6 %collective-permute-start.7 = (bf16[128,1152]{1,0:T(8,128)(2,1)S(1)}, bf16[128,1152]{1,0:T(8,128)(2,1)S(1)}, u32[]{:S(2)}, u32[]{:S(2)}) collective-permute-start(bf16[128,1152]{1,0:T(8,128)(2,1)S(1)} %get-tuple-element.23), channel_id=1, source_target_pairs={{0,480},{32,0},{64,32},{96,64},{128,96},{160,128},{192,160},{224,1... | collective-permute-start | bytes 884744 | tf_op jit(solution)/shard_map/ppermute | solution.py:251

commit v9 on v8

--- a/solution.py
+++ b/solution.py
@@ -10,7 +10,6 @@
 temper = 0.1
 prior = 0.01
 gone = -3e38
-near = (0, 1, 2, -1)
 f32 = jnp.float32
 bf16 = jnp.bfloat16
 i32 = jnp.int32
@@ -171,12 +170,16 @@
             more = jnp.dot(part, ref[: part.shape[1], at], preferred_element_type=f32)
             total = more if total is None else total + more
         total = total.astype(bf16)
-        for k, out_ref in enumerate(out_refs):
-            out_ref[:, at] = total[k * lane : (k + 1) * lane]
+        base = 0
+        for out_ref in out_refs:
+            out_ref[:, at] = total[base : base + out_ref.shape[0]]
+            base += out_ref.shape[0]
     mass = sum(jnp.sum(part.astype(f32), axis=1, keepdims=True) for part in parts)
     tail = halves(mass)
-    for k, out_ref in enumerate(out_refs):
-        out_ref[:, width:] = tail[k * lane : (k + 1) * lane]
+    base = 0
+    for out_ref in out_refs:
+        out_ref[:, width:] = tail[base : base + out_ref.shape[0]]
+        base += out_ref.shape[0]
 
 
 def added(pieces, width):
@@ -192,9 +195,10 @@
     return jnp.where(lanes == 0, high, jnp.where(lanes == 1, mass - high, 0.0)).astype(bf16)
 
 
-def near_kernel(a, b, c, d, out):
+def near_kernel(a, low, high, b, c, out):
     width = a.shape[1] - lane
-    total, mass = added([a[...], b[...], c[...], d[...]], width)
+    pair = jnp.concatenate([low[...], high[...]])
+    total, mass = added([a[...], pair, b[...], c[...]], width)
     out[:, :width] = total.astype(bf16)
     out[:, width:] = halves(mass)
 
@@ -272,12 +276,12 @@
     own = lax.dynamic_slice(centroids, (n * rows, 0), (rows, width))
     copies = jnp.broadcast_to(own, (peers, rows, width))
     group = team_exchange(copies).reshape(size, width)
-    first, group = lax.optimization_barrier((first, group))
-    second = lax.ppermute(first, "c", swap)
-    pieces = [group] + [along(group, -d) for d in near[1:]]
-    flops = 2 * len(near) * size * count * width
+    middle = size // 2
+    two = [along(group[:middle], -2), along(group[middle:], 2)]
+    pieces = [group, along(group, -1), *two, along(group, 1)]
+    flops = 2 * 4 * size * count * width
     stat = sds((2, count), f32)
-    expo = sds((len(near) * size, count), f32)
+    expo = sds((4 * size, count), f32)
 
     def listed(*other):
         return call(
@@ -288,7 +292,8 @@
             moved=8 << 20,
         )
 
-    mask = listed()
+    first, mask, *pieces = lax.optimization_barrier((first, listed(), *pieces))
+    second = lax.ppermute(first, "c", swap)
     expo_a, stat_a = call(
         score_kernel, (expo, stat), (*pieces, mask, points), flops=flops, moved=6 << 20
     )
@@ -297,7 +302,7 @@
         other_kernel,
         (expo, stat, sds((2, count), f32)),
         (place, stat_a, *pieces, mask, first, second),
-        smem + vmem(8),
+        smem + vmem(4 + len(pieces)),
         flops=flops,
         moved=6 << 20,
     )
@@ -305,10 +310,10 @@
     copies = jnp.broadcast_to(both, (2 * parts, 2, count))
     shared = lax.all_to_all(copies, pool, 0, 0, tiled=True)
 
-    def sums(*groups):
+    def sums(groups, cuts):
         return call(
             functools.partial(sums_kernel, groups),
-            (sds((size, padded), bf16),) * len(groups),
+            tuple(sds((cut, padded), bf16) for cut in cuts),
             (place, shared, points, first, second, expo_a, stat_a, expo_b, stat_b),
             smem + vmem(8),
             flops=flops,
@@ -316,9 +321,9 @@
             scratch=[pltpu.VMEM((2, 1, count), f32)],
         )
 
-    two, one, three = sums(2, 1, 3)
-    (kept,) = sums(0)
-    got = [kept, along(one, near[1]), along(two, near[2]), along(three, near[3])]
+    low, high, one, three = sums((2, 1, 3), (size // 2, size // 2, size, size))
+    (kept,) = sums((0,), (size,))
+    got = [kept, along(low, 2), along(high, -2), along(one, 1), along(three, -1)]
     summed = call(near_kernel, sds((size, padded), bf16), tuple(got))
     got = team_exchange(summed.reshape(peers, rows, padded))
     table = call(last_kernel, sds((parts, rows, padded), bf16), (got, own))

time: 170 us -> 154 us (0.906)
  the two profiles are of different devices: /device:TPU:33 before, /device:TPU:1 now
where the time goes in v9:
time: 154 us; the launch traced here: 153 us
  blocking collectives  77.5 us (50%)
  starting transfers between devices  41.1 us (27%)
  Pallas kernels  19.4 us (13%)
  waiting for transfers between devices  10 us (6%)
  local copies, waits for them, and re-layouts  3.53 us (2%)
  between operations  1.56 us (1%)
    all_to_all x2, blocking collectives, team_exchange(): return lax.all_to_all(a, far, 0, 0, axis_index_groups=teams, tiled=True)  52.6 us
    ppermute x8, starting transfers between devices, along(): return lax.ppermute(a, deep, [(i, (i + by) % zs) for i in range(zs)])  31.6 us
    pallas_call x10, Pallas kernels, call(): pl.pallas_call(kernel, out_shape=outs, in_specs=specs or vmem(len(args)),...  19.4 us
    all_to_all x1, blocking collectives, shards(): whole = lax.all_to_all(table, narrow, 0, 0, tiled=True)  13.8 us
    all_to_all x1, blocking collectives, shards(): shared = lax.all_to_all(copies, pool, 0, 0, tiled=True)  11.1 us
    ppermute x8, waiting for transfers between devices, along(): return lax.ppermute(a, deep, [(i, (i + by) % zs) for i in range(zs)])  10 us
    ppermute x1, starting transfers between devices, shards(): second = lax.ppermute(first, 'c', swap)  5.56 us
    ppermute x1, starting transfers between devices, shards(): first = lax.ppermute(half, 'xl', swap)  3.95 us
  transfers between devices with their start and end apart: 10, of which 3 were waited for; matrix products, arithmetic and copies ran while one was open for 0% of the time, Pallas kernels for 5%

profile of v9, /device:TPU:1, one launch (start us, length us, event | category | flops | bytes accessed | tf_op | source)
XLA Modules:
  0.0 153.1 jit_solution(11432905276055149496)
XLA Ops:
  0.6 0.0 copy-start
  1.3 0.1 stack.23.place_ref
  1.4 0.0 copy-start.1
  1.4 1.9 %copy-done.1 = bf16[1536,1024]{1,0:T(8,128)(2,1)S(1)} copy-done((bf16[1536,1024]{1,0:T(8,128)(2,1)S(1)}, bf16[1536,1024]{1,0:T(8,128)(2,1)}, u32[]{:S(2)}) %copy-start.1) | copy-done | bytes 3145752
  3.3 0.0 copy-start.3
  3.3 0.0 copy-start.2
  3.3 1.7 %shard_map.68 = bf16[784,1024]{1,0:T(8,128)(2,1)} custom-call(s32[6]{0:T(128)S(1)} %stack.23.place_ref, bf16[1536,1024]{1,0:T(8,128)(2,1)S(1)} %copy-done.1), custom_call_target="tpu_custom_call" | custom-call | bytes 3145728 | tf_op jit(solution)/shard_map/pallas_call | solution.py:229
  5.1 4.0 %collective-permute-start = (bf16[784,1024]{1,0:T(8,128)(2,1)}, bf16[784,1024]{1,0:T(8,128)(2,1)}, u32[]{:S(2)}, u32[]{:S(2)}) collective-permute-start(bf16[784,1024]{1,0:T(8,128)(2,1)} %shard_map.68), channel_id=1, source_target_pairs={{0,8},{8,0},{1,9},{9,1},{2,10},{10,2},{3,11},{11,3},{4,12},{12,4},... | collective-permute-start | bytes 4816904 | tf_op jit(solution)/shard_map/ppermute | solution.py:275
  9.0 0.0 copy-done
  9.1 30.8 %all_to_all.20 = bf16[8,16,1024]{2,1,0:T(8,128)(2,1)S(1)} all-to-all(bf16[8,16,1024]{2,1,0:T(8,128)(2,1)S(1)} %broadcast_in_dim.6), channel_id=1, replica_groups={{0,128,256,384,24,152,280,408},{8,136,264,392,16,144,272,400},{1,129,25..., dimensions={0} | all-to-all | bytes 524288 | tf_op jit(solution)/shard_map/all_to_all | solution.py:258
  39.9 9.6 %collective-permute-start.4 = (bf16[128,1024]{1,0:T(8,128)(2,1)S(1)}, bf16[128,1024]{1,0:T(8,128)(2,1)S(1)}, u32[]{:S(2)}, u32[]{:S(2)}) collective-permute-start(bf16[128,1024]{1,0:T(8,128)(2,1)S(1)} %bitcast.12), channel_id=1, source_target_pairs={{0,32},{32,64},{64,96},{96,128},{128,160},{160,192},{192,224},{224... | collective-permute-start | bytes 786440 | tf_op jit(solution)/shard_map/ppermute | solution.py:255
  49.5 1.9 %collective-permute-start.1 = (bf16[128,1024]{1,0:T(8,128)(2,1)S(1)}, bf16[128,1024]{1,0:T(8,128)(2,1)S(1)}, u32[]{:S(2)}, u32[]{:S(2)}) collective-permute-start(bf16[128,1024]{1,0:T(8,128)(2,1)S(1)} %bitcast.13), channel_id=1, source_target_pairs={{0,480},{32,0},{64,32},{96,64},{128,96},{160,128},{192,160},{224,1... | collective-permute-start | bytes 786440 | tf_op jit(solution)/shard_map/ppermute | solution.py:255
  51.4 2.9 %collective-permute-start.2 = (bf16[64,1024]{1,0:T(8,128)(2,1)S(1)}, bf16[64,1024]{1,0:T(8,128)(2,1)S(1)}, u32[]{:S(2)}, u32[]{:S(2)}) collective-permute-start(bf16[64,1024]{1,0:T(8,128)(2,1)S(1)} %bitcast.19), channel_id=1, source_target_pairs={{0,448},{32,480},{64,0},{96,32},{128,64},{160,96},{192,128},{224,1... | collective-permute-start | bytes 393224 | tf_op jit(solution)/shard_map/ppermute | solution.py:255
  54.3 3.3 %collective-permute-start.3 = (bf16[64,1024]{1,0:T(8,128)(2,1)S(1)}, bf16[64,1024]{1,0:T(8,128)(2,1)S(1)}, u32[]{:S(2)}, u32[]{:S(2)}) collective-permute-start(bf16[64,1024]{1,0:T(8,128)(2,1)S(1)} %bitcast.18), channel_id=1, source_target_pairs={{0,64},{32,96},{64,128},{96,160},{128,192},{160,224},{192,256},{22... | collective-permute-start | bytes 393224 | tf_op jit(solution)/shard_map/ppermute | solution.py:255
  57.6 0.0 copy-done.3
  57.6 0.0 copy-start.4
  57.6 0.7 copy-done.4
  58.4 1.5 shard_map.69.refs_5_
  59.9 0.0 collective-permute-done.2.refs_2_
  59.9 3.7 %collective-permute-done.3.refs_3_ = bf16[64,1024]{1,0:T(8,128)(2,1)S(1)} collective-permute-done((bf16[64,1024]{1,0:T(8,128)(2,1)S(1)}, bf16[64,1024]{1,0:T(8,128)(2,1)S(1)}, u32[]{:S(2)}, u32[]{:S(2)}) %collective-permute-start.3) | collective-permute-done | bytes 131104 | tf_op jit(solution)/shard_map/ppermute | solution.py:255
  63.6 0.0 collective-permute-done.4.refs_4_
  63.6 0.0 collective-permute-done.1.refs_1_
  63.6 0.0 collective-permute-done.refs_6_.first_ref
  63.6 5.6 %collective-permute-start.5 = (bf16[784,1024]{1,0:T(8,128)(2,1)}, bf16[784,1024]{1,0:T(8,128)(2,1)S(1)}, u32[]{:S(2)}, u32[]{:S(2)}) collective-permute-start(bf16[784,1024]{1,0:T(8,128)(2,1)} %collective-permute-done.refs_6_.first_ref), channel_id=1, source_target_pairs={{0,1},{1,0},{2,3},{3,2},{4,5},{5,4},{6,7},{7,6},{8,9},{9,8},{10,11... | collective-permute-start | bytes 4816904 | tf_op jit(solution)/shard_map/ppermute | solution.py:296
  69.2 0.7 slice.19.refs_0_
  69.9 1.5 shard_map.71.refs_5_
  71.4 0.0 copy-done.2
  71.4 2.5 %shard_map.70 = (f32[512,1536]{1,0:T(8,128)S(1)}, f32[2,1536]{1,0:T(2,128)S(1)}) custom-call(bf16[128,1024]{1,0:T(8,128)(2,1)S(1)} %bitcast.14, bf16[128,1024]{1,0:T(8,128)(2,1)S(1)} %collective-permute-done.1.refs_1_, bf16[64,1024]{1,0:T(8,128)(2,1)S(1)} %collective-permute-done.2.refs_2_, bf16[64,1024]{1,0:T(8,128)(2,1)S(1)} %collective-permute-done.3.refs_3_, ...), custom_call_target="tpu_custom_call" | custom-call | flops 1610612736 | bytes 6291456 | tf_op jit(solution)/shard_map/pallas_call | solution.py:229
  73.9 0.0 collective-permute-done.5.refs_7_.second_ref
  73.9 3.9 %shard_map.72 = (f32[512,1536]{1,0:T(8,128)S(1)}, f32[2,1536]{1,0:T(2,128)S(1)}, f32[2,1536]{1,0:T(2,128)S(1)}) custom-call(s32[6]{0:T(128)S(1)} %stack.23.place_ref, f32[2,1536]{1,0:T(2,128)S(1)} %get-tuple-element.26.old_ref.stat_a, bf16[128,1024]{1,0:T(8,128)(2,1)S(1)} %bitcast.15, bf16[128,1024]{1,0:T(8,128)(2,1)S(1)} %collective-permute-done.1.refs_1_, ...), custom_call_target="tpu_custom_call" | custom-call | flops 1610612736 | bytes 6291456 | tf_op jit(solution)/shard_map/pallas_call | solution.py:229
  77.9 0.1 broadcast_in_dim.7
  77.9 11.1 %all_to_all.21.all_ref = f32[16,2,1536]{2,1,0:T(2,128)S(1)} all-to-all(f32[16,2,1536]{2,1,0:T(2,128)S(1)} %broadcast_in_dim.7), channel_id=1, replica_groups=mesh['zh'=4,'zl'=4,'xh'=2,'xl'=2,'y'=4,'c'=2] {'xl','y','c'}, dimensions={0} | all-to-all | bytes 393216 | tf_op jit(solution)/shard_map/all_to_all | solution.py:311
  89.0 4.2 %shard_map.74 = (bf16[64,1152]{1,0:T(8,128)(2,1)S(1)}, bf16[64,1152]{1,0:T(8,128)(2,1)S(1)}, bf16[128,1152]{1,0:T(8,128)(2,1)S(1)}, bf16[128,1152]{1,0:T(8,128)(2,1)S(1)}) custom-call(s32[6]{0:T(128)S(1)} %stack.23.place_ref, f32[16,2,1536]{2,1,0:T(2,128)S(1)} %all_to_all.21.all_ref, bf16[1536,1024]{1,0:T(8,128)(2,1)S(1)} %copy-done.2, ...), custom_call_target="tpu_custom_call" | custom-call | flops 1610612736 | bytes 10485760 | tf_op jit(solution)/shard_map/pallas_call | solution.py:229
  93.2 1.9 %collective-permute-start.8 = (bf16[128,1152]{1,0:T(8,128)(2,1)S(1)}, bf16[128,1152]{1,0:T(8,128)(2,1)S(1)}, u32[]{:S(2)}, u32[]{:S(2)}) collective-permute-start(bf16[128,1152]{1,0:T(8,128)(2,1)S(1)} %get-tuple-element.34), channel_id=1, source_target_pairs={{0,32},{32,64},{64,96},{96,128},{128,160},{160,192},{192,224},{224... | collective-permute-start | bytes 884744 | tf_op jit(solution)/shard_map/ppermute | solution.py:255
  95.1 4.6 %collective-permute-start.9 = (bf16[128,1152]{1,0:T(8,128)(2,1)S(1)}, bf16[128,1152]{1,0:T(8,128)(2,1)S(1)}, u32[]{:S(2)}, u32[]{:S(2)}) collective-permute-start(bf16[128,1152]{1,0:T(8,128)(2,1)S(1)} %get-tuple-element.35), channel_id=1, source_target_pairs={{0,480},{32,0},{64,32},{96,64},{128,96},{160,128},{192,160},{224,1... | collective-permute-start | bytes 884744 | tf_op jit(solution)/shard_map/ppermute | solution.py:255
  99.7 1.9 %collective-permute-start.6 = (bf16[64,1152]{1,0:T(8,128)(2,1)S(1)}, bf16[64,1152]{1,0:T(8,128)(2,1)S(1)}, u32[]{:S(2)}, u32[]{:S(2)}) collective-permute-start(bf16[64,1152]{1,0:T(8,128)(2,1)S(1)} %get-tuple-element.32), channel_id=1, source_target_pairs={{0,64},{32,96},{64,128},{96,160},{128,192},{160,224},{192,256},{22... | collective-permute-start | bytes 442376 | tf_op jit(solution)/shard_map/ppermute | solution.py:255
  101.6 5.5 %collective-permute-start.7 = (bf16[64,1152]{1,0:T(8,128)(2,1)S(1)}, bf16[64,1152]{1,0:T(8,128)(2,1)S(1)}, u32[]{:S(2)}, u32[]{:S(2)}) collective-permute-start(bf16[64,1152]{1,0:T(8,128)(2,1)S(1)} %get-tuple-element.33), channel_id=1, source_target_pairs={{0,448},{32,480},{64,0},{96,32},{128,64},{160,96},{192,128},{224,1... | collective-permute-start | bytes 442376 | tf_op jit(solution)/shard_map/ppermute | solution.py:255
  107.1 2.6 %shard_map.73.a = bf16[128,1152]{1,0:T(8,128)(2,1)S(1)} custom-call(s32[6]{0:T(128)S(1)} %stack.23.place_ref, f32[16,2,1536]{2,1,0:T(2,128)S(1)} %all_to_all.21.all_ref, bf16[1536,1024]{1,0:T(8,128)(2,1)S(1)} %copy-done.2, bf16[784,1024]{1,0:T(8,128)(2,1)} %collective-permute-done.refs_6_.first_ref, ...), custom_call_target="tpu_custom_call" | custom-call | flops 1610612736 | bytes 10485760 | tf_op jit(solution)/shard_map/pallas_call | solution.py:229
  109.7 2.1 %collective-permute-done.6.low = bf16[64,1152]{1,0:T(8,128)(2,1)S(1)} collective-permute-done((bf16[64,1152]{1,0:T(8,128)(2,1)S(1)}, bf16[64,1152]{1,0:T(8,128)(2,1)S(1)}, u32[]{:S(2)}, u32[]{:S(2)}) %collective-permute-start.6) | collective-permute-done | bytes 147488 | tf_op jit(solution)/shard_map/ppermute | solution.py:255
  111.8 4.2 %collective-permute-done.7.high = bf16[64,1152]{1,0:T(8,128)(2,1)S(1)} collective-permute-done((bf16[64,1152]{1,0:T(8,128)(2,1)S(1)}, bf16[64,1152]{1,0:T(8,128)(2,1)S(1)}, u32[]{:S(2)}, u32[]{:S(2)}) %collective-permute-start.7) | collective-permute-done | bytes 147488 | tf_op jit(solution)/shard_map/ppermute | solution.py:255
  116.1 0.0 collective-permute-done.8.b
  116.1 0.0 collective-permute-done.9.c
  116.1 0.3 shard_map.75
  116.4 21.9 %all_to_all.22.ref = bf16[8,16,1152]{2,1,0:T(8,128)(2,1)S(1)} all-to-all(bf16[8,16,1152]{2,1,0:T(8,128)(2,1)S(1)} %bitcast.11), channel_id=1, replica_groups={{0,128,256,384,24,152,280,408},{8,136,264,392,16,144,272,400},{1,129,25..., dimensions={0} | all-to-all | bytes 589824 | tf_op jit(solution)/shard_map/all_to_all | solution.py:258
  138.3 0.2 shard_map.76
  138.4 13.8 %all_to_all.23.ref = bf16[8,16,1152]{2,1,0:T(8,128)(2,1)S(1)} all-to-all(bf16[8,16,1152]{2,1,0:T(8,128)(2,1)S(1)} %shard_map.76), channel_id=1, replica_groups=mesh['zh'=4,'zl'=4,'xh'=2,'xl'=2,'y'=4,'c'=2] {'y','c'}, dimensions={0} | all-to-all | bytes 589824 | tf_op jit(solution)/shard_map/all_to_all | solution.py:330
  152.3 0.8 shard_map.77
  (3 shorter events, 0.0 us)
Async XLA Ops:
  0.6 8.4 %copy-start = (bf16[128,1024]{1,0:T(8,128)(2,1)S(1)}, bf16[128,1024]{1,0:T(8,128)(2,1)}, u32[]{:S(2)}) copy-start(bf16[128,1024]{1,0:T(8,128)(2,1)} %param.9) | copy-start | bytes 786436
  1.4 1.9 %copy-start.1 = (bf16[1536,1024]{1,0:T(8,128)(2,1)S(1)}, bf16[1536,1024]{1,0:T(8,128)(2,1)}, u32[]{:S(2)}) copy-start(bf16[1536,1024]{1,0:T(8,128)(2,1)} %points_ref.5) | copy-start | bytes 9437188
  3.3 54.3 %copy-start.3 = (s32[16,2048]{1,0:T(8,128)S(1)}, s32[16,2048]{1,0:T(8,128)}, u32[]{:S(2)}) copy-start(s32[16,2048]{1,0:T(8,128)} %lists_ref.3) | copy-start | bytes 393220
  3.3 68.1 %copy-start.2 = (bf16[1536,1024]{1,0:T(8,128)(2,1)S(1)}, bf16[1536,1024]{1,0:T(8,128)(2,1)}, u32[]{:S(2)}) copy-start(bf16[1536,1024]{1,0:T(8,128)(2,1)} %points_ref.5) | copy-start | bytes 9437188
  5.1 58.5 %collective-permute-start = (bf16[784,1024]{1,0:T(8,128)(2,1)}, bf16[784,1024]{1,0:T(8,128)(2,1)}, u32[]{:S(2)}, u32[]{:S(2)}) collective-permute-start(bf16[784,1024]{1,0:T(8,128)(2,1)} %shard_map.68), channel_id=1, source_target_pairs={{0,8},{8,0},{1,9},{9,1},{2,10},{10,2},{3,11},{11,3},{4,12},{12,4},... | collective-permute-start | bytes 4816904 | tf_op jit(solution)/shard_map/ppermute | solution.py:275
  39.9 23.7 %collective-permute-start.4 = (bf16[128,1024]{1,0:T(8,128)(2,1)S(1)}, bf16[128,1024]{1,0:T(8,128)(2,1)S(1)}, u32[]{:S(2)}, u32[]{:S(2)}) collective-permute-start(bf16[128,1024]{1,0:T(8,128)(2,1)S(1)} %bitcast.12), channel_id=1, source_target_pairs={{0,32},{32,64},{64,96},{96,128},{128,160},{160,192},{192,224},{224... | collective-permute-start | bytes 786440 | tf_op jit(solution)/shard_map/ppermute | solution.py:255
  49.5 14.1 %collective-permute-start.1 = (bf16[128,1024]{1,0:T(8,128)(2,1)S(1)}, bf16[128,1024]{1,0:T(8,128)(2,1)S(1)}, u32[]{:S(2)}, u32[]{:S(2)}) collective-permute-start(bf16[128,1024]{1,0:T(8,128)(2,1)S(1)} %bitcast.13), channel_id=1, source_target_pairs={{0,480},{32,0},{64,32},{96,64},{128,96},{160,128},{192,160},{224,1... | collective-permute-start | bytes 786440 | tf_op jit(solution)/shard_map/ppermute | solution.py:255
  51.4 8.5 %collective-permute-start.2 = (bf16[64,1024]{1,0:T(8,128)(2,1)S(1)}, bf16[64,1024]{1,0:T(8,128)(2,1)S(1)}, u32[]{:S(2)}, u32[]{:S(2)}) collective-permute-start(bf16[64,1024]{1,0:T(8,128)(2,1)S(1)} %bitcast.19), channel_id=1, source_target_pairs={{0,448},{32,480},{64,0},{96,32},{128,64},{160,96},{192,128},{224,1... | collective-permute-start | bytes 393224 | tf_op jit(solution)/shard_map/ppermute | solution.py:255
  54.3 9.2 %collective-permute-start.3 = (bf16[64,1024]{1,0:T(8,128)(2,1)S(1)}, bf16[64,1024]{1,0:T(8,128)(2,1)S(1)}, u32[]{:S(2)}, u32[]{:S(2)}) collective-permute-start(bf16[64,1024]{1,0:T(8,128)(2,1)S(1)} %bitcast.18), channel_id=1, source_target_pairs={{0,64},{32,96},{64,128},{96,160},{128,192},{160,224},{192,256},{22... | collective-permute-start | bytes 393224 | tf_op jit(solution)/shard_map/ppermute | solution.py:255
  57.6 0.8 copy-start.4
  63.6 10.3 %collective-permute-start.5 = (bf16[784,1024]{1,0:T(8,128)(2,1)}, bf16[784,1024]{1,0:T(8,128)(2,1)S(1)}, u32[]{:S(2)}, u32[]{:S(2)}) collective-permute-start(bf16[784,1024]{1,0:T(8,128)(2,1)} %collective-permute-done.refs_6_.first_ref), channel_id=1, source_target_pairs={{0,1},{1,0},{2,3},{3,2},{4,5},{5,4},{6,7},{7,6},{8,9},{9,8},{10,11... | collective-permute-start | bytes 4816904 | tf_op jit(solution)/shard_map/ppermute | solution.py:296
  93.2 22.8 %collective-permute-start.8 = (bf16[128,1152]{1,0:T(8,128)(2,1)S(1)}, bf16[128,1152]{1,0:T(8,128)(2,1)S(1)}, u32[]{:S(2)}, u32[]{:S(2)}) collective-permute-start(bf16[128,1152]{1,0:T(8,128)(2,1)S(1)} %get-tuple-element.34), channel_id=1, source_target_pairs={{0,32},{32,64},{64,96},{96,128},{128,160},{160,192},{192,224},{224... | collective-permute-start | bytes 884744 | tf_op jit(solution)/shard_map/ppermute | solution.py:255
  95.1 20.9 %collective-permute-start.9 = (bf16[128,1152]{1,0:T(8,128)(2,1)S(1)}, bf16[128,1152]{1,0:T(8,128)(2,1)S(1)}, u32[]{:S(2)}, u32[]{:S(2)}) collective-permute-start(bf16[128,1152]{1,0:T(8,128)(2,1)S(1)} %get-tuple-element.35), channel_id=1, source_target_pairs={{0,480},{32,0},{64,32},{96,64},{128,96},{160,128},{192,160},{224,1... | collective-permute-start | bytes 884744 | tf_op jit(solution)/shard_map/ppermute | solution.py:255
  99.7 12.1 %collective-permute-start.6 = (bf16[64,1152]{1,0:T(8,128)(2,1)S(1)}, bf16[64,1152]{1,0:T(8,128)(2,1)S(1)}, u32[]{:S(2)}, u32[]{:S(2)}) collective-permute-start(bf16[64,1152]{1,0:T(8,128)(2,1)S(1)} %get-tuple-element.32), channel_id=1, source_target_pairs={{0,64},{32,96},{64,128},{96,160},{128,192},{160,224},{192,256},{22... | collective-permute-start | bytes 442376 | tf_op jit(solution)/shard_map/ppermute | solution.py:255
  101.6 14.4 %collective-permute-start.7 = (bf16[64,1152]{1,0:T(8,128)(2,1)S(1)}, bf16[64,1152]{1,0:T(8,128)(2,1)S(1)}, u32[]{:S(2)}, u32[]{:S(2)}) collective-permute-start(bf16[64,1152]{1,0:T(8,128)(2,1)S(1)} %get-tuple-element.33), channel_id=1, source_target_pairs={{0,448},{32,480},{64,0},{96,32},{128,64},{160,96},{192,128},{224,1... | collective-permute-start | bytes 442376 | tf_op jit(solution)/shard_map/ppermute | solution.py:255

commit v10 on v9

--- a/solution.py
+++ b/solution.py
@@ -25,14 +25,20 @@
 
 
 def mask_kernel(place_ref, lists_ref, owner_ref, *refs):
-    *other, mask_ref = refs
+    if len(refs) == 1:
+        (mask_ref,) = refs
+        cluster = place_ref[0]
+    else:
+        other_ref, mask_ref, keep_ref = refs
+        kept = keep_ref.shape[0]
+        keep_ref[...] = other_ref[:kept, :]
+        cluster = other_ref[kept : kept + 16, :lane].astype(f32)[0:1, 0:1].astype(i32)
     n, zl, x = place_ref[1], place_ref[4], place_ref[5]
     count = lists_ref.shape[1]
     blocks = owner_ref.shape[0]
     in_block = lax.broadcasted_iota(i32, (lane, count), 0)
     of_blocks = lax.broadcasted_iota(i32, (blocks, count), 0)
     of_lists = lax.broadcasted_iota(i32, lists_ref.shape, 0)
-    cluster = other[0][0:1, 0:1].astype(f32).astype(i32) if other else place_ref[0]
     ids = jnp.sum(jnp.where(of_lists == cluster, lists_ref[...], 0), axis=0, keepdims=True)
     which = (of_blocks == (ids >> 7)).astype(bf16)
     here = in_block == (ids & 127)
@@ -286,22 +292,23 @@
     def listed(*other):
         return call(
             mask_kernel,
-            sds((lane, lane), f32),
+            (sds((lane, lane), f32),) + tuple(sds((count // 2, width), bf16) for _ in other),
             (place, lists, owner_map.reshape(-1, lane)) + other,
             smem + vmem(2 + len(other)),
             moved=8 << 20,
         )
 
-    first, mask, *pieces = lax.optimization_barrier((first, listed(), *pieces))
+    (mask,) = listed()
+    mask_b, first = listed(first)
+    first, mask, mask_b, *pieces = lax.optimization_barrier((first, mask, mask_b, *pieces))
     second = lax.ppermute(first, "c", swap)
     expo_a, stat_a = call(
         score_kernel, (expo, stat), (*pieces, mask, points), flops=flops, moved=6 << 20
     )
-    mask = listed(first[count // 2 :, :lane])
     expo_b, stat_b, both = call(
         other_kernel,
         (expo, stat, sds((2, count), f32)),
-        (place, stat_a, *pieces, mask, first, second),
+        (place, stat_a, *pieces, mask_b, first, second),
         smem + vmem(4 + len(pieces)),
         flops=flops,
         moved=6 << 20,

time: 154 us -> 150 us (0.974)
  Pallas kernels: 19.4 us -> 15.8 us
    pallas_call x10, Pallas kernels: 19.4 us -> 15.8 us  [call(): pl.pallas_call(kernel, out_shape=outs, in_specs=specs or vmem(len(args)),...]
  transfers between devices with their start and end apart: 10 -> 10, of which waited for: 3 -> 4; matrix products, arithmetic and copies ran while one was open for 0% -> 0% of each run, Pallas kernels for 5% -> 5%
where the time goes in v10:
time: 150 us; the launch traced here: 149 us
  blocking collectives  78 us (52%)
  starting transfers between devices  41.1 us (27%)
  Pallas kernels  15.8 us (11%)
  waiting for transfers between devices  9.59 us (6%)
  local copies, waits for them, and re-layouts  3 us (2%)
  between operations  1.57 us (1%)
    all_to_all x2, blocking collectives, team_exchange(): return lax.all_to_all(a, far, 0, 0, axis_index_groups=teams, tiled=True)  52.9 us
    ppermute x8, starting transfers between devices, along(): return lax.ppermute(a, deep, [(i, (i + by) % zs) for i in range(zs)])  31.6 us
    pallas_call x10, Pallas kernels, call(): pl.pallas_call(kernel, out_shape=outs, in_specs=specs or vmem(len(args)),...  15.8 us
    all_to_all x1, blocking collectives, shards(): whole = lax.all_to_all(table, narrow, 0, 0, tiled=True)  13.8 us
    all_to_all x1, blocking collectives, shards(): shared = lax.all_to_all(copies, pool, 0, 0, tiled=True)  11.3 us
    ppermute x8, waiting for transfers between devices, along(): return lax.ppermute(a, deep, [(i, (i + by) % zs) for i in range(zs)])  9.15 us
    ppermute x1, starting transfers between devices, shards(): second = lax.ppermute(first, 'c', swap)  5.55 us
    ppermute x1, starting transfers between devices, shards(): first = lax.ppermute(half, 'xl', swap)  3.95 us
  transfers between devices with their start and end apart: 10, of which 4 were waited for; matrix products, arithmetic and copies ran while one was open for 0% of the time, Pallas kernels for 5%

profile of v10, /device:TPU:1, one launch (start us, length us, event | category | flops | bytes accessed | tf_op | source)
XLA Modules:
  0.0 149.0 jit_solution(7789846342353108589)
XLA Ops:
  0.6 0.0 copy-start
  1.3 0.1 stack.23.place_ref
  1.4 0.0 copy-start.1
  1.4 1.9 %copy-done.1 = bf16[1536,1024]{1,0:T(8,128)(2,1)S(1)} copy-done((bf16[1536,1024]{1,0:T(8,128)(2,1)S(1)}, bf16[1536,1024]{1,0:T(8,128)(2,1)}, u32[]{:S(2)}) %copy-start.1) | copy-done | bytes 3145752
  3.3 0.0 copy-start.4
  3.3 0.7 shard_map.68
  4.0 3.9 %collective-permute-start = (bf16[784,1024]{1,0:T(8,128)(2,1)S(1)}, bf16[784,1024]{1,0:T(8,128)(2,1)S(1)}, u32[]{:S(2)}, u32[]{:S(2)}) collective-permute-start(bf16[784,1024]{1,0:T(8,128)(2,1)S(1)} %shard_map.68), channel_id=1, source_target_pairs={{0,8},{8,0},{1,9},{9,1},{2,10},{10,2},{3,11},{11,3},{4,12},{12,4},... | collective-permute-start | bytes 4816904 | tf_op jit(solution)/shard_map/ppermute | solution.py:281
  8.0 0.0 copy-done
  8.0 0.0 copy-start.2
  8.1 31.1 %all_to_all.20 = bf16[8,16,1024]{2,1,0:T(8,128)(2,1)S(1)} all-to-all(bf16[8,16,1024]{2,1,0:T(8,128)(2,1)S(1)} %broadcast_in_dim.6), channel_id=1, replica_groups={{0,128,256,384,24,152,280,408},{8,136,264,392,16,144,272,400},{1,129,25..., dimensions={0} | all-to-all | bytes 524288 | tf_op jit(solution)/shard_map/all_to_all | solution.py:264
  39.1 9.6 %collective-permute-start.4 = (bf16[128,1024]{1,0:T(8,128)(2,1)S(1)}, bf16[128,1024]{1,0:T(8,128)(2,1)S(1)}, u32[]{:S(2)}, u32[]{:S(2)}) collective-permute-start(bf16[128,1024]{1,0:T(8,128)(2,1)S(1)} %bitcast.12), channel_id=1, source_target_pairs={{0,32},{32,64},{64,96},{96,128},{128,160},{160,192},{192,224},{224... | collective-permute-start | bytes 786440 | tf_op jit(solution)/shard_map/ppermute | solution.py:261
  48.7 1.9 %collective-permute-start.1 = (bf16[128,1024]{1,0:T(8,128)(2,1)S(1)}, bf16[128,1024]{1,0:T(8,128)(2,1)S(1)}, u32[]{:S(2)}, u32[]{:S(2)}) collective-permute-start(bf16[128,1024]{1,0:T(8,128)(2,1)S(1)} %bitcast.13), channel_id=1, source_target_pairs={{0,480},{32,0},{64,32},{96,64},{128,96},{160,128},{192,160},{224,1... | collective-permute-start | bytes 786440 | tf_op jit(solution)/shard_map/ppermute | solution.py:261
  50.7 2.9 %collective-permute-start.2 = (bf16[64,1024]{1,0:T(8,128)(2,1)S(1)}, bf16[64,1024]{1,0:T(8,128)(2,1)S(1)}, u32[]{:S(2)}, u32[]{:S(2)}) collective-permute-start(bf16[64,1024]{1,0:T(8,128)(2,1)S(1)} %bitcast.19), channel_id=1, source_target_pairs={{0,448},{32,480},{64,0},{96,32},{128,64},{160,96},{192,128},{224,1... | collective-permute-start | bytes 393224 | tf_op jit(solution)/shard_map/ppermute | solution.py:261
  53.6 3.3 %collective-permute-start.3 = (bf16[64,1024]{1,0:T(8,128)(2,1)S(1)}, bf16[64,1024]{1,0:T(8,128)(2,1)S(1)}, u32[]{:S(2)}, u32[]{:S(2)}) collective-permute-start(bf16[64,1024]{1,0:T(8,128)(2,1)S(1)} %bitcast.18), channel_id=1, source_target_pairs={{0,64},{32,96},{64,128},{96,160},{128,192},{160,224},{192,256},{22... | collective-permute-start | bytes 393224 | tf_op jit(solution)/shard_map/ppermute | solution.py:261
  56.9 0.0 copy-done.4
  56.9 0.0 copy-start.3
  56.9 0.9 copy-done.3
  57.8 1.5 %shard_map.70.refs_5_ = f32[128,128]{1,0:T(8,128)S(1)} custom-call(s32[6]{0:T(128)S(1)} %stack.23.place_ref, s32[16,2048]{1,0:T(8,128)S(1)} %copy-done.3, s32[64,128]{1,0:T(8,128)S(1)} %bitcast.16), custom_call_target="tpu_custom_call" | custom-call | bytes 8388608 | tf_op jit(solution)/shard_map/pallas_call | solution.py:235
  59.3 0.0 collective-permute-done.refs_0_
  59.3 1.6 %shard_map.69 = (f32[128,128]{1,0:T(8,128)S(1)}, bf16[768,1024]{1,0:T(8,128)(2,1)S(1)}) custom-call(s32[6]{0:T(128)S(1)} %stack.23.place_ref, s32[16,2048]{1,0:T(8,128)S(1)} %copy-done.3, s32[64,128]{1,0:T(8,128)S(1)} %bitcast.17, bf16[784,1024]{1,0:T(8,128)(2,1)S(1)} %collective-permute-done.refs_0_), custom_call_target="tpu_custom_call" | custom-call | bytes 8388608 | tf_op jit(solution)/shard_map/pallas_call | solution.py:235
  61.0 0.0 collective-permute-done.2.refs_2_
  61.0 1.9 %collective-permute-done.3.refs_3_ = bf16[64,1024]{1,0:T(8,128)(2,1)S(1)} collective-permute-done((bf16[64,1024]{1,0:T(8,128)(2,1)S(1)}, bf16[64,1024]{1,0:T(8,128)(2,1)S(1)}, u32[]{:S(2)}, u32[]{:S(2)}) %collective-permute-start.3) | collective-permute-done | bytes 131104 | tf_op jit(solution)/shard_map/ppermute | solution.py:261
  62.8 0.0 collective-permute-done.4.refs_4_
  62.8 0.0 collective-permute-done.1.refs_1_
  62.8 5.6 %collective-permute-start.5 = (bf16[768,1024]{1,0:T(8,128)(2,1)S(1)}, bf16[768,1024]{1,0:T(8,128)(2,1)S(1)}, u32[]{:S(2)}, u32[]{:S(2)}) collective-permute-start(bf16[768,1024]{1,0:T(8,128)(2,1)S(1)} %get-tuple-element.33.refs_6_.first_ref), channel_id=1, source_target_pairs={{0,1},{1,0},{2,3},{3,2},{4,5},{5,4},{6,7},{7,6},{8,9},{9,8},{10,11... | collective-permute-start | bytes 4718600 | tf_op jit(solution)/shard_map/ppermute | solution.py:304
  68.4 0.0 copy-done.2
  68.4 2.6 %shard_map.71 = (f32[512,1536]{1,0:T(8,128)S(1)}, f32[2,1536]{1,0:T(2,128)S(1)}) custom-call(bf16[128,1024]{1,0:T(8,128)(2,1)S(1)} %bitcast.14, bf16[128,1024]{1,0:T(8,128)(2,1)S(1)} %collective-permute-done.1.refs_1_, bf16[64,1024]{1,0:T(8,128)(2,1)S(1)} %collective-permute-done.2.refs_2_, bf16[64,1024]{1,0:T(8,128)(2,1)S(1)} %collective-permute-done.3.refs_3_, ...), custom_call_target="tpu_custom_call" | custom-call | flops 1610612736 | bytes 6291456 | tf_op jit(solution)/shard_map/pallas_call | solution.py:235
  71.0 0.4 collective-permute-done.5.refs_7_.second_ref
  71.4 3.0 %shard_map.72 = (f32[512,1536]{1,0:T(8,128)S(1)}, f32[2,1536]{1,0:T(2,128)S(1)}, f32[2,1536]{1,0:T(2,128)S(1)}) custom-call(s32[6]{0:T(128)S(1)} %stack.23.place_ref, f32[2,1536]{1,0:T(2,128)S(1)} %get-tuple-element.31.old_ref.stat_a, bf16[128,1024]{1,0:T(8,128)(2,1)S(1)} %bitcast.15, bf16[128,1024]{1,0:T(8,128)(2,1)S(1)} %collective-permute-done.1.refs_1_, ...), custom_call_target="tpu_custom_call" | custom-call | flops 1610612736 | bytes 6291456 | tf_op jit(solution)/shard_map/pallas_call | solution.py:235
  74.5 0.1 broadcast_in_dim.7
  74.5 11.3 %all_to_all.21.all_ref = f32[16,2,1536]{2,1,0:T(2,128)S(1)} all-to-all(f32[16,2,1536]{2,1,0:T(2,128)S(1)} %broadcast_in_dim.7), channel_id=1, replica_groups=mesh['zh'=4,'zl'=4,'xh'=2,'xl'=2,'y'=4,'c'=2] {'xl','y','c'}, dimensions={0} | all-to-all | bytes 393216 | tf_op jit(solution)/shard_map/all_to_all | solution.py:318
  85.8 3.3 %shard_map.74 = (bf16[64,1152]{1,0:T(8,128)(2,1)S(1)}, bf16[64,1152]{1,0:T(8,128)(2,1)S(1)}, bf16[128,1152]{1,0:T(8,128)(2,1)S(1)}, bf16[128,1152]{1,0:T(8,128)(2,1)S(1)}) custom-call(s32[6]{0:T(128)S(1)} %stack.23.place_ref, f32[16,2,1536]{2,1,0:T(2,128)S(1)} %all_to_all.21.all_ref, bf16[1536,1024]{1,0:T(8,128)(2,1)S(1)} %copy-done.2, ...), custom_call_target="tpu_custom_call" | custom-call | flops 1610612736 | bytes 10485760 | tf_op jit(solution)/shard_map/pallas_call | solution.py:235
  89.2 1.9 %collective-permute-start.8 = (bf16[128,1152]{1,0:T(8,128)(2,1)S(1)}, bf16[128,1152]{1,0:T(8,128)(2,1)S(1)}, u32[]{:S(2)}, u32[]{:S(2)}) collective-permute-start(bf16[128,1152]{1,0:T(8,128)(2,1)S(1)} %get-tuple-element.40), channel_id=1, source_target_pairs={{0,32},{32,64},{64,96},{96,128},{128,160},{160,192},{192,224},{224... | collective-permute-start | bytes 884744 | tf_op jit(solution)/shard_map/ppermute | solution.py:261
  91.1 4.6 %collective-permute-start.9 = (bf16[128,1152]{1,0:T(8,128)(2,1)S(1)}, bf16[128,1152]{1,0:T(8,128)(2,1)S(1)}, u32[]{:S(2)}, u32[]{:S(2)}) collective-permute-start(bf16[128,1152]{1,0:T(8,128)(2,1)S(1)} %get-tuple-element.41), channel_id=1, source_target_pairs={{0,480},{32,0},{64,32},{96,64},{128,96},{160,128},{192,160},{224,1... | collective-permute-start | bytes 884744 | tf_op jit(solution)/shard_map/ppermute | solution.py:261
  95.7 2.0 %collective-permute-start.6 = (bf16[64,1152]{1,0:T(8,128)(2,1)S(1)}, bf16[64,1152]{1,0:T(8,128)(2,1)S(1)}, u32[]{:S(2)}, u32[]{:S(2)}) collective-permute-start(bf16[64,1152]{1,0:T(8,128)(2,1)S(1)} %get-tuple-element.38), channel_id=1, source_target_pairs={{0,64},{32,96},{64,128},{96,160},{128,192},{160,224},{192,256},{22... | collective-permute-start | bytes 442376 | tf_op jit(solution)/shard_map/ppermute | solution.py:261
  97.7 5.4 %collective-permute-start.7 = (bf16[64,1152]{1,0:T(8,128)(2,1)S(1)}, bf16[64,1152]{1,0:T(8,128)(2,1)S(1)}, u32[]{:S(2)}, u32[]{:S(2)}) collective-permute-start(bf16[64,1152]{1,0:T(8,128)(2,1)S(1)} %get-tuple-element.39), channel_id=1, source_target_pairs={{0,448},{32,480},{64,0},{96,32},{128,64},{160,96},{192,128},{224,1... | collective-permute-start | bytes 442376 | tf_op jit(solution)/shard_map/ppermute | solution.py:261
  103.1 1.7 %shard_map.73.a = bf16[128,1152]{1,0:T(8,128)(2,1)S(1)} custom-call(s32[6]{0:T(128)S(1)} %stack.23.place_ref, f32[16,2,1536]{2,1,0:T(2,128)S(1)} %all_to_all.21.all_ref, bf16[1536,1024]{1,0:T(8,128)(2,1)S(1)} %copy-done.2, bf16[768,1024]{1,0:T(8,128)(2,1)S(1)} %get-tuple-element.33.refs_6_.first_ref, ...), custom_call_target="tpu_custom_call" | custom-call | flops 1610612736 | bytes 10485760 | tf_op jit(solution)/shard_map/pallas_call | solution.py:235
  104.8 3.0 %collective-permute-done.6.low = bf16[64,1152]{1,0:T(8,128)(2,1)S(1)} collective-permute-done((bf16[64,1152]{1,0:T(8,128)(2,1)S(1)}, bf16[64,1152]{1,0:T(8,128)(2,1)S(1)}, u32[]{:S(2)}, u32[]{:S(2)}) %collective-permute-start.6) | collective-permute-done | bytes 147488 | tf_op jit(solution)/shard_map/ppermute | solution.py:261
  107.8 4.2 %collective-permute-done.7.high = bf16[64,1152]{1,0:T(8,128)(2,1)S(1)} collective-permute-done((bf16[64,1152]{1,0:T(8,128)(2,1)S(1)}, bf16[64,1152]{1,0:T(8,128)(2,1)S(1)}, u32[]{:S(2)}, u32[]{:S(2)}) %collective-permute-start.7) | collective-permute-done | bytes 147488 | tf_op jit(solution)/shard_map/ppermute | solution.py:261
  112.0 0.0 collective-permute-done.8.b
  112.0 0.0 collective-permute-done.9.c
  112.0 0.3 shard_map.75
  112.4 21.9 %all_to_all.22.ref = bf16[8,16,1152]{2,1,0:T(8,128)(2,1)S(1)} all-to-all(bf16[8,16,1152]{2,1,0:T(8,128)(2,1)S(1)} %bitcast.11), channel_id=1, replica_groups={{0,128,256,384,24,152,280,408},{8,136,264,392,16,144,272,400},{1,129,25..., dimensions={0} | all-to-all | bytes 589824 | tf_op jit(solution)/shard_map/all_to_all | solution.py:264
  134.2 0.2 shard_map.76
  134.4 13.8 %all_to_all.23.ref = bf16[8,16,1152]{2,1,0:T(8,128)(2,1)S(1)} all-to-all(bf16[8,16,1152]{2,1,0:T(8,128)(2,1)S(1)} %shard_map.76), channel_id=1, replica_groups=mesh['zh'=4,'zl'=4,'xh'=2,'xl'=2,'y'=4,'c'=2] {'y','c'}, dimensions={0} | all-to-all | bytes 589824 | tf_op jit(solution)/shard_map/all_to_all | solution.py:337
  148.2 0.8 shard_map.77
  (3 shorter events, 0.0 us)
Async XLA Ops:
  0.6 7.4 %copy-start = (bf16[128,1024]{1,0:T(8,128)(2,1)S(1)}, bf16[128,1024]{1,0:T(8,128)(2,1)}, u32[]{:S(2)}) copy-start(bf16[128,1024]{1,0:T(8,128)(2,1)} %param.9) | copy-start | bytes 786436
  1.4 1.9 %copy-start.1 = (bf16[1536,1024]{1,0:T(8,128)(2,1)S(1)}, bf16[1536,1024]{1,0:T(8,128)(2,1)}, u32[]{:S(2)}) copy-start(bf16[1536,1024]{1,0:T(8,128)(2,1)} %points_ref.5) | copy-start | bytes 9437188
  3.3 53.6 %copy-start.4 = (s32[8192]{0:T(1024)S(1)}, s32[8192]{0:T(1024)}, u32[]{:S(2)}) copy-start(s32[8192]{0:T(1024)} %param.8) | copy-start | bytes 98308
  4.0 55.3 %collective-permute-start = (bf16[784,1024]{1,0:T(8,128)(2,1)S(1)}, bf16[784,1024]{1,0:T(8,128)(2,1)S(1)}, u32[]{:S(2)}, u32[]{:S(2)}) collective-permute-start(bf16[784,1024]{1,0:T(8,128)(2,1)S(1)} %shard_map.68), channel_id=1, source_target_pairs={{0,8},{8,0},{1,9},{9,1},{2,10},{10,2},{3,11},{11,3},{4,12},{12,4},... | collective-permute-start | bytes 4816904 | tf_op jit(solution)/shard_map/ppermute | solution.py:281
  8.0 60.4 %copy-start.2 = (bf16[1536,1024]{1,0:T(8,128)(2,1)S(1)}, bf16[1536,1024]{1,0:T(8,128)(2,1)}, u32[]{:S(2)}) copy-start(bf16[1536,1024]{1,0:T(8,128)(2,1)} %points_ref.5) | copy-start | bytes 9437188
  39.1 23.7 %collective-permute-start.4 = (bf16[128,1024]{1,0:T(8,128)(2,1)S(1)}, bf16[128,1024]{1,0:T(8,128)(2,1)S(1)}, u32[]{:S(2)}, u32[]{:S(2)}) collective-permute-start(bf16[128,1024]{1,0:T(8,128)(2,1)S(1)} %bitcast.12), channel_id=1, source_target_pairs={{0,32},{32,64},{64,96},{96,128},{128,160},{160,192},{192,224},{224... | collective-permute-start | bytes 786440 | tf_op jit(solution)/shard_map/ppermute | solution.py:261
  48.7 14.1 %collective-permute-start.1 = (bf16[128,1024]{1,0:T(8,128)(2,1)S(1)}, bf16[128,1024]{1,0:T(8,128)(2,1)S(1)}, u32[]{:S(2)}, u32[]{:S(2)}) collective-permute-start(bf16[128,1024]{1,0:T(8,128)(2,1)S(1)} %bitcast.13), channel_id=1, source_target_pairs={{0,480},{32,0},{64,32},{96,64},{128,96},{160,128},{192,160},{224,1... | collective-permute-start | bytes 786440 | tf_op jit(solution)/shard_map/ppermute | solution.py:261
  50.7 10.3 %collective-permute-start.2 = (bf16[64,1024]{1,0:T(8,128)(2,1)S(1)}, bf16[64,1024]{1,0:T(8,128)(2,1)S(1)}, u32[]{:S(2)}, u32[]{:S(2)}) collective-permute-start(bf16[64,1024]{1,0:T(8,128)(2,1)S(1)} %bitcast.19), channel_id=1, source_target_pairs={{0,448},{32,480},{64,0},{96,32},{128,64},{160,96},{192,128},{224,1... | collective-permute-start | bytes 393224 | tf_op jit(solution)/shard_map/ppermute | solution.py:261
  53.6 9.2 %collective-permute-start.3 = (bf16[64,1024]{1,0:T(8,128)(2,1)S(1)}, bf16[64,1024]{1,0:T(8,128)(2,1)S(1)}, u32[]{:S(2)}, u32[]{:S(2)}) collective-permute-start(bf16[64,1024]{1,0:T(8,128)(2,1)S(1)} %bitcast.18), channel_id=1, source_target_pairs={{0,64},{32,96},{64,128},{96,160},{128,192},{160,224},{192,256},{22... | collective-permute-start | bytes 393224 | tf_op jit(solution)/shard_map/ppermute | solution.py:261
  56.9 0.9 copy-start.3
  62.8 8.6 %collective-permute-start.5 = (bf16[768,1024]{1,0:T(8,128)(2,1)S(1)}, bf16[768,1024]{1,0:T(8,128)(2,1)S(1)}, u32[]{:S(2)}, u32[]{:S(2)}) collective-permute-start(bf16[768,1024]{1,0:T(8,128)(2,1)S(1)} %get-tuple-element.33.refs_6_.first_ref), channel_id=1, source_target_pairs={{0,1},{1,0},{2,3},{3,2},{4,5},{5,4},{6,7},{7,6},{8,9},{9,8},{10,11... | collective-permute-start | bytes 4718600 | tf_op jit(solution)/shard_map/ppermute | solution.py:304
  89.2 22.9 %collective-permute-start.8 = (bf16[128,1152]{1,0:T(8,128)(2,1)S(1)}, bf16[128,1152]{1,0:T(8,128)(2,1)S(1)}, u32[]{:S(2)}, u32[]{:S(2)}) collective-permute-start(bf16[128,1152]{1,0:T(8,128)(2,1)S(1)} %get-tuple-element.40), channel_id=1, source_target_pairs={{0,32},{32,64},{64,96},{96,128},{128,160},{160,192},{192,224},{224... | collective-permute-start | bytes 884744 | tf_op jit(solution)/shard_map/ppermute | solution.py:261
  91.1 20.9 %collective-permute-start.9 = (bf16[128,1152]{1,0:T(8,128)(2,1)S(1)}, bf16[128,1152]{1,0:T(8,128)(2,1)S(1)}, u32[]{:S(2)}, u32[]{:S(2)}) collective-permute-start(bf16[128,1152]{1,0:T(8,128)(2,1)S(1)} %get-tuple-element.41), channel_id=1, source_target_pairs={{0,480},{32,0},{64,32},{96,64},{128,96},{160,128},{192,160},{224,1... | collective-permute-start | bytes 884744 | tf_op jit(solution)/shard_map/ppermute | solution.py:261
  95.7 12.1 %collective-permute-start.6 = (bf16[64,1152]{1,0:T(8,128)(2,1)S(1)}, bf16[64,1152]{1,0:T(8,128)(2,1)S(1)}, u32[]{:S(2)}, u32[]{:S(2)}) collective-permute-start(bf16[64,1152]{1,0:T(8,128)(2,1)S(1)} %get-tuple-element.38), channel_id=1, source_target_pairs={{0,64},{32,96},{64,128},{96,160},{128,192},{160,224},{192,256},{22... | collective-permute-start | bytes 442376 | tf_op jit(solution)/shard_map/ppermute | solution.py:261
  97.7 14.4 %collective-permute-start.7 = (bf16[64,1152]{1,0:T(8,128)(2,1)S(1)}, bf16[64,1152]{1,0:T(8,128)(2,1)S(1)}, u32[]{:S(2)}, u32[]{:S(2)}) collective-permute-start(bf16[64,1152]{1,0:T(8,128)(2,1)S(1)} %get-tuple-element.39), channel_id=1, source_target_pairs={{0,448},{32,480},{64,0},{96,32},{128,64},{160,96},{192,128},{224,1... | collective-permute-start | bytes 442376 | tf_op jit(solution)/shard_map/ppermute | solution.py:261

commit v11 on v10

--- a/solution.py
+++ b/solution.py
@@ -280,8 +280,7 @@
     )
     first = lax.ppermute(half, "xl", swap)
     own = lax.dynamic_slice(centroids, (n * rows, 0), (rows, width))
-    copies = jnp.broadcast_to(own, (peers, rows, width))
-    group = team_exchange(copies).reshape(size, width)
+    group = lax.all_gather(own, far, axis=0, axis_index_groups=teams, tiled=True)
     middle = size // 2
     two = [along(group[:middle], -2), along(group[middle:], 2)]
     pieces = [group, along(group, -1), *two, along(group, 1)]

time: 150 us -> 170 us (1.13)
  blocking collectives: 78 us -> 101 us
  waiting for transfers between devices: 9.59 us -> 5.46 us
  Pallas kernels: 15.8 us -> 17.7 us
    all_gather x0 -> x1, blocking collectives: none -> 47.4 us  [shards(): lax.all_gather(own, far, axis=0, axis_index_groups=teams, tiled=True)]
    all_to_all x2 -> x1, blocking collectives: 52.9 us -> 31.5 us  [team_exchange(): return lax.all_to_all(a, far, 0, 0, axis_index_groups=teams, tiled=True)]
    ppermute x8, waiting for transfers between devices: 9.15 us -> 4.96 us  [along(): return lax.ppermute(a, deep, [(i, (i + by) % zs) for i in range(zs)])]
    ppermute x8, starting transfers between devices: 31.6 us -> 27.8 us  [along(): return lax.ppermute(a, deep, [(i, (i + by) % zs) for i in range(zs)])]
    ppermute x1, starting transfers between devices: 5.55 us -> 8.87 us  [shards(): second = lax.ppermute(first, 'c', swap)]
    all_to_all x1, blocking collectives: 13.8 us -> 10.6 us  [shards(): whole = lax.all_to_all(table, narrow, 0, 0, tiled=True)]
    pallas_call x10, Pallas kernels: 15.8 us -> 17.7 us  [call(): pl.pallas_call(kernel, out_shape=outs, in_specs=specs or vmem(len(args)),...]
  transfers between devices with their start and end apart: 10 -> 10, of which waited for: 4 -> 2; matrix products, arithmetic and copies ran while one was open for 0% -> 0% of each run, Pallas kernels for 5% -> 5%
where the time goes in v11:
time: 170 us; the launch traced here: 169 us
  blocking collectives  101 us (59%)
  starting transfers between devices  40.6 us (24%)
  Pallas kernels  17.7 us (10%)
  waiting for transfers between devices  5.46 us (3%)
  local copies, waits for them, and re-layouts  2.83 us (2%)
    all_gather x1, blocking collectives, shards(): lax.all_gather(own, far, axis=0, axis_index_groups=teams, tiled=True)  47.4 us
    all_to_all x1, blocking collectives, team_exchange(): return lax.all_to_all(a, far, 0, 0, axis_index_groups=teams, tiled=True)  31.5 us
    ppermute x8, starting transfers between devices, along(): return lax.ppermute(a, deep, [(i, (i + by) % zs) for i in range(zs)])  27.8 us
    pallas_call x10, Pallas kernels, call(): pl.pallas_call(kernel, out_shape=outs, in_specs=specs or vmem(len(args)),...  17.7 us
    all_to_all x1, blocking collectives, shards(): shared = lax.all_to_all(copies, pool, 0, 0, tiled=True)  11.3 us
    all_to_all x1, blocking collectives, shards(): whole = lax.all_to_all(table, narrow, 0, 0, tiled=True)  10.6 us
    ppermute x1, starting transfers between devices, shards(): second = lax.ppermute(first, 'c', swap)  8.87 us
    ppermute x8, waiting for transfers between devices, along(): return lax.ppermute(a, deep, [(i, (i + by) % zs) for i in range(zs)])  4.96 us
  transfers between devices with their start and end apart: 10, of which 2 were waited for; matrix products, arithmetic and copies ran while one was open for 0% of the time, Pallas kernels for 5%

profile of v11, /device:TPU:1, one launch (start us, length us, event | category | flops | bytes accessed | tf_op | source)
XLA Modules:
  0.0 169.0 jit_solution(11166386858208236696)
XLA Ops:
  0.6 0.0 copy-start
  1.3 0.1 stack.23.place_ref
  1.4 0.0 copy-start.1
  1.4 1.9 %copy-done.1 = bf16[1536,1024]{1,0:T(8,128)(2,1)S(1)} copy-done((bf16[1536,1024]{1,0:T(8,128)(2,1)S(1)}, bf16[1536,1024]{1,0:T(8,128)(2,1)}, u32[]{:S(2)}) %copy-start.1) | copy-done | bytes 3145752
  3.3 0.0 copy-start.3
  3.3 0.0 copy-start.2
  3.3 1.7 %shard_map.68 = bf16[784,1024]{1,0:T(8,128)(2,1)} custom-call(s32[6]{0:T(128)S(1)} %stack.23.place_ref, bf16[1536,1024]{1,0:T(8,128)(2,1)S(1)} %copy-done.1), custom_call_target="tpu_custom_call" | custom-call | bytes 3145728 | tf_op jit(solution)/shard_map/pallas_call | solution.py:235
  5.1 4.0 %collective-permute-start = (bf16[784,1024]{1,0:T(8,128)(2,1)}, bf16[784,1024]{1,0:T(8,128)(2,1)}, u32[]{:S(2)}, u32[]{:S(2)}) collective-permute-start(bf16[784,1024]{1,0:T(8,128)(2,1)} %shard_map.68), channel_id=1, source_target_pairs={{0,8},{8,0},{1,9},{9,1},{2,10},{10,2},{3,11},{11,3},{4,12},{12,4},... | collective-permute-start | bytes 4816904 | tf_op jit(solution)/shard_map/ppermute | solution.py:281
  9.0 0.0 copy-done
  9.1 47.4 %all_gather.3.refs_0_ = bf16[128,1024]{1,0:T(8,128)(2,1)S(1)} all-gather(bf16[16,1024]{1,0:T(8,128)(2,1)S(1)} %constant_dynamic-slice_fusion.cen), channel_id=1, replica_groups={{0,128,256,384,24,152,280,408},{8,136,264,392,16,144,272,400},{1,129,25..., dimensions={0}, use_global_device_ids=true | all-gather | bytes 294912 | tf_op jit(solution)/shard_map/all_gather | solution.py:283
  56.5 1.9 %collective-permute-start.4 = (bf16[128,1024]{1,0:T(8,128)(2,1)S(1)}, bf16[128,1024]{1,0:T(8,128)(2,1)S(1)}, u32[]{:S(2)}, u32[]{:S(2)}) collective-permute-start(bf16[128,1024]{1,0:T(8,128)(2,1)S(1)} %all_gather.3.refs_0_), channel_id=1, source_target_pairs={{0,32},{32,64},{64,96},{96,128},{128,160},{160,192},{192,224},{224... | collective-permute-start | bytes 786440 | tf_op jit(solution)/shard_map/ppermute | solution.py:261
  58.4 4.6 %collective-permute-start.1 = (bf16[128,1024]{1,0:T(8,128)(2,1)S(1)}, bf16[128,1024]{1,0:T(8,128)(2,1)S(1)}, u32[]{:S(2)}, u32[]{:S(2)}) collective-permute-start(bf16[128,1024]{1,0:T(8,128)(2,1)S(1)} %all_gather.3.refs_0_), channel_id=1, source_target_pairs={{0,480},{32,0},{64,32},{96,64},{128,96},{160,128},{192,160},{224,1... | collective-permute-start | bytes 786440 | tf_op jit(solution)/shard_map/ppermute | solution.py:261
  63.0 1.9 %collective-permute-start.3 = (bf16[64,1024]{1,0:T(8,128)(2,1)S(1)}, bf16[64,1024]{1,0:T(8,128)(2,1)S(1)}, u32[]{:S(2)}, u32[]{:S(2)}) collective-permute-start(bf16[64,1024]{1,0:T(8,128)(2,1)S(1)} %get-tuple-element.44), channel_id=1, source_target_pairs={{0,64},{32,96},{64,128},{96,160},{128,192},{160,224},{192,256},{22... | collective-permute-start | bytes 393224 | tf_op jit(solution)/shard_map/ppermute | solution.py:261
  64.9 5.5 %collective-permute-start.2 = (bf16[64,1024]{1,0:T(8,128)(2,1)S(1)}, bf16[64,1024]{1,0:T(8,128)(2,1)S(1)}, u32[]{:S(2)}, u32[]{:S(2)}) collective-permute-start(bf16[64,1024]{1,0:T(8,128)(2,1)S(1)} %get-tuple-element.45), channel_id=1, source_target_pairs={{0,448},{32,480},{64,0},{96,32},{128,64},{160,96},{192,128},{224,1... | collective-permute-start | bytes 393224 | tf_op jit(solution)/shard_map/ppermute | solution.py:261
  70.4 0.0 copy-done.3
  70.4 0.0 copy-start.4
  70.4 0.7 copy-done.4
  71.2 1.5 shard_map.70.refs_5_
  72.7 0.0 collective-permute-done.refs_0_
  72.7 2.5 %shard_map.69 = (f32[128,128]{1,0:T(8,128)S(1)}, bf16[768,1024]{1,0:T(8,128)(2,1)S(1)}) custom-call(s32[6]{0:T(128)S(1)} %stack.23.place_ref, s32[16,2048]{1,0:T(8,128)S(1)} %copy-done.3, s32[64,128]{1,0:T(8,128)S(1)} %bitcast.10, bf16[784,1024]{1,0:T(8,128)(2,1)} %collective-permute-done.refs_0_), custom_call_target="tpu_custom_call" | custom-call | bytes 8388608 | tf_op jit(solution)/shard_map/pallas_call | solution.py:235
  75.2 0.0 collective-permute-done.3.refs_3_
  75.2 0.0 collective-permute-done.2.refs_2_
  75.2 0.0 collective-permute-done.4.refs_4_
  75.3 0.0 collective-permute-done.1.refs_1_
  75.3 8.9 %collective-permute-start.5 = (bf16[768,1024]{1,0:T(8,128)(2,1)S(1)}, bf16[768,1024]{1,0:T(8,128)(2,1)S(1)}, u32[]{:S(2)}, u32[]{:S(2)}) collective-permute-start(bf16[768,1024]{1,0:T(8,128)(2,1)S(1)} %get-tuple-element.33.refs_6_.first_ref), channel_id=1, source_target_pairs={{0,1},{1,0},{2,3},{3,2},{4,5},{5,4},{6,7},{7,6},{8,9},{9,8},{10,11... | collective-permute-start | bytes 4718600 | tf_op jit(solution)/shard_map/ppermute | solution.py:303
  84.1 0.0 copy-done.2
  84.2 2.5 %shard_map.71 = (f32[512,1536]{1,0:T(8,128)S(1)}, f32[2,1536]{1,0:T(2,128)S(1)}) custom-call(bf16[128,1024]{1,0:T(8,128)(2,1)S(1)} %all_gather.3.refs_0_, bf16[128,1024]{1,0:T(8,128)(2,1)S(1)} %collective-permute-done.1.refs_1_, bf16[64,1024]{1,0:T(8,128)(2,1)S(1)} %collective-permute-done.2.refs_2_, bf16[64,1024]{1,0:T(8,128)(2,1)S(1)} %collective-permute-done.3.refs_3_, ...), custom_call_target="tpu_custom_call" | custom-call | flops 1610612736 | bytes 6291456 | tf_op jit(solution)/shard_map/pallas_call | solution.py:235
  86.7 0.5 collective-permute-done.5.refs_7_.second_ref
  87.2 3.0 %shard_map.72 = (f32[512,1536]{1,0:T(8,128)S(1)}, f32[2,1536]{1,0:T(2,128)S(1)}, f32[2,1536]{1,0:T(2,128)S(1)}) custom-call(s32[6]{0:T(128)S(1)} %stack.23.place_ref, f32[2,1536]{1,0:T(2,128)S(1)} %get-tuple-element.31.old_ref.stat_a, bf16[128,1024]{1,0:T(8,128)(2,1)S(1)} %all_gather.3.refs_0_, bf16[128,1024]{1,0:T(8,128)(2,1)S(1)} %collective-permute-done.1.refs_1_, ...), custom_call_target="tpu_custom_call" | custom-call | flops 1610612736 | bytes 6291456 | tf_op jit(solution)/shard_map/pallas_call | solution.py:235
  90.2 0.1 broadcast_in_dim.3
  90.3 11.3 %all_to_all.15.all_ref = f32[16,2,1536]{2,1,0:T(2,128)S(1)} all-to-all(f32[16,2,1536]{2,1,0:T(2,128)S(1)} %broadcast_in_dim.3), channel_id=1, replica_groups=mesh['zh'=4,'zl'=4,'xh'=2,'xl'=2,'y'=4,'c'=2] {'xl','y','c'}, dimensions={0} | all-to-all | bytes 393216 | tf_op jit(solution)/shard_map/all_to_all | solution.py:317
  101.6 3.3 %shard_map.74 = (bf16[64,1152]{1,0:T(8,128)(2,1)S(1)}, bf16[64,1152]{1,0:T(8,128)(2,1)S(1)}, bf16[128,1152]{1,0:T(8,128)(2,1)S(1)}, bf16[128,1152]{1,0:T(8,128)(2,1)S(1)}) custom-call(s32[6]{0:T(128)S(1)} %stack.23.place_ref, f32[16,2,1536]{2,1,0:T(2,128)S(1)} %all_to_all.15.all_ref, bf16[1536,1024]{1,0:T(8,128)(2,1)S(1)} %copy-done.2, ...), custom_call_target="tpu_custom_call" | custom-call | flops 1610612736 | bytes 10485760 | tf_op jit(solution)/shard_map/pallas_call | solution.py:235
  104.9 1.9 %collective-permute-start.8 = (bf16[128,1152]{1,0:T(8,128)(2,1)S(1)}, bf16[128,1152]{1,0:T(8,128)(2,1)S(1)}, u32[]{:S(2)}, u32[]{:S(2)}) collective-permute-start(bf16[128,1152]{1,0:T(8,128)(2,1)S(1)} %get-tuple-element.40), channel_id=1, source_target_pairs={{0,32},{32,64},{64,96},{96,128},{128,160},{160,192},{192,224},{224... | collective-permute-start | bytes 884744 | tf_op jit(solution)/shard_map/ppermute | solution.py:261
  106.9 4.6 %collective-permute-start.9 = (bf16[128,1152]{1,0:T(8,128)(2,1)S(1)}, bf16[128,1152]{1,0:T(8,128)(2,1)S(1)}, u32[]{:S(2)}, u32[]{:S(2)}) collective-permute-start(bf16[128,1152]{1,0:T(8,128)(2,1)S(1)} %get-tuple-element.41), channel_id=1, source_target_pairs={{0,480},{32,0},{64,32},{96,64},{128,96},{160,128},{192,160},{224,1... | collective-permute-start | bytes 884744 | tf_op jit(solution)/shard_map/ppermute | solution.py:261
  111.4 2.5 %collective-permute-start.6 = (bf16[64,1152]{1,0:T(8,128)(2,1)S(1)}, bf16[64,1152]{1,0:T(8,128)(2,1)S(1)}, u32[]{:S(2)}, u32[]{:S(2)}) collective-permute-start(bf16[64,1152]{1,0:T(8,128)(2,1)S(1)} %get-tuple-element.38), channel_id=1, source_target_pairs={{0,64},{32,96},{64,128},{96,160},{128,192},{160,224},{192,256},{22... | collective-permute-start | bytes 442376 | tf_op jit(solution)/shard_map/ppermute | solution.py:261
  114.0 4.8 %collective-permute-start.7 = (bf16[64,1152]{1,0:T(8,128)(2,1)S(1)}, bf16[64,1152]{1,0:T(8,128)(2,1)S(1)}, u32[]{:S(2)}, u32[]{:S(2)}) collective-permute-start(bf16[64,1152]{1,0:T(8,128)(2,1)S(1)} %get-tuple-element.39), channel_id=1, source_target_pairs={{0,448},{32,480},{64,0},{96,32},{128,64},{160,96},{192,128},{224,1... | collective-permute-start | bytes 442376 | tf_op jit(solution)/shard_map/ppermute | solution.py:261
  118.8 1.7 shard_map.73.a
  120.5 0.0 collective-permute-done.6.low
  120.6 4.9 %collective-permute-done.7.high = bf16[64,1152]{1,0:T(8,128)(2,1)S(1)} collective-permute-done((bf16[64,1152]{1,0:T(8,128)(2,1)S(1)}, bf16[64,1152]{1,0:T(8,128)(2,1)S(1)}, u32[]{:S(2)}, u32[]{:S(2)}) %collective-permute-start.7) | collective-permute-done | bytes 147488 | tf_op jit(solution)/shard_map/ppermute | solution.py:261
  125.5 0.0 collective-permute-done.8.b
  125.5 0.0 collective-permute-done.9.c
  125.5 0.3 shard_map.75
  125.8 31.5 %all_to_all.16.ref = bf16[8,16,1152]{2,1,0:T(8,128)(2,1)S(1)} all-to-all(bf16[8,16,1152]{2,1,0:T(8,128)(2,1)S(1)} %bitcast.8), channel_id=1, replica_groups={{0,128,256,384,24,152,280,408},{8,136,264,392,16,144,272,400},{1,129,25..., dimensions={0} | all-to-all | bytes 589824 | tf_op jit(solution)/shard_map/all_to_all | solution.py:264
  157.4 0.2 shard_map.76
  157.5 10.6 %all_to_all.17.ref = bf16[8,16,1152]{2,1,0:T(8,128)(2,1)S(1)} all-to-all(bf16[8,16,1152]{2,1,0:T(8,128)(2,1)S(1)} %shard_map.76), channel_id=1, replica_groups=mesh['zh'=4,'zl'=4,'xh'=2,'xl'=2,'y'=4,'c'=2] {'y','c'}, dimensions={0} | all-to-all | bytes 589824 | tf_op jit(solution)/shard_map/all_to_all | solution.py:336
  168.2 0.8 shard_map.77
  (2 shorter events, 0.0 us)
Async XLA Ops:
  0.6 8.4 %copy-start = (bf16[128,1024]{1,0:T(8,128)(2,1)S(1)}, bf16[128,1024]{1,0:T(8,128)(2,1)}, u32[]{:S(2)}) copy-start(bf16[128,1024]{1,0:T(8,128)(2,1)} %param.9) | copy-start | bytes 786436
  1.4 1.9 %copy-start.1 = (bf16[1536,1024]{1,0:T(8,128)(2,1)S(1)}, bf16[1536,1024]{1,0:T(8,128)(2,1)}, u32[]{:S(2)}) copy-start(bf16[1536,1024]{1,0:T(8,128)(2,1)} %points_ref.5) | copy-start | bytes 9437188
  3.3 67.1 %copy-start.3 = (s32[16,2048]{1,0:T(8,128)S(1)}, s32[16,2048]{1,0:T(8,128)}, u32[]{:S(2)}) copy-start(s32[16,2048]{1,0:T(8,128)} %lists_ref.3) | copy-start | bytes 393220
  3.3 80.8 %copy-start.2 = (bf16[1536,1024]{1,0:T(8,128)(2,1)S(1)}, bf16[1536,1024]{1,0:T(8,128)(2,1)}, u32[]{:S(2)}) copy-start(bf16[1536,1024]{1,0:T(8,128)(2,1)} %points_ref.5) | copy-start | bytes 9437188
  5.1 67.6 %collective-permute-start = (bf16[784,1024]{1,0:T(8,128)(2,1)}, bf16[784,1024]{1,0:T(8,128)(2,1)}, u32[]{:S(2)}, u32[]{:S(2)}) collective-permute-start(bf16[784,1024]{1,0:T(8,128)(2,1)} %shard_map.68), channel_id=1, source_target_pairs={{0,8},{8,0},{1,9},{9,1},{2,10},{10,2},{3,11},{11,3},{4,12},{12,4},... | collective-permute-start | bytes 4816904 | tf_op jit(solution)/shard_map/ppermute | solution.py:281
  56.5 18.8 %collective-permute-start.4 = (bf16[128,1024]{1,0:T(8,128)(2,1)S(1)}, bf16[128,1024]{1,0:T(8,128)(2,1)S(1)}, u32[]{:S(2)}, u32[]{:S(2)}) collective-permute-start(bf16[128,1024]{1,0:T(8,128)(2,1)S(1)} %all_gather.3.refs_0_), channel_id=1, source_target_pairs={{0,32},{32,64},{64,96},{96,128},{128,160},{160,192},{192,224},{224... | collective-permute-start | bytes 786440 | tf_op jit(solution)/shard_map/ppermute | solution.py:261
  58.4 16.9 %collective-permute-start.1 = (bf16[128,1024]{1,0:T(8,128)(2,1)S(1)}, bf16[128,1024]{1,0:T(8,128)(2,1)S(1)}, u32[]{:S(2)}, u32[]{:S(2)}) collective-permute-start(bf16[128,1024]{1,0:T(8,128)(2,1)S(1)} %all_gather.3.refs_0_), channel_id=1, source_target_pairs={{0,480},{32,0},{64,32},{96,64},{128,96},{160,128},{192,160},{224,1... | collective-permute-start | bytes 786440 | tf_op jit(solution)/shard_map/ppermute | solution.py:261
  63.0 12.2 %collective-permute-start.3 = (bf16[64,1024]{1,0:T(8,128)(2,1)S(1)}, bf16[64,1024]{1,0:T(8,128)(2,1)S(1)}, u32[]{:S(2)}, u32[]{:S(2)}) collective-permute-start(bf16[64,1024]{1,0:T(8,128)(2,1)S(1)} %get-tuple-element.44), channel_id=1, source_target_pairs={{0,64},{32,96},{64,128},{96,160},{128,192},{160,224},{192,256},{22... | collective-permute-start | bytes 393224 | tf_op jit(solution)/shard_map/ppermute | solution.py:261
  64.9 10.3 %collective-permute-start.2 = (bf16[64,1024]{1,0:T(8,128)(2,1)S(1)}, bf16[64,1024]{1,0:T(8,128)(2,1)S(1)}, u32[]{:S(2)}, u32[]{:S(2)}) collective-permute-start(bf16[64,1024]{1,0:T(8,128)(2,1)S(1)} %get-tuple-element.45), channel_id=1, source_target_pairs={{0,448},{32,480},{64,0},{96,32},{128,64},{160,96},{192,128},{224,1... | collective-permute-start | bytes 393224 | tf_op jit(solution)/shard_map/ppermute | solution.py:261
  70.4 0.8 copy-start.4
  75.3 11.9 %collective-permute-start.5 = (bf16[768,1024]{1,0:T(8,128)(2,1)S(1)}, bf16[768,1024]{1,0:T(8,128)(2,1)S(1)}, u32[]{:S(2)}, u32[]{:S(2)}) collective-permute-start(bf16[768,1024]{1,0:T(8,128)(2,1)S(1)} %get-tuple-element.33.refs_6_.first_ref), channel_id=1, source_target_pairs={{0,1},{1,0},{2,3},{3,2},{4,5},{5,4},{6,7},{7,6},{8,9},{9,8},{10,11... | collective-permute-start | bytes 4718600 | tf_op jit(solution)/shard_map/ppermute | solution.py:303
  104.9 20.6 %collective-permute-start.8 = (bf16[128,1152]{1,0:T(8,128)(2,1)S(1)}, bf16[128,1152]{1,0:T(8,128)(2,1)S(1)}, u32[]{:S(2)}, u32[]{:S(2)}) collective-permute-start(bf16[128,1152]{1,0:T(8,128)(2,1)S(1)} %get-tuple-element.40), channel_id=1, source_target_pairs={{0,32},{32,64},{64,96},{96,128},{128,160},{160,192},{192,224},{224... | collective-permute-start | bytes 884744 | tf_op jit(solution)/shard_map/ppermute | solution.py:261
  106.9 18.6 %collective-permute-start.9 = (bf16[128,1152]{1,0:T(8,128)(2,1)S(1)}, bf16[128,1152]{1,0:T(8,128)(2,1)S(1)}, u32[]{:S(2)}, u32[]{:S(2)}) collective-permute-start(bf16[128,1152]{1,0:T(8,128)(2,1)S(1)} %get-tuple-element.41), channel_id=1, source_target_pairs={{0,480},{32,0},{64,32},{96,64},{128,96},{160,128},{192,160},{224,1... | collective-permute-start | bytes 884744 | tf_op jit(solution)/shard_map/ppermute | solution.py:261
  111.4 9.1 %collective-permute-start.6 = (bf16[64,1152]{1,0:T(8,128)(2,1)S(1)}, bf16[64,1152]{1,0:T(8,128)(2,1)S(1)}, u32[]{:S(2)}, u32[]{:S(2)}) collective-permute-start(bf16[64,1152]{1,0:T(8,128)(2,1)S(1)} %get-tuple-element.38), channel_id=1, source_target_pairs={{0,64},{32,96},{64,128},{96,160},{128,192},{160,224},{192,256},{22... | collective-permute-start | bytes 442376 | tf_op jit(solution)/shard_map/ppermute | solution.py:261
  114.0 11.5 %collective-permute-start.7 = (bf16[64,1152]{1,0:T(8,128)(2,1)S(1)}, bf16[64,1152]{1,0:T(8,128)(2,1)S(1)}, u32[]{:S(2)}, u32[]{:S(2)}) collective-permute-start(bf16[64,1152]{1,0:T(8,128)(2,1)S(1)} %get-tuple-element.39), channel_id=1, source_target_pairs={{0,448},{32,480},{64,0},{96,32},{128,64},{160,96},{192,128},{224,1... | collective-permute-start | bytes 442376 | tf_op jit(solution)/shard_map/ppermute | solution.py:261

commit v12 on v10

--- a/solution.py
+++ b/solution.py
@@ -152,22 +152,22 @@
     me, core = place_ref[2], place_ref[3]
     half = points_ref.shape[0] // 2
     width = points_ref.shape[1]
-    for slab, which in enumerate((me, 1 - me)):
-        each = [all_ref[k, pl.ds(which, 1), :] for k in range(all_ref.shape[0])]
-        top = functools.reduce(jnp.maximum, each)
-        total = functools.reduce(jnp.add, [jnp.exp(one - top) for one in each])
-        norm_ref[slab] = top + jnp.log(total)
+    each = [all_ref[k] for k in range(all_ref.shape[0])]
+    top = functools.reduce(jnp.maximum, each)
+    total = functools.reduce(jnp.add, [jnp.exp(one - top) for one in each])
+    norm_ref[...] = top + jnp.log(total)
+    mine, theirs = pl.ds(me, 1), pl.ds(1 - me, 1)
 
     def shares(expo, stat, lanes, norm):
         scale = jnp.exp(stat[0:1, lanes] - norm)
         rows = [expo[j * lane : (j + 1) * lane, lanes] for j in groups]
         return jnp.concatenate([(row * scale).astype(bf16) for row in rows])
 
-    parts = [shares(expo_a, stat_a, slice(None), norm_ref[0])]
+    parts = [shares(expo_a, stat_a, slice(None), norm_ref[mine, :])]
     for h in range(2):
         from_ = pl.ds(pl.multiple_of((core if h == 0 else 1 - core) * half, lane), half)
         at = slice(h * half, (h + 1) * half)
-        parts.append(shares(expo_b, stat_b, at, norm_ref[1, :, from_]))
+        parts.append(shares(expo_b, stat_b, at, norm_ref[theirs, from_]))
     step = 256
     for c in range(width // step):
         at = slice(c * step, (c + 1) * step)
@@ -325,7 +325,7 @@
             smem + vmem(8),
             flops=flops,
             moved=10 << 20,
-            scratch=[pltpu.VMEM((2, 1, count), f32)],
+            scratch=[pltpu.VMEM((2, count), f32)],
         )
 
     low, high, one, three = sums((2, 1, 3), (size // 2, size // 2, size, size))

time: 150 us -> 150 us (level)
  no operation moved by 1% of the time
where the time goes in v12:
time: 150 us; the launch traced here: 149 us
  blocking collectives  78 us (52%)
  starting transfers between devices  41.1 us (27%)
  Pallas kernels  15.8 us (11%)
  waiting for transfers between devices  9.6 us (6%)
  local copies, waits for them, and re-layouts  3 us (2%)
  between operations  1.57 us (1%)
    all_to_all x2, blocking collectives, team_exchange(): return lax.all_to_all(a, far, 0, 0, axis_index_groups=teams, tiled=True)  52.9 us
    ppermute x8, starting transfers between devices, along(): return lax.ppermute(a, deep, [(i, (i + by) % zs) for i in range(zs)])  31.6 us
    pallas_call x10, Pallas kernels, call(): pl.pallas_call(kernel, out_shape=outs, in_specs=specs or vmem(len(args)),...  15.8 us
    all_to_all x1, blocking collectives, shards(): whole = lax.all_to_all(table, narrow, 0, 0, tiled=True)  13.8 us
    all_to_all x1, blocking collectives, shards(): shared = lax.all_to_all(copies, pool, 0, 0, tiled=True)  11.3 us
    ppermute x8, waiting for transfers between devices, along(): return lax.ppermute(a, deep, [(i, (i + by) % zs) for i in range(zs)])  9.16 us
    ppermute x1, starting transfers between devices, shards(): second = lax.ppermute(first, 'c', swap)  5.55 us
    ppermute x1, starting transfers between devices, shards(): first = lax.ppermute(half, 'xl', swap)  3.95 us
  transfers between devices with their start and end apart: 10, of which 4 were waited for; matrix products, arithmetic and copies ran while one was open for 0% of the time, Pallas kernels for 5%

profile of v12, /device:TPU:1, one launch (start us, length us, event | category | flops | bytes accessed | tf_op | source)
XLA Modules:
  0.0 149.0 jit_solution(3642132174614056433)
XLA Ops:
  0.6 0.0 copy-start
  1.3 0.1 stack.23.place_ref
  1.4 0.0 copy-start.1
  1.4 1.9 %copy-done.1 = bf16[1536,1024]{1,0:T(8,128)(2,1)S(1)} copy-done((bf16[1536,1024]{1,0:T(8,128)(2,1)S(1)}, bf16[1536,1024]{1,0:T(8,128)(2,1)}, u32[]{:S(2)}) %copy-start.1) | copy-done | bytes 3145752
  3.3 0.0 copy-start.4
  3.3 0.7 shard_map.68
  4.0 3.9 %collective-permute-start = (bf16[784,1024]{1,0:T(8,128)(2,1)S(1)}, bf16[784,1024]{1,0:T(8,128)(2,1)S(1)}, u32[]{:S(2)}, u32[]{:S(2)}) collective-permute-start(bf16[784,1024]{1,0:T(8,128)(2,1)S(1)} %shard_map.68), channel_id=1, source_target_pairs={{0,8},{8,0},{1,9},{9,1},{2,10},{10,2},{3,11},{11,3},{4,12},{12,4},... | collective-permute-start | bytes 4816904 | tf_op jit(solution)/shard_map/ppermute | solution.py:281
  8.0 0.0 copy-done
  8.0 0.0 copy-start.2
  8.1 31.1 %all_to_all.20 = bf16[8,16,1024]{2,1,0:T(8,128)(2,1)S(1)} all-to-all(bf16[8,16,1024]{2,1,0:T(8,128)(2,1)S(1)} %broadcast_in_dim.6), channel_id=1, replica_groups={{0,128,256,384,24,152,280,408},{8,136,264,392,16,144,272,400},{1,129,25..., dimensions={0} | all-to-all | bytes 524288 | tf_op jit(solution)/shard_map/all_to_all | solution.py:264
  39.1 9.6 %collective-permute-start.4 = (bf16[128,1024]{1,0:T(8,128)(2,1)S(1)}, bf16[128,1024]{1,0:T(8,128)(2,1)S(1)}, u32[]{:S(2)}, u32[]{:S(2)}) collective-permute-start(bf16[128,1024]{1,0:T(8,128)(2,1)S(1)} %bitcast.12), channel_id=1, source_target_pairs={{0,32},{32,64},{64,96},{96,128},{128,160},{160,192},{192,224},{224... | collective-permute-start | bytes 786440 | tf_op jit(solution)/shard_map/ppermute | solution.py:261
  48.7 1.9 %collective-permute-start.1 = (bf16[128,1024]{1,0:T(8,128)(2,1)S(1)}, bf16[128,1024]{1,0:T(8,128)(2,1)S(1)}, u32[]{:S(2)}, u32[]{:S(2)}) collective-permute-start(bf16[128,1024]{1,0:T(8,128)(2,1)S(1)} %bitcast.13), channel_id=1, source_target_pairs={{0,480},{32,0},{64,32},{96,64},{128,96},{160,128},{192,160},{224,1... | collective-permute-start | bytes 786440 | tf_op jit(solution)/shard_map/ppermute | solution.py:261
  50.7 2.9 %collective-permute-start.2 = (bf16[64,1024]{1,0:T(8,128)(2,1)S(1)}, bf16[64,1024]{1,0:T(8,128)(2,1)S(1)}, u32[]{:S(2)}, u32[]{:S(2)}) collective-permute-start(bf16[64,1024]{1,0:T(8,128)(2,1)S(1)} %bitcast.19), channel_id=1, source_target_pairs={{0,448},{32,480},{64,0},{96,32},{128,64},{160,96},{192,128},{224,1... | collective-permute-start | bytes 393224 | tf_op jit(solution)/shard_map/ppermute | solution.py:261
  53.6 3.3 %collective-permute-start.3 = (bf16[64,1024]{1,0:T(8,128)(2,1)S(1)}, bf16[64,1024]{1,0:T(8,128)(2,1)S(1)}, u32[]{:S(2)}, u32[]{:S(2)}) collective-permute-start(bf16[64,1024]{1,0:T(8,128)(2,1)S(1)} %bitcast.18), channel_id=1, source_target_pairs={{0,64},{32,96},{64,128},{96,160},{128,192},{160,224},{192,256},{22... | collective-permute-start | bytes 393224 | tf_op jit(solution)/shard_map/ppermute | solution.py:261
  56.9 0.0 copy-done.4
  56.9 0.0 copy-start.3
  56.9 0.9 copy-done.3
  57.8 1.5 %shard_map.70.refs_5_ = f32[128,128]{1,0:T(8,128)S(1)} custom-call(s32[6]{0:T(128)S(1)} %stack.23.place_ref, s32[16,2048]{1,0:T(8,128)S(1)} %copy-done.3, s32[64,128]{1,0:T(8,128)S(1)} %bitcast.16), custom_call_target="tpu_custom_call" | custom-call | bytes 8388608 | tf_op jit(solution)/shard_map/pallas_call | solution.py:235
  59.3 0.0 collective-permute-done.refs_0_
  59.3 1.6 %shard_map.69 = (f32[128,128]{1,0:T(8,128)S(1)}, bf16[768,1024]{1,0:T(8,128)(2,1)S(1)}) custom-call(s32[6]{0:T(128)S(1)} %stack.23.place_ref, s32[16,2048]{1,0:T(8,128)S(1)} %copy-done.3, s32[64,128]{1,0:T(8,128)S(1)} %bitcast.17, bf16[784,1024]{1,0:T(8,128)(2,1)S(1)} %collective-permute-done.refs_0_), custom_call_target="tpu_custom_call" | custom-call | bytes 8388608 | tf_op jit(solution)/shard_map/pallas_call | solution.py:235
  61.0 0.0 collective-permute-done.2.refs_2_
  61.0 1.9 %collective-permute-done.3.refs_3_ = bf16[64,1024]{1,0:T(8,128)(2,1)S(1)} collective-permute-done((bf16[64,1024]{1,0:T(8,128)(2,1)S(1)}, bf16[64,1024]{1,0:T(8,128)(2,1)S(1)}, u32[]{:S(2)}, u32[]{:S(2)}) %collective-permute-start.3) | collective-permute-done | bytes 131104 | tf_op jit(solution)/shard_map/ppermute | solution.py:261
  62.8 0.0 collective-permute-done.4.refs_4_
  62.8 0.0 collective-permute-done.1.refs_1_
  62.8 5.6 %collective-permute-start.5 = (bf16[768,1024]{1,0:T(8,128)(2,1)S(1)}, bf16[768,1024]{1,0:T(8,128)(2,1)S(1)}, u32[]{:S(2)}, u32[]{:S(2)}) collective-permute-start(bf16[768,1024]{1,0:T(8,128)(2,1)S(1)} %get-tuple-element.33.refs_6_.first_ref), channel_id=1, source_target_pairs={{0,1},{1,0},{2,3},{3,2},{4,5},{5,4},{6,7},{7,6},{8,9},{9,8},{10,11... | collective-permute-start | bytes 4718600 | tf_op jit(solution)/shard_map/ppermute | solution.py:304
  68.4 0.0 copy-done.2
  68.4 2.6 %shard_map.71 = (f32[512,1536]{1,0:T(8,128)S(1)}, f32[2,1536]{1,0:T(2,128)S(1)}) custom-call(bf16[128,1024]{1,0:T(8,128)(2,1)S(1)} %bitcast.14, bf16[128,1024]{1,0:T(8,128)(2,1)S(1)} %collective-permute-done.1.refs_1_, bf16[64,1024]{1,0:T(8,128)(2,1)S(1)} %collective-permute-done.2.refs_2_, bf16[64,1024]{1,0:T(8,128)(2,1)S(1)} %collective-permute-done.3.refs_3_, ...), custom_call_target="tpu_custom_call" | custom-call | flops 1610612736 | bytes 6291456 | tf_op jit(solution)/shard_map/pallas_call | solution.py:235
  71.0 0.4 collective-permute-done.5.refs_7_.second_ref
  71.4 3.0 %shard_map.72 = (f32[512,1536]{1,0:T(8,128)S(1)}, f32[2,1536]{1,0:T(2,128)S(1)}, f32[2,1536]{1,0:T(2,128)S(1)}) custom-call(s32[6]{0:T(128)S(1)} %stack.23.place_ref, f32[2,1536]{1,0:T(2,128)S(1)} %get-tuple-element.31.old_ref.stat_a, bf16[128,1024]{1,0:T(8,128)(2,1)S(1)} %bitcast.15, bf16[128,1024]{1,0:T(8,128)(2,1)S(1)} %collective-permute-done.1.refs_1_, ...), custom_call_target="tpu_custom_call" | custom-call | flops 1610612736 | bytes 6291456 | tf_op jit(solution)/shard_map/pallas_call | solution.py:235
  74.5 0.1 broadcast_in_dim.7
  74.5 11.3 %all_to_all.21.all_ref = f32[16,2,1536]{2,1,0:T(2,128)S(1)} all-to-all(f32[16,2,1536]{2,1,0:T(2,128)S(1)} %broadcast_in_dim.7), channel_id=1, replica_groups=mesh['zh'=4,'zl'=4,'xh'=2,'xl'=2,'y'=4,'c'=2] {'xl','y','c'}, dimensions={0} | all-to-all | bytes 393216 | tf_op jit(solution)/shard_map/all_to_all | solution.py:318
  85.8 3.3 %shard_map.74 = (bf16[64,1152]{1,0:T(8,128)(2,1)S(1)}, bf16[64,1152]{1,0:T(8,128)(2,1)S(1)}, bf16[128,1152]{1,0:T(8,128)(2,1)S(1)}, bf16[128,1152]{1,0:T(8,128)(2,1)S(1)}) custom-call(s32[6]{0:T(128)S(1)} %stack.23.place_ref, f32[16,2,1536]{2,1,0:T(2,128)S(1)} %all_to_all.21.all_ref, bf16[1536,1024]{1,0:T(8,128)(2,1)S(1)} %copy-done.2, ...), custom_call_target="tpu_custom_call" | custom-call | flops 1610612736 | bytes 10485760 | tf_op jit(solution)/shard_map/pallas_call | solution.py:235
  89.2 1.9 %collective-permute-start.8 = (bf16[128,1152]{1,0:T(8,128)(2,1)S(1)}, bf16[128,1152]{1,0:T(8,128)(2,1)S(1)}, u32[]{:S(2)}, u32[]{:S(2)}) collective-permute-start(bf16[128,1152]{1,0:T(8,128)(2,1)S(1)} %get-tuple-element.40), channel_id=1, source_target_pairs={{0,32},{32,64},{64,96},{96,128},{128,160},{160,192},{192,224},{224... | collective-permute-start | bytes 884744 | tf_op jit(solution)/shard_map/ppermute | solution.py:261
  91.1 4.6 %collective-permute-start.9 = (bf16[128,1152]{1,0:T(8,128)(2,1)S(1)}, bf16[128,1152]{1,0:T(8,128)(2,1)S(1)}, u32[]{:S(2)}, u32[]{:S(2)}) collective-permute-start(bf16[128,1152]{1,0:T(8,128)(2,1)S(1)} %get-tuple-element.41), channel_id=1, source_target_pairs={{0,480},{32,0},{64,32},{96,64},{128,96},{160,128},{192,160},{224,1... | collective-permute-start | bytes 884744 | tf_op jit(solution)/shard_map/ppermute | solution.py:261
  95.7 2.0 %collective-permute-start.6 = (bf16[64,1152]{1,0:T(8,128)(2,1)S(1)}, bf16[64,1152]{1,0:T(8,128)(2,1)S(1)}, u32[]{:S(2)}, u32[]{:S(2)}) collective-permute-start(bf16[64,1152]{1,0:T(8,128)(2,1)S(1)} %get-tuple-element.38), channel_id=1, source_target_pairs={{0,64},{32,96},{64,128},{96,160},{128,192},{160,224},{192,256},{22... | collective-permute-start | bytes 442376 | tf_op jit(solution)/shard_map/ppermute | solution.py:261
  97.7 5.4 %collective-permute-start.7 = (bf16[64,1152]{1,0:T(8,128)(2,1)S(1)}, bf16[64,1152]{1,0:T(8,128)(2,1)S(1)}, u32[]{:S(2)}, u32[]{:S(2)}) collective-permute-start(bf16[64,1152]{1,0:T(8,128)(2,1)S(1)} %get-tuple-element.39), channel_id=1, source_target_pairs={{0,448},{32,480},{64,0},{96,32},{128,64},{160,96},{192,128},{224,1... | collective-permute-start | bytes 442376 | tf_op jit(solution)/shard_map/ppermute | solution.py:261
  103.1 1.6 %shard_map.73.a = bf16[128,1152]{1,0:T(8,128)(2,1)S(1)} custom-call(s32[6]{0:T(128)S(1)} %stack.23.place_ref, f32[16,2,1536]{2,1,0:T(2,128)S(1)} %all_to_all.21.all_ref, bf16[1536,1024]{1,0:T(8,128)(2,1)S(1)} %copy-done.2, bf16[768,1024]{1,0:T(8,128)(2,1)S(1)} %get-tuple-element.33.refs_6_.first_ref, ...), custom_call_target="tpu_custom_call" | custom-call | flops 1610612736 | bytes 10485760 | tf_op jit(solution)/shard_map/pallas_call | solution.py:235
  104.7 3.1 %collective-permute-done.6.low = bf16[64,1152]{1,0:T(8,128)(2,1)S(1)} collective-permute-done((bf16[64,1152]{1,0:T(8,128)(2,1)S(1)}, bf16[64,1152]{1,0:T(8,128)(2,1)S(1)}, u32[]{:S(2)}, u32[]{:S(2)}) %collective-permute-start.6) | collective-permute-done | bytes 147488 | tf_op jit(solution)/shard_map/ppermute | solution.py:261
  107.8 4.2 %collective-permute-done.7.high = bf16[64,1152]{1,0:T(8,128)(2,1)S(1)} collective-permute-done((bf16[64,1152]{1,0:T(8,128)(2,1)S(1)}, bf16[64,1152]{1,0:T(8,128)(2,1)S(1)}, u32[]{:S(2)}, u32[]{:S(2)}) %collective-permute-start.7) | collective-permute-done | bytes 147488 | tf_op jit(solution)/shard_map/ppermute | solution.py:261
  112.0 0.0 collective-permute-done.8.b
  112.0 0.0 collective-permute-done.9.c
  112.0 0.3 shard_map.75
  112.4 21.9 %all_to_all.22.ref = bf16[8,16,1152]{2,1,0:T(8,128)(2,1)S(1)} all-to-all(bf16[8,16,1152]{2,1,0:T(8,128)(2,1)S(1)} %bitcast.11), channel_id=1, replica_groups={{0,128,256,384,24,152,280,408},{8,136,264,392,16,144,272,400},{1,129,25..., dimensions={0} | all-to-all | bytes 589824 | tf_op jit(solution)/shard_map/all_to_all | solution.py:264
  134.2 0.2 shard_map.76
  134.4 13.8 %all_to_all.23.ref = bf16[8,16,1152]{2,1,0:T(8,128)(2,1)S(1)} all-to-all(bf16[8,16,1152]{2,1,0:T(8,128)(2,1)S(1)} %shard_map.76), channel_id=1, replica_groups=mesh['zh'=4,'zl'=4,'xh'=2,'xl'=2,'y'=4,'c'=2] {'y','c'}, dimensions={0} | all-to-all | bytes 589824 | tf_op jit(solution)/shard_map/all_to_all | solution.py:337
  148.2 0.8 shard_map.77
  (3 shorter events, 0.0 us)
Async XLA Ops:
  0.6 7.4 %copy-start = (bf16[128,1024]{1,0:T(8,128)(2,1)S(1)}, bf16[128,1024]{1,0:T(8,128)(2,1)}, u32[]{:S(2)}) copy-start(bf16[128,1024]{1,0:T(8,128)(2,1)} %param.9) | copy-start | bytes 786436
  1.4 1.9 %copy-start.1 = (bf16[1536,1024]{1,0:T(8,128)(2,1)S(1)}, bf16[1536,1024]{1,0:T(8,128)(2,1)}, u32[]{:S(2)}) copy-start(bf16[1536,1024]{1,0:T(8,128)(2,1)} %points_ref.5) | copy-start | bytes 9437188
  3.3 53.6 %copy-start.4 = (s32[8192]{0:T(1024)S(1)}, s32[8192]{0:T(1024)}, u32[]{:S(2)}) copy-start(s32[8192]{0:T(1024)} %param.8) | copy-start | bytes 98308
  4.0 55.3 %collective-permute-start = (bf16[784,1024]{1,0:T(8,128)(2,1)S(1)}, bf16[784,1024]{1,0:T(8,128)(2,1)S(1)}, u32[]{:S(2)}, u32[]{:S(2)}) collective-permute-start(bf16[784,1024]{1,0:T(8,128)(2,1)S(1)} %shard_map.68), channel_id=1, source_target_pairs={{0,8},{8,0},{1,9},{9,1},{2,10},{10,2},{3,11},{11,3},{4,12},{12,4},... | collective-permute-start | bytes 4816904 | tf_op jit(solution)/shard_map/ppermute | solution.py:281
  8.0 60.4 %copy-start.2 = (bf16[1536,1024]{1,0:T(8,128)(2,1)S(1)}, bf16[1536,1024]{1,0:T(8,128)(2,1)}, u32[]{:S(2)}) copy-start(bf16[1536,1024]{1,0:T(8,128)(2,1)} %points_ref.5) | copy-start | bytes 9437188
  39.1 23.7 %collective-permute-start.4 = (bf16[128,1024]{1,0:T(8,128)(2,1)S(1)}, bf16[128,1024]{1,0:T(8,128)(2,1)S(1)}, u32[]{:S(2)}, u32[]{:S(2)}) collective-permute-start(bf16[128,1024]{1,0:T(8,128)(2,1)S(1)} %bitcast.12), channel_id=1, source_target_pairs={{0,32},{32,64},{64,96},{96,128},{128,160},{160,192},{192,224},{224... | collective-permute-start | bytes 786440 | tf_op jit(solution)/shard_map/ppermute | solution.py:261
  48.7 14.1 %collective-permute-start.1 = (bf16[128,1024]{1,0:T(8,128)(2,1)S(1)}, bf16[128,1024]{1,0:T(8,128)(2,1)S(1)}, u32[]{:S(2)}, u32[]{:S(2)}) collective-permute-start(bf16[128,1024]{1,0:T(8,128)(2,1)S(1)} %bitcast.13), channel_id=1, source_target_pairs={{0,480},{32,0},{64,32},{96,64},{128,96},{160,128},{192,160},{224,1... | collective-permute-start | bytes 786440 | tf_op jit(solution)/shard_map/ppermute | solution.py:261
  50.7 10.3 %collective-permute-start.2 = (bf16[64,1024]{1,0:T(8,128)(2,1)S(1)}, bf16[64,1024]{1,0:T(8,128)(2,1)S(1)}, u32[]{:S(2)}, u32[]{:S(2)}) collective-permute-start(bf16[64,1024]{1,0:T(8,128)(2,1)S(1)} %bitcast.19), channel_id=1, source_target_pairs={{0,448},{32,480},{64,0},{96,32},{128,64},{160,96},{192,128},{224,1... | collective-permute-start | bytes 393224 | tf_op jit(solution)/shard_map/ppermute | solution.py:261
  53.6 9.2 %collective-permute-start.3 = (bf16[64,1024]{1,0:T(8,128)(2,1)S(1)}, bf16[64,1024]{1,0:T(8,128)(2,1)S(1)}, u32[]{:S(2)}, u32[]{:S(2)}) collective-permute-start(bf16[64,1024]{1,0:T(8,128)(2,1)S(1)} %bitcast.18), channel_id=1, source_target_pairs={{0,64},{32,96},{64,128},{96,160},{128,192},{160,224},{192,256},{22... | collective-permute-start | bytes 393224 | tf_op jit(solution)/shard_map/ppermute | solution.py:261
  56.9 0.9 copy-start.3
  62.8 8.6 %collective-permute-start.5 = (bf16[768,1024]{1,0:T(8,128)(2,1)S(1)}, bf16[768,1024]{1,0:T(8,128)(2,1)S(1)}, u32[]{:S(2)}, u32[]{:S(2)}) collective-permute-start(bf16[768,1024]{1,0:T(8,128)(2,1)S(1)} %get-tuple-element.33.refs_6_.first_ref), channel_id=1, source_target_pairs={{0,1},{1,0},{2,3},{3,2},{4,5},{5,4},{6,7},{7,6},{8,9},{9,8},{10,11... | collective-permute-start | bytes 4718600 | tf_op jit(solution)/shard_map/ppermute | solution.py:304
  89.2 22.9 %collective-permute-start.8 = (bf16[128,1152]{1,0:T(8,128)(2,1)S(1)}, bf16[128,1152]{1,0:T(8,128)(2,1)S(1)}, u32[]{:S(2)}, u32[]{:S(2)}) collective-permute-start(bf16[128,1152]{1,0:T(8,128)(2,1)S(1)} %get-tuple-element.40), channel_id=1, source_target_pairs={{0,32},{32,64},{64,96},{96,128},{128,160},{160,192},{192,224},{224... | collective-permute-start | bytes 884744 | tf_op jit(solution)/shard_map/ppermute | solution.py:261
  91.1 20.9 %collective-permute-start.9 = (bf16[128,1152]{1,0:T(8,128)(2,1)S(1)}, bf16[128,1152]{1,0:T(8,128)(2,1)S(1)}, u32[]{:S(2)}, u32[]{:S(2)}) collective-permute-start(bf16[128,1152]{1,0:T(8,128)(2,1)S(1)} %get-tuple-element.41), channel_id=1, source_target_pairs={{0,480},{32,0},{64,32},{96,64},{128,96},{160,128},{192,160},{224,1... | collective-permute-start | bytes 884744 | tf_op jit(solution)/shard_map/ppermute | solution.py:261
  95.7 12.1 %collective-permute-start.6 = (bf16[64,1152]{1,0:T(8,128)(2,1)S(1)}, bf16[64,1152]{1,0:T(8,128)(2,1)S(1)}, u32[]{:S(2)}, u32[]{:S(2)}) collective-permute-start(bf16[64,1152]{1,0:T(8,128)(2,1)S(1)} %get-tuple-element.38), channel_id=1, source_target_pairs={{0,64},{32,96},{64,128},{96,160},{128,192},{160,224},{192,256},{22... | collective-permute-start | bytes 442376 | tf_op jit(solution)/shard_map/ppermute | solution.py:261
  97.7 14.4 %collective-permute-start.7 = (bf16[64,1152]{1,0:T(8,128)(2,1)S(1)}, bf16[64,1152]{1,0:T(8,128)(2,1)S(1)}, u32[]{:S(2)}, u32[]{:S(2)}) collective-permute-start(bf16[64,1152]{1,0:T(8,128)(2,1)S(1)} %get-tuple-element.39), channel_id=1, source_target_pairs={{0,448},{32,480},{64,0},{96,32},{128,64},{160,96},{192,128},{224,1... | collective-permute-start | bytes 442376 | tf_op jit(solution)/shard_map/ppermute | solution.py:261

commit v13 on v12

--- a/solution.py
+++ b/solution.py
@@ -328,7 +328,8 @@
             scratch=[pltpu.VMEM((2, count), f32)],
         )
 
-    low, high, one, three = sums((2, 1, 3), (size // 2, size // 2, size, size))
+    one, three = sums((1, 3), (size, size))
+    low, high = sums((2,), (size // 2, size // 2))
     (kept,) = sums((0,), (size,))
     got = [kept, along(low, 2), along(high, -2), along(one, 1), along(three, -1)]
     summed = call(near_kernel, sds((size, padded), bf16), tuple(got))

time: 150 us -> 151 us (level)
    pallas_call x10 -> x11, Pallas kernels: 15.8 us -> 16.5 us  [call(): pl.pallas_call(kernel, out_shape=outs, in_specs=specs or vmem(len(args)),...]
  transfers between devices with their start and end apart: 10 -> 10, of which waited for: 4 -> 4; matrix products, arithmetic and copies ran while one was open for 0% -> 0% of each run, Pallas kernels for 5% -> 6%
where the time goes in v13:
time: 151 us; the launch traced here: 150 us
  blocking collectives  78.1 us (52%)
  starting transfers between devices  41.1 us (27%)
  Pallas kernels  16.5 us (11%)
  waiting for transfers between devices  9.26 us (6%)
  local copies, waits for them, and re-layouts  3 us (2%)
  between operations  1.57 us (1%)
    all_to_all x2, blocking collectives, team_exchange(): return lax.all_to_all(a, far, 0, 0, axis_index_groups=teams, tiled=True)  53.3 us
    ppermute x8, starting transfers between devices, along(): return lax.ppermute(a, deep, [(i, (i + by) % zs) for i in range(zs)])  31.6 us
    pallas_call x11, Pallas kernels, call(): pl.pallas_call(kernel, out_shape=outs, in_specs=specs or vmem(len(args)),...  16.5 us
    all_to_all x1, blocking collectives, shards(): whole = lax.all_to_all(table, narrow, 0, 0, tiled=True)  13.5 us
    all_to_all x1, blocking collectives, shards(): shared = lax.all_to_all(copies, pool, 0, 0, tiled=True)  11.3 us
    ppermute x8, waiting for transfers between devices, along(): return lax.ppermute(a, deep, [(i, (i + by) % zs) for i in range(zs)])  8.82 us
    ppermute x1, starting transfers between devices, shards(): second = lax.ppermute(first, 'c', swap)  5.62 us
    ppermute x1, starting transfers between devices, shards(): first = lax.ppermute(half, 'xl', swap)  3.95 us
  transfers between devices with their start and end apart: 10, of which 4 were waited for; matrix products, arithmetic and copies ran while one was open for 0% of the time, Pallas kernels for 6%

profile of v13, /device:TPU:1, one launch (start us, length us, event | category | flops | bytes accessed | tf_op | source)
XLA Modules:
  0.0 149.6 jit_solution(14211943721502694274)
XLA Ops:
  0.6 0.0 copy-start
  1.3 0.1 stack.23.place_ref
  1.4 0.0 copy-start.1
  1.4 1.9 %copy-done.1 = bf16[1536,1024]{1,0:T(8,128)(2,1)S(1)} copy-done((bf16[1536,1024]{1,0:T(8,128)(2,1)S(1)}, bf16[1536,1024]{1,0:T(8,128)(2,1)}, u32[]{:S(2)}) %copy-start.1) | copy-done | bytes 3145752
  3.3 0.0 copy-start.4
  3.3 0.7 shard_map.68
  4.0 3.9 %collective-permute-start = (bf16[784,1024]{1,0:T(8,128)(2,1)S(1)}, bf16[784,1024]{1,0:T(8,128)(2,1)S(1)}, u32[]{:S(2)}, u32[]{:S(2)}) collective-permute-start(bf16[784,1024]{1,0:T(8,128)(2,1)S(1)} %shard_map.68), channel_id=1, source_target_pairs={{0,8},{8,0},{1,9},{9,1},{2,10},{10,2},{3,11},{11,3},{4,12},{12,4},... | collective-permute-start | bytes 4816904 | tf_op jit(solution)/shard_map/ppermute | solution.py:281
  8.0 0.0 copy-done
  8.0 0.0 copy-start.2
  8.1 31.1 %all_to_all.20 = bf16[8,16,1024]{2,1,0:T(8,128)(2,1)S(1)} all-to-all(bf16[8,16,1024]{2,1,0:T(8,128)(2,1)S(1)} %broadcast_in_dim.6), channel_id=1, replica_groups={{0,128,256,384,24,152,280,408},{8,136,264,392,16,144,272,400},{1,129,25..., dimensions={0} | all-to-all | bytes 524288 | tf_op jit(solution)/shard_map/all_to_all | solution.py:264
  39.1 3.2 %collective-permute-start.1 = (bf16[128,1024]{1,0:T(8,128)(2,1)S(1)}, bf16[128,1024]{1,0:T(8,128)(2,1)S(1)}, u32[]{:S(2)}, u32[]{:S(2)}) collective-permute-start(bf16[128,1024]{1,0:T(8,128)(2,1)S(1)} %bitcast.12), channel_id=1, source_target_pairs={{0,480},{32,0},{64,32},{96,64},{128,96},{160,128},{192,160},{224,1... | collective-permute-start | bytes 786440 | tf_op jit(solution)/shard_map/ppermute | solution.py:261
  42.4 8.3 %collective-permute-start.4 = (bf16[128,1024]{1,0:T(8,128)(2,1)S(1)}, bf16[128,1024]{1,0:T(8,128)(2,1)S(1)}, u32[]{:S(2)}, u32[]{:S(2)}) collective-permute-start(bf16[128,1024]{1,0:T(8,128)(2,1)S(1)} %bitcast.13), channel_id=1, source_target_pairs={{0,32},{32,64},{64,96},{96,128},{128,160},{160,192},{192,224},{224... | collective-permute-start | bytes 786440 | tf_op jit(solution)/shard_map/ppermute | solution.py:261
  50.7 2.9 %collective-permute-start.2 = (bf16[64,1024]{1,0:T(8,128)(2,1)S(1)}, bf16[64,1024]{1,0:T(8,128)(2,1)S(1)}, u32[]{:S(2)}, u32[]{:S(2)}) collective-permute-start(bf16[64,1024]{1,0:T(8,128)(2,1)S(1)} %bitcast.19), channel_id=1, source_target_pairs={{0,448},{32,480},{64,0},{96,32},{128,64},{160,96},{192,128},{224,1... | collective-permute-start | bytes 393224 | tf_op jit(solution)/shard_map/ppermute | solution.py:261
  53.6 3.3 %collective-permute-start.3 = (bf16[64,1024]{1,0:T(8,128)(2,1)S(1)}, bf16[64,1024]{1,0:T(8,128)(2,1)S(1)}, u32[]{:S(2)}, u32[]{:S(2)}) collective-permute-start(bf16[64,1024]{1,0:T(8,128)(2,1)S(1)} %bitcast.18), channel_id=1, source_target_pairs={{0,64},{32,96},{64,128},{96,160},{128,192},{160,224},{192,256},{22... | collective-permute-start | bytes 393224 | tf_op jit(solution)/shard_map/ppermute | solution.py:261
  56.9 0.0 copy-done.4
  56.9 0.0 copy-start.3
  56.9 0.9 copy-done.3
  57.8 1.5 %shard_map.70.refs_5_ = f32[128,128]{1,0:T(8,128)S(1)} custom-call(s32[6]{0:T(128)S(1)} %stack.23.place_ref, s32[16,2048]{1,0:T(8,128)S(1)} %copy-done.3, s32[64,128]{1,0:T(8,128)S(1)} %bitcast.16), custom_call_target="tpu_custom_call" | custom-call | bytes 8388608 | tf_op jit(solution)/shard_map/pallas_call | solution.py:235
  59.3 0.0 collective-permute-done.refs_0_
  59.3 1.6 %shard_map.69 = (f32[128,128]{1,0:T(8,128)S(1)}, bf16[768,1024]{1,0:T(8,128)(2,1)S(1)}) custom-call(s32[6]{0:T(128)S(1)} %stack.23.place_ref, s32[16,2048]{1,0:T(8,128)S(1)} %copy-done.3, s32[64,128]{1,0:T(8,128)S(1)} %bitcast.17, bf16[784,1024]{1,0:T(8,128)(2,1)S(1)} %collective-permute-done.refs_0_), custom_call_target="tpu_custom_call" | custom-call | bytes 8388608 | tf_op jit(solution)/shard_map/pallas_call | solution.py:235
  61.0 0.0 collective-permute-done.2.refs_2_
  61.0 1.9 %collective-permute-done.3.refs_3_ = bf16[64,1024]{1,0:T(8,128)(2,1)S(1)} collective-permute-done((bf16[64,1024]{1,0:T(8,128)(2,1)S(1)}, bf16[64,1024]{1,0:T(8,128)(2,1)S(1)}, u32[]{:S(2)}, u32[]{:S(2)}) %collective-permute-start.3) | collective-permute-done | bytes 131104 | tf_op jit(solution)/shard_map/ppermute | solution.py:261
  62.8 0.0 collective-permute-done.1.refs_1_
  62.8 0.0 collective-permute-done.4.refs_4_
  62.8 5.6 %collective-permute-start.5 = (bf16[768,1024]{1,0:T(8,128)(2,1)S(1)}, bf16[768,1024]{1,0:T(8,128)(2,1)S(1)}, u32[]{:S(2)}, u32[]{:S(2)}) collective-permute-start(bf16[768,1024]{1,0:T(8,128)(2,1)S(1)} %get-tuple-element.33.refs_6_.first_ref), channel_id=1, source_target_pairs={{0,1},{1,0},{2,3},{3,2},{4,5},{5,4},{6,7},{7,6},{8,9},{9,8},{10,11... | collective-permute-start | bytes 4718600 | tf_op jit(solution)/shard_map/ppermute | solution.py:304
  68.5 0.0 copy-done.2
  68.5 2.6 %shard_map.71 = (f32[512,1536]{1,0:T(8,128)S(1)}, f32[2,1536]{1,0:T(2,128)S(1)}) custom-call(bf16[128,1024]{1,0:T(8,128)(2,1)S(1)} %bitcast.14, bf16[128,1024]{1,0:T(8,128)(2,1)S(1)} %collective-permute-done.1.refs_1_, bf16[64,1024]{1,0:T(8,128)(2,1)S(1)} %collective-permute-done.2.refs_2_, bf16[64,1024]{1,0:T(8,128)(2,1)S(1)} %collective-permute-done.3.refs_3_, ...), custom_call_target="tpu_custom_call" | custom-call | flops 1610612736 | bytes 6291456 | tf_op jit(solution)/shard_map/pallas_call | solution.py:235
  71.0 0.4 collective-permute-done.5.refs_7_.second_ref
  71.5 3.0 %shard_map.72 = (f32[512,1536]{1,0:T(8,128)S(1)}, f32[2,1536]{1,0:T(2,128)S(1)}, f32[2,1536]{1,0:T(2,128)S(1)}) custom-call(s32[6]{0:T(128)S(1)} %stack.23.place_ref, f32[2,1536]{1,0:T(2,128)S(1)} %get-tuple-element.31.old_ref.stat_a, bf16[128,1024]{1,0:T(8,128)(2,1)S(1)} %bitcast.15, bf16[128,1024]{1,0:T(8,128)(2,1)S(1)} %collective-permute-done.1.refs_1_, ...), custom_call_target="tpu_custom_call" | custom-call | flops 1610612736 | bytes 6291456 | tf_op jit(solution)/shard_map/pallas_call | solution.py:235
  74.5 0.1 broadcast_in_dim.7
  74.6 11.3 %all_to_all.21.all_ref = f32[16,2,1536]{2,1,0:T(2,128)S(1)} all-to-all(f32[16,2,1536]{2,1,0:T(2,128)S(1)} %broadcast_in_dim.7), channel_id=1, replica_groups=mesh['zh'=4,'zl'=4,'xh'=2,'xl'=2,'y'=4,'c'=2] {'xl','y','c'}, dimensions={0} | all-to-all | bytes 393216 | tf_op jit(solution)/shard_map/all_to_all | solution.py:318
  85.9 2.4 %shard_map.75 = (bf16[128,1152]{1,0:T(8,128)(2,1)S(1)}, bf16[128,1152]{1,0:T(8,128)(2,1)S(1)}) custom-call(s32[6]{0:T(128)S(1)} %stack.23.place_ref, f32[16,2,1536]{2,1,0:T(2,128)S(1)} %all_to_all.21.all_ref, bf16[1536,1024]{1,0:T(8,128)(2,1)S(1)} %copy-done.2, bf16[768,1024]{1,0:T(8,128)(2,1)S(1)} %get-tuple-element.33.refs_6_.first_ref, ...), custom_call_target="tpu_custom_call" | custom-call | flops 1610612736 | bytes 10485760 | tf_op jit(solution)/shard_map/pallas_call | solution.py:235
  88.4 3.6 %collective-permute-start.8 = (bf16[128,1152]{1,0:T(8,128)(2,1)S(1)}, bf16[128,1152]{1,0:T(8,128)(2,1)S(1)}, u32[]{:S(2)}, u32[]{:S(2)}) collective-permute-start(bf16[128,1152]{1,0:T(8,128)(2,1)S(1)} %get-tuple-element.40), channel_id=1, source_target_pairs={{0,32},{32,64},{64,96},{96,128},{128,160},{160,192},{192,224},{224... | collective-permute-start | bytes 884744 | tf_op jit(solution)/shard_map/ppermute | solution.py:261
  92.0 2.9 %collective-permute-start.9 = (bf16[128,1152]{1,0:T(8,128)(2,1)S(1)}, bf16[128,1152]{1,0:T(8,128)(2,1)S(1)}, u32[]{:S(2)}, u32[]{:S(2)}) collective-permute-start(bf16[128,1152]{1,0:T(8,128)(2,1)S(1)} %get-tuple-element.41), channel_id=1, source_target_pairs={{0,480},{32,0},{64,32},{96,64},{128,96},{160,128},{192,160},{224,1... | collective-permute-start | bytes 884744 | tf_op jit(solution)/shard_map/ppermute | solution.py:261
  94.9 1.6 %shard_map.74 = (bf16[64,1152]{1,0:T(8,128)(2,1)S(1)}, bf16[64,1152]{1,0:T(8,128)(2,1)S(1)}) custom-call(s32[6]{0:T(128)S(1)} %stack.23.place_ref, f32[16,2,1536]{2,1,0:T(2,128)S(1)} %all_to_all.21.all_ref, bf16[1536,1024]{1,0:T(8,128)(2,1)S(1)} %copy-done.2, bf16[768,1024]{1,0:T(8,128)(2,1)S(1)} %get-tuple-element.33.refs_6_.first_ref, ...), custom_call_target="tpu_custom_call" | custom-call | flops 1610612736 | bytes 10485760 | tf_op jit(solution)/shard_map/pallas_call | solution.py:235
  96.5 2.1 %collective-permute-start.6 = (bf16[64,1152]{1,0:T(8,128)(2,1)S(1)}, bf16[64,1152]{1,0:T(8,128)(2,1)S(1)}, u32[]{:S(2)}, u32[]{:S(2)}) collective-permute-start(bf16[64,1152]{1,0:T(8,128)(2,1)S(1)} %get-tuple-element.38), channel_id=1, source_target_pairs={{0,64},{32,96},{64,128},{96,160},{128,192},{160,224},{192,256},{22... | collective-permute-start | bytes 442376 | tf_op jit(solution)/shard_map/ppermute | solution.py:261
  98.6 5.3 %collective-permute-start.7 = (bf16[64,1152]{1,0:T(8,128)(2,1)S(1)}, bf16[64,1152]{1,0:T(8,128)(2,1)S(1)}, u32[]{:S(2)}, u32[]{:S(2)}) collective-permute-start(bf16[64,1152]{1,0:T(8,128)(2,1)S(1)} %get-tuple-element.39), channel_id=1, source_target_pairs={{0,448},{32,480},{64,0},{96,32},{128,64},{160,96},{192,128},{224,1... | collective-permute-start | bytes 442376 | tf_op jit(solution)/shard_map/ppermute | solution.py:261
  103.9 1.7 %shard_map.73.a = bf16[128,1152]{1,0:T(8,128)(2,1)S(1)} custom-call(s32[6]{0:T(128)S(1)} %stack.23.place_ref, f32[16,2,1536]{2,1,0:T(2,128)S(1)} %all_to_all.21.all_ref, bf16[1536,1024]{1,0:T(8,128)(2,1)S(1)} %copy-done.2, bf16[768,1024]{1,0:T(8,128)(2,1)S(1)} %get-tuple-element.33.refs_6_.first_ref, ...), custom_call_target="tpu_custom_call" | custom-call | flops 1610612736 | bytes 10485760 | tf_op jit(solution)/shard_map/pallas_call | solution.py:235
  105.6 3.1 %collective-permute-done.6.low = bf16[64,1152]{1,0:T(8,128)(2,1)S(1)} collective-permute-done((bf16[64,1152]{1,0:T(8,128)(2,1)S(1)}, bf16[64,1152]{1,0:T(8,128)(2,1)S(1)}, u32[]{:S(2)}, u32[]{:S(2)}) %collective-permute-start.6) | collective-permute-done | bytes 147488 | tf_op jit(solution)/shard_map/ppermute | solution.py:261
  108.7 3.8 %collective-permute-done.7.high = bf16[64,1152]{1,0:T(8,128)(2,1)S(1)} collective-permute-done((bf16[64,1152]{1,0:T(8,128)(2,1)S(1)}, bf16[64,1152]{1,0:T(8,128)(2,1)S(1)}, u32[]{:S(2)}, u32[]{:S(2)}) %collective-permute-start.7) | collective-permute-done | bytes 147488 | tf_op jit(solution)/shard_map/ppermute | solution.py:261
  112.5 0.0 collective-permute-done.8.b
  112.5 0.0 collective-permute-done.9.c
  112.5 0.3 shard_map.76
  112.9 22.3 %all_to_all.22.ref = bf16[8,16,1152]{2,1,0:T(8,128)(2,1)S(1)} all-to-all(bf16[8,16,1152]{2,1,0:T(8,128)(2,1)S(1)} %bitcast.11), channel_id=1, replica_groups={{0,128,256,384,24,152,280,408},{8,136,264,392,16,144,272,400},{1,129,25..., dimensions={0} | all-to-all | bytes 589824 | tf_op jit(solution)/shard_map/all_to_all | solution.py:264
  135.1 0.2 shard_map.77
  135.3 13.5 %all_to_all.23.ref = bf16[8,16,1152]{2,1,0:T(8,128)(2,1)S(1)} all-to-all(bf16[8,16,1152]{2,1,0:T(8,128)(2,1)S(1)} %shard_map.77), channel_id=1, replica_groups=mesh['zh'=4,'zl'=4,'xh'=2,'xl'=2,'y'=4,'c'=2] {'y','c'}, dimensions={0} | all-to-all | bytes 589824 | tf_op jit(solution)/shard_map/all_to_all | solution.py:338
  148.8 0.8 shard_map.78
  (3 shorter events, 0.0 us)
Async XLA Ops:
  0.6 7.4 %copy-start = (bf16[128,1024]{1,0:T(8,128)(2,1)S(1)}, bf16[128,1024]{1,0:T(8,128)(2,1)}, u32[]{:S(2)}) copy-start(bf16[128,1024]{1,0:T(8,128)(2,1)} %param.9) | copy-start | bytes 786436
  1.4 1.9 %copy-start.1 = (bf16[1536,1024]{1,0:T(8,128)(2,1)S(1)}, bf16[1536,1024]{1,0:T(8,128)(2,1)}, u32[]{:S(2)}) copy-start(bf16[1536,1024]{1,0:T(8,128)(2,1)} %points_ref.7) | copy-start | bytes 9437188
  3.3 53.6 %copy-start.4 = (s32[8192]{0:T(1024)S(1)}, s32[8192]{0:T(1024)}, u32[]{:S(2)}) copy-start(s32[8192]{0:T(1024)} %param.8) | copy-start | bytes 98308
  4.0 55.3 %collective-permute-start = (bf16[784,1024]{1,0:T(8,128)(2,1)S(1)}, bf16[784,1024]{1,0:T(8,128)(2,1)S(1)}, u32[]{:S(2)}, u32[]{:S(2)}) collective-permute-start(bf16[784,1024]{1,0:T(8,128)(2,1)S(1)} %shard_map.68), channel_id=1, source_target_pairs={{0,8},{8,0},{1,9},{9,1},{2,10},{10,2},{3,11},{11,3},{4,12},{12,4},... | collective-permute-start | bytes 4816904 | tf_op jit(solution)/shard_map/ppermute | solution.py:281
  8.0 60.4 %copy-start.2 = (bf16[1536,1024]{1,0:T(8,128)(2,1)S(1)}, bf16[1536,1024]{1,0:T(8,128)(2,1)}, u32[]{:S(2)}) copy-start(bf16[1536,1024]{1,0:T(8,128)(2,1)} %points_ref.7) | copy-start | bytes 9437188
  39.1 23.7 %collective-permute-start.1 = (bf16[128,1024]{1,0:T(8,128)(2,1)S(1)}, bf16[128,1024]{1,0:T(8,128)(2,1)S(1)}, u32[]{:S(2)}, u32[]{:S(2)}) collective-permute-start(bf16[128,1024]{1,0:T(8,128)(2,1)S(1)} %bitcast.12), channel_id=1, source_target_pairs={{0,480},{32,0},{64,32},{96,64},{128,96},{160,128},{192,160},{224,1... | collective-permute-start | bytes 786440 | tf_op jit(solution)/shard_map/ppermute | solution.py:261
  42.4 20.4 %collective-permute-start.4 = (bf16[128,1024]{1,0:T(8,128)(2,1)S(1)}, bf16[128,1024]{1,0:T(8,128)(2,1)S(1)}, u32[]{:S(2)}, u32[]{:S(2)}) collective-permute-start(bf16[128,1024]{1,0:T(8,128)(2,1)S(1)} %bitcast.13), channel_id=1, source_target_pairs={{0,32},{32,64},{64,96},{96,128},{128,160},{160,192},{192,224},{224... | collective-permute-start | bytes 786440 | tf_op jit(solution)/shard_map/ppermute | solution.py:261
  50.7 10.3 %collective-permute-start.2 = (bf16[64,1024]{1,0:T(8,128)(2,1)S(1)}, bf16[64,1024]{1,0:T(8,128)(2,1)S(1)}, u32[]{:S(2)}, u32[]{:S(2)}) collective-permute-start(bf16[64,1024]{1,0:T(8,128)(2,1)S(1)} %bitcast.19), channel_id=1, source_target_pairs={{0,448},{32,480},{64,0},{96,32},{128,64},{160,96},{192,128},{224,1... | collective-permute-start | bytes 393224 | tf_op jit(solution)/shard_map/ppermute | solution.py:261
  53.6 9.2 %collective-permute-start.3 = (bf16[64,1024]{1,0:T(8,128)(2,1)S(1)}, bf16[64,1024]{1,0:T(8,128)(2,1)S(1)}, u32[]{:S(2)}, u32[]{:S(2)}) collective-permute-start(bf16[64,1024]{1,0:T(8,128)(2,1)S(1)} %bitcast.18), channel_id=1, source_target_pairs={{0,64},{32,96},{64,128},{96,160},{128,192},{160,224},{192,256},{22... | collective-permute-start | bytes 393224 | tf_op jit(solution)/shard_map/ppermute | solution.py:261
  56.9 0.9 copy-start.3
  62.8 8.6 %collective-permute-start.5 = (bf16[768,1024]{1,0:T(8,128)(2,1)S(1)}, bf16[768,1024]{1,0:T(8,128)(2,1)S(1)}, u32[]{:S(2)}, u32[]{:S(2)}) collective-permute-start(bf16[768,1024]{1,0:T(8,128)(2,1)S(1)} %get-tuple-element.33.refs_6_.first_ref), channel_id=1, source_target_pairs={{0,1},{1,0},{2,3},{3,2},{4,5},{5,4},{6,7},{7,6},{8,9},{9,8},{10,11... | collective-permute-start | bytes 4718600 | tf_op jit(solution)/shard_map/ppermute | solution.py:304
  88.4 24.2 %collective-permute-start.8 = (bf16[128,1152]{1,0:T(8,128)(2,1)S(1)}, bf16[128,1152]{1,0:T(8,128)(2,1)S(1)}, u32[]{:S(2)}, u32[]{:S(2)}) collective-permute-start(bf16[128,1152]{1,0:T(8,128)(2,1)S(1)} %get-tuple-element.40), channel_id=1, source_target_pairs={{0,32},{32,64},{64,96},{96,128},{128,160},{160,192},{192,224},{224... | collective-permute-start | bytes 884744 | tf_op jit(solution)/shard_map/ppermute | solution.py:261
  92.0 20.6 %collective-permute-start.9 = (bf16[128,1152]{1,0:T(8,128)(2,1)S(1)}, bf16[128,1152]{1,0:T(8,128)(2,1)S(1)}, u32[]{:S(2)}, u32[]{:S(2)}) collective-permute-start(bf16[128,1152]{1,0:T(8,128)(2,1)S(1)} %get-tuple-element.41), channel_id=1, source_target_pairs={{0,480},{32,0},{64,32},{96,64},{128,96},{160,128},{192,160},{224,1... | collective-permute-start | bytes 884744 | tf_op jit(solution)/shard_map/ppermute | solution.py:261
  96.5 12.2 %collective-permute-start.6 = (bf16[64,1152]{1,0:T(8,128)(2,1)S(1)}, bf16[64,1152]{1,0:T(8,128)(2,1)S(1)}, u32[]{:S(2)}, u32[]{:S(2)}) collective-permute-start(bf16[64,1152]{1,0:T(8,128)(2,1)S(1)} %get-tuple-element.38), channel_id=1, source_target_pairs={{0,64},{32,96},{64,128},{96,160},{128,192},{160,224},{192,256},{22... | collective-permute-start | bytes 442376 | tf_op jit(solution)/shard_map/ppermute | solution.py:261
  98.6 13.9 %collective-permute-start.7 = (bf16[64,1152]{1,0:T(8,128)(2,1)S(1)}, bf16[64,1152]{1,0:T(8,128)(2,1)S(1)}, u32[]{:S(2)}, u32[]{:S(2)}) collective-permute-start(bf16[64,1152]{1,0:T(8,128)(2,1)S(1)} %get-tuple-element.39), channel_id=1, source_target_pairs={{0,448},{32,480},{64,0},{96,32},{128,64},{160,96},{192,128},{224,1... | collective-permute-start | bytes 442376 | tf_op jit(solution)/shard_map/ppermute | solution.py:261
